TPU v7x, 256 devices: a whole 4x4x8 slice. The times are simulated.
256 devices in a mesh: pb: 16 (over x, y_lo, core), pa: 16 (over z, y_hi).
Axes of the slice: x: 4, y: 4 (y_hi: 2, y_lo: 2; y = y_hi * 2 + y_lo), z: 8, core: 2. Of those that a mesh axis runs over, the one named last changes fastest.
Arguments:
- queries: bfloat16 [4096, 128], P('pb'), may hold values from -10.5 to 10.5, as said below
- encoder_outputs: bfloat16 [16, 256, 128, 1024], P('pb', 'pa'), may hold values from -6 to 6
- proj_weight: bfloat16 [1024, 128], replicated, may hold values from -0.1875 to 0.1875
- bm25_rank: int32 [128, 16, 128], P('pb', 'pa'), may hold values from 0 to 199
- dense_rank: int32 [128, 16, 128], P('pb', 'pa'), may hold values from 0 to 199
- custodian_document_index: int32 [16, 256], P('pb', 'pa'), may hold values from -1 to 127, as said below
Outputs:
- query_grad: float32 [4096, 128], P(('pb', 'pa'))
- encoder_output_derivative: bfloat16 [16, 256, 128, 1024], P('pb', 'pa')
Inputs may be any that keep to these rules, and one draw needn't show every extreme that they name: `queries`: A custom draw: each entry lies between the bounds; rows may differ in scale. `custodian_document_index`: within each row b every number n from 0 to 127 appears exactly once and stands for passage (n // 8, b * 8 + n % 8); all other entries are -1. The owner of columns o * 16 to o * 16 + 15 is index o of pa; an owner holds 0, 8 or 16 passages, and at most 1 with the same n // 8. Some owner is full and some owner holds exactly 1 passages with the same n // 8 in every row.
All inputs are finite; a program needn't handle non-finite values.
Results may differ from a plain program's by a relative error of at most 0.025.
The roundings to bfloat16 on the way count: a program that leaves them out, or rounds other values in their place, can miss the bound.
Values may be sent and summed in bfloat16 or wider, within the bound.
No kernel may reach another device: no remote copies, remote signals or barrier semaphores. Data moves between devices by JAX's collectives and lax.ppermute only.
A program may use at most 64 MiB of HBM per device.

v0:
```python
import jax
import jax.numpy as jnp
from jax import lax
from jax.sharding import PartitionSpec as P

DIM = 128
H = 1024
QT = 32
LEN = 128
PD = 8
DEPTH = 100
CAP = 16


tau = 0.05
inv_temp = 20.0
rrf_offset = 60.0
norm_eps = 1e-06


def normalize(hid_rows, weight):
    projected = jnp.dot(hid_rows, weight, preferred_element_type=jnp.float32)
    scaling = lax.rsqrt(jnp.sum(projected * projected, axis=-1, keepdims=True) + norm_eps)
    return (projected * scaling, scaling)


def joined_target(bm25_rank, dense_rank):
    first = jnp.where(
        bm25_rank < DEPTH, rrf_offset / (rrf_offset + bm25_rank.astype(jnp.float32)), 0.0
    )
    second = jnp.where(
        dense_rank < DEPTH, rrf_offset / (rrf_offset + dense_rank.astype(jnp.float32)), 0.0
    )
    return first + second


def routing(slot_ids, width_pa, sendable):
    filled = slot_ids >= 0
    destination = jnp.where(filled, slot_ids // PD, -1)
    positions = jnp.arange(CAP, dtype=jnp.int32)
    earlier = (destination[None, :] == destination[:, None]) & (
        positions[None, :] < positions[:, None]
    )
    rank_in = jnp.sum(earlier.astype(jnp.int32), axis=1)
    target_at = jnp.where(filled, destination * sendable + rank_in, width_pa * sendable)
    flat_index = jnp.arange(width_pa * sendable, dtype=jnp.int32)
    matches = target_at[None, :] == flat_index[:, None]
    present = jnp.any(matches, axis=1)
    source = jnp.sum(jnp.where(matches, positions[None, :], 0), axis=1)
    labels = jnp.sum(jnp.where(matches, slot_ids[None, :] % PD, 0), axis=1)
    labels = jnp.where(present, labels, -1)
    return (filled, target_at, source, present, labels)


def pick_rows(table, index_list, keep):
    picked = jnp.take(table, jnp.clip(index_list, 0, table.shape[0] - 1), axis=0)
    keep_shape = keep.reshape(keep.shape + (1,) * (picked.ndim - 1))
    return jnp.where(keep_shape, picked, jnp.zeros((), picked.dtype))


def arrival_index(labels):
    wanted = jnp.arange(PD, dtype=jnp.int32)
    matches = labels[None, :] == wanted[:, None]
    slot_numbers = jnp.arange(labels.shape[0], dtype=jnp.int32)
    return jnp.sum(jnp.where(matches, slot_numbers[None, :], 0), axis=1)


def similarity(query_rows, key_block):
    shards = key_block.shape[0]
    flat_keys = key_block.reshape(shards * LEN, key_block.shape[-1])
    raw = (
        jnp.einsum("rd,kd->rk", query_rows, flat_keys, preferred_element_type=jnp.float32)
        * inv_temp
    )
    return raw.reshape(query_rows.shape[0], shards, LEN)


def log_total(raw):
    largest = jnp.max(raw, axis=2, keepdims=True)
    return largest[:, :, 0] + jnp.log(jnp.sum(jnp.exp(raw - largest), axis=2))


def on_device(
    queries, encoder_outputs, proj_weight, bm25_rank, dense_rank, custodian_document_index
):
    width_pa = lax.axis_size("pa")
    sendable = (2 * PD + width_pa - 1) // width_pa
    query_rows = queries.shape[0]
    query_count = query_rows // QT
    passages_all = bm25_rank.shape[2]
    zero_index = jnp.int32(0)
    hid_slots = encoder_outputs[0]
    slot_ids = custodian_document_index[0]
    filled, target_at, source, present, labels = routing(slot_ids, width_pa, sendable)
    unit_rows, scaling = normalize(hid_slots.reshape(CAP * LEN, H), proj_weight)
    emb_slots = unit_rows.astype(jnp.bfloat16).reshape(CAP, LEN, DIM)
    outgoing = pick_rows(emb_slots, source, present).reshape(width_pa, sendable, LEN, DIM)
    arrived, arrived_labels = (
        lax.all_to_all(outgoing, "pa", split_axis=0, concat_axis=0, tiled=True),
        lax.all_to_all(
            labels.reshape(width_pa, sendable), "pa", split_axis=0, concat_axis=0, tiled=True
        ),
    )
    arrived_flat = arrived.reshape(width_pa * sendable, LEN, DIM)
    label_flat = arrived_labels.reshape(width_pa * sendable)
    local_emb = jnp.take(arrived_flat, arrival_index(label_flat), axis=0)
    lse_start = jnp.zeros((query_rows, passages_all), jnp.float32)
    forward_start = (lse_start,)
    key_pieces = lax.all_gather(local_emb, "pb", axis=0, tiled=True)
    begin_at = jnp.int32(0)
    shards = key_pieces.shape[0] // PD

    def forward_one_shard(turn, state):
        key_block = lax.dynamic_slice_in_dim(key_pieces, turn * PD, PD, 0)
        sums = log_total(similarity(queries, key_block))
        return lax.dynamic_update_slice(state, sums, (zero_index, turn * PD))

    lse_part = lax.fori_loop(0, shards, forward_one_shard, forward_start[0])
    kept_parts = tuple(
        (
            lax.dynamic_update_slice_in_dim(kept, key_pieces, begin_at, 0)
            for kept in forward_start[1:]
        )
    )
    forward_state = (lse_part,) + kept_parts
    lse_all = forward_state[0]
    score = lse_all.reshape(query_count, QT, passages_all).sum(axis=1) * (tau / QT)
    residual = (score - joined_target(bm25_rank[:, 0, :], dense_rank[:, 0, :])).astype(jnp.bfloat16)
    residual_rows = jnp.repeat(residual, QT, axis=0)
    residual_wide = residual_rows.astype(jnp.float32)
    start_state = (
        jnp.zeros((query_rows, DIM), jnp.float32),
        jnp.zeros((passages_all * LEN, DIM), jnp.float32),
    )
    backward_key_pieces = lax.all_gather(local_emb, "pb", axis=0, tiled=True)
    shards = backward_key_pieces.shape[0] // PD

    def backward_one_shard(turn, state):
        query_acc, emb_acc = state
        offset = turn * PD
        key_block = lax.dynamic_slice_in_dim(backward_key_pieces, turn * PD, PD, 0)
        raw = similarity(queries, key_block)
        log_sums = lax.dynamic_slice_in_dim(lse_all, offset, PD, 1)
        weights = jnp.exp(raw - log_sums[:, :, None])
        residual_cols = lax.dynamic_slice_in_dim(residual_wide, offset, PD, 1)
        coefficient = (
            ((residual_cols / QT)[:, :, None] * weights)
            .astype(jnp.bfloat16)
            .reshape(query_rows, PD * LEN)
        )
        query_acc = query_acc + jnp.dot(
            coefficient, key_block.reshape(PD * LEN, DIM), preferred_element_type=jnp.float32
        )
        emb_part = jnp.einsum("rk,rd->kd", coefficient, queries, preferred_element_type=jnp.float32)
        emb_acc = lax.dynamic_update_slice(emb_acc, emb_part, (offset * LEN, zero_index))
        return (query_acc, emb_acc)

    query_acc, emb_acc = lax.fori_loop(0, shards, backward_one_shard, start_state)
    query_grad = lax.psum_scatter(
        query_acc.astype(jnp.bfloat16), "pa", scatter_dimension=0, tiled=True
    ).astype(jnp.float32)
    emb_grad = lax.psum_scatter(
        emb_acc.astype(jnp.bfloat16), "pb", scatter_dimension=0, tiled=True
    ).reshape(PD, LEN, DIM)
    keep_back = label_flat >= 0
    returning = pick_rows(emb_grad, label_flat, keep_back).reshape(width_pa, sendable, LEN, DIM)
    came_back = lax.all_to_all(returning, "pa", split_axis=0, concat_axis=0, tiled=True).reshape(
        width_pa * sendable, LEN, DIM
    )
    slot_grad = pick_rows(came_back, target_at, filled).astype(jnp.float32).reshape(CAP * LEN, DIM)
    inner = jnp.sum(unit_rows * slot_grad, axis=-1, keepdims=True)
    slot_proj_grad = ((slot_grad - unit_rows * inner) * scaling).astype(jnp.bfloat16)
    hid_grad = jnp.einsum(
        "rd,hd->rh", slot_proj_grad, proj_weight, preferred_element_type=jnp.float32
    )
    encoder_output_derivative = hid_grad.astype(jnp.bfloat16).reshape(1, CAP, LEN, H)
    return (query_grad, encoder_output_derivative)


def solution(mesh):
    return jax.shard_map(
        on_device,
        mesh=mesh,
        in_specs=(
            P("pb", None),
            P("pb", "pa", None, None),
            P(),
            P("pb", "pa", None),
            P("pb", "pa", None),
            P("pb", "pa"),
        ),
        out_specs=(P(("pb", "pa"), None), P("pb", "pa", None, None)),
        check_vma=False,
    )
```

profile of v0, /device:TPU:2, one launch (start us, length us, event | category | flops | bytes accessed | tf_op | source)
XLA Modules:
  0.0 435.1 jit_solution(17482702924343745071)
XLA Ops:
  10.3 11.2 %all-to-all-start = ((s32[16,1,1]{2,1,0:T(1,128)}), s32[16,1,1]{2,1,0:T(1,128)S(1)}, u32[]{:S(2)}, u32[]{:S(2)}) async-start(s32[16,1,1]{2,1,0:T(1,128)} %copy.32), calls=%async_computation | async-start | bytes 16384 | tf_op jit(solution)/shard_map/all_to_all | solution.py:100
  21.6 3.5 multiply_reduce_fusion
  28.0 3.5 all-to-all-done
  31.5 6.1 %all-to-all-start.1 = ((bf16[16,1,128,128]{3,2,1,0:T(8,128)(2,1)}), bf16[16,1,128,128]{3,2,1,0:T(8,128)(2,1)S(1)}, u32[]{:S(2)}, u32[]{:S(2)}) async-start(bf16[16,1,128,128]{3,2,1,0:T(8,128)(2,1)} %fusion.13), calls=%async_computation.1 | async-start | bytes 1048576 | tf_op jit(solution)/shard_map/all_to_all | solution.py:99
  38.5 17.3 %all-to-all-done.1 = bf16[16,1,128,128]{3,2,1,0:T(8,128)(2,1)S(1)} async-done(((bf16[16,1,128,128]{3,2,1,0:T(8,128)(2,1)}), bf16[16,1,128,128]{3,2,1,0:T(8,128)(2,1)S(1)}, u32[]{:S(2)}, u32[]{:S(2)}) %all-to-all-start.1) | async-done | bytes 524320 | tf_op jit(solution)/shard_map/all_to_all | solution.py:99
  57.3 34.7 %all-gather.2.cloned.1.call-done = bf16[128,128,128]{2,1,0:T(8,128)(2,1)} async-done(((bf16[8,128,128]{2,1,0:T(8,128)(2,1)}), bf16[128,128,128]{2,1,0:T(8,128)(2,1)}) %all-gather.2.cloned.1.call-update) | async-done | bytes 4194320 | tf_op jit(solution)/shard_map/all_gather | solution.py:135
  92.0 23.9 %while.31 = (s32[]{:T(128)}, f32[256,128]{0,1:T(8,128)S(1)}, bf16[128,128,128]{2,1,0:T(8,128)(2,1)}, bf16[256,128]{1,0:T(8,128)(2,1)S(1)}, s32[]{:T(128)}, /*index=5*/s32[]{:T(128)}, s32[]{:T(128)}, s32[]{:T(128)}) while((s32[]{:T(128)}, f32[256,128]{0,1:T(8,128)S(1)}, bf16[128,128,128]{2,1,0:T(8,128)(2,1)}, bf16[256,128]{1,0:T(8,128)(2,1)S(1)}, ...), condition=%wide.region_9.11_spmd, body=%wide.region_6.10_spmd.sunk | while | flops 68155400 | bytes 2998419 | solution.py:118
  92.0 1.0 constant_dynamic-slice_fusion.5
  93.5 1.0 constant_dynamic-slice_fusion.5
  95.0 1.0 constant_dynamic-slice_fusion.5
  96.5 1.0 constant_dynamic-slice_fusion.5
  98.0 1.0 constant_dynamic-slice_fusion.5
  99.5 1.0 constant_dynamic-slice_fusion.5
  101.0 1.0 constant_dynamic-slice_fusion.5
  102.5 1.0 constant_dynamic-slice_fusion.5
  104.0 1.0 constant_dynamic-slice_fusion.5
  105.5 1.0 constant_dynamic-slice_fusion.5
  107.0 1.0 constant_dynamic-slice_fusion.5
  108.5 1.0 constant_dynamic-slice_fusion.5
  110.0 1.0 constant_dynamic-slice_fusion.5
  111.5 1.0 constant_dynamic-slice_fusion.5
  112.9 1.0 constant_dynamic-slice_fusion.5
  114.4 1.0 constant_dynamic-slice_fusion.5
  116.8 2.1 broadcast_in_dim.126
  119.0 66.3 %while.32 = (s32[]{:T(128)}, f32[256,128]{1,0:T(8,128)S(1)}, bf16[16384,128]{1,0:T(8,128)(2,1)}, f32[256,128]{0,1:T(8,128)}, bf16[128,128,128]{2,1,0:T(8,128)(2,...) while((s32[]{:T(128)}, f32[256,128]{1,0:T(8,128)S(1)}, ...), condition=%wide.region_12.14_spmd.clone, body=%wide.region_11.13_spmd.clone.sunk | while | flops 203229184 | bytes 7274743 | solution.py:158
  122.1 1.0 convolution_dynamic-update-slice_fusion.2
  123.1 1.0 constant_dynamic-slice_fusion.6
  126.2 1.0 convolution_dynamic-update-slice_fusion.2
  130.4 1.0 convolution_dynamic-update-slice_fusion.2
  134.5 1.0 convolution_dynamic-update-slice_fusion.2
  138.7 1.0 convolution_dynamic-update-slice_fusion.2
  142.8 1.0 convolution_dynamic-update-slice_fusion.2
  146.9 1.0 convolution_dynamic-update-slice_fusion.2
  151.1 1.0 convolution_dynamic-update-slice_fusion.2
  155.3 1.0 convolution_dynamic-update-slice_fusion.2
  159.4 1.0 convolution_dynamic-update-slice_fusion.2
  163.5 1.0 convolution_dynamic-update-slice_fusion.2
  167.7 1.0 convolution_dynamic-update-slice_fusion.2
  171.8 1.0 convolution_dynamic-update-slice_fusion.2
  175.9 1.0 convolution_dynamic-update-slice_fusion.2
  180.1 1.0 convolution_dynamic-update-slice_fusion.2
  184.2 1.0 convolution_dynamic-update-slice_fusion.2
  185.7 63.7 %reduce-scatter.5.cloned.1.call-done = bf16[1024,128]{1,0:T(8,128)(2,1)} async-done(((bf16[16384,128]{1,0:T(8,128)(2,1)}), bf16[1024,128]{1,0:T(8,128)(2,1)}) %reduce-scatter.5.cloned.1.call-update) | async-done | bytes 262160 | tf_op jit(solution)/shard_map/reduce_scatter | solution.py:162
  249.3 1.6 gather_fusion.1
  251.9 9.6 %all-to-all-start.2 = ((bf16[16,1,128,128]{3,2,1,0:T(8,128)(2,1)}), bf16[16,1,128,128]{3,2,1,0:T(8,128)(2,1)S(1)}, u32[]{:S(2)}, u32[]{:S(2)}) async-start(bf16[16,1,128,128]{3,2,1,0:T(8,128)(2,1)} %fusion.12), calls=%async_computation.4 | async-start | bytes 1048576 | tf_op jit(solution)/shard_map/all_to_all | solution.py:167
  262.3 160.6 %reduce-scatter.3.cloned.1.call-done = bf16[16,128]{1,0:T(8,128)(2,1)} async-done(((bf16[256,128]{1,0:T(8,128)(2,1)}), bf16[16,128]{1,0:T(8,128)(2,1)}) %reduce-scatter.3.cloned.1.call-update) | async-done | bytes 4112 | tf_op jit(solution)/shard_map/reduce_scatter | solution.py:159
  422.9 1.3 convert_element_type.66
  425.6 2.9 convolution_convert_fusion
  (188 shorter events, 68.9 us)
Async XLA Ops:
  7.2 14.4 %copy-start = (bf16[1024,128]{1,0:T(8,128)(2,1)S(1)}, bf16[1024,128]{1,0:T(8,128)(2,1)}, u32[]{:S(2)}) copy-start(bf16[1024,128]{1,0:T(8,128)(2,1)} %param.14) | copy-start | bytes 786436
  10.3 21.1 %all-to-all-start = ((s32[16,1,1]{2,1,0:T(1,128)}), s32[16,1,1]{2,1,0:T(1,128)S(1)}, u32[]{:S(2)}, u32[]{:S(2)}) async-start(s32[16,1,1]{2,1,0:T(1,128)} %copy.32), calls=%async_computation | async-start | bytes 16384 | tf_op jit(solution)/shard_map/all_to_all | solution.py:100
  25.1 1.0 copy-start.1
  25.1 32.2 %copy-start.4 = (s32[8,1,128]{2,1,0:T(1,128)S(1)}, s32[8,1,128]{2,1,0:T(1,128)}, u32[]{:S(2)}) copy-start(s32[8,1,128]{2,1,0:T(1,128)} %param.15) | copy-start | bytes 12292
  25.1 32.2 %copy-start.5 = (s32[8,1,128]{2,1,0:T(1,128)S(1)}, s32[8,1,128]{2,1,0:T(1,128)}, u32[]{:S(2)}) copy-start(s32[8,1,128]{2,1,0:T(1,128)} %param.16) | copy-start | bytes 12292
  25.1 66.9 %copy-start.3 = (bf16[256,128]{1,0:T(8,128)(2,1)S(1)}, bf16[256,128]{1,0:T(8,128)(2,1)}, u32[]{:S(2)}) copy-start(bf16[256,128]{1,0:T(8,128)(2,1)} %param.12) | copy-start | bytes 196612
  31.5 24.3 %all-to-all-start.1 = ((bf16[16,1,128,128]{3,2,1,0:T(8,128)(2,1)}), bf16[16,1,128,128]{3,2,1,0:T(8,128)(2,1)S(1)}, u32[]{:S(2)}, u32[]{:S(2)}) async-start(bf16[16,1,128,128]{3,2,1,0:T(8,128)(2,1)} %fusion.13), calls=%async_computation.1 | async-start | bytes 1048576 | tf_op jit(solution)/shard_map/all_to_all | solution.py:99
  37.6 54.4 %all-gather.2.cloned.1.call-start = ((), (), s32[]{:S(2)}) async-start(), calls=%async_computation.5 | async-start | bytes 4456448 | tf_op jit(solution)/shard_map/all_gather | solution.py:135
  57.2 192.1 %reduce-scatter.5.cloned.1.call-start = ((), (), s32[]{:S(2)}) async-start(), calls=%async_computation.7 | async-start | bytes 4456448 | tf_op jit(solution)/shard_map/reduce_scatter | solution.py:162
  185.2 77.0 %copy-start.6 = (s32[1,16]{1,0:T(1,128)S(1)}, s32[1,16]{1,0:T(1,128)}, u32[]{:S(2)}) copy-start(s32[1,16]{1,0:T(1,128)} %param.17) | copy-start | bytes 196
  185.2 239.7 %copy-start.2 = (f32[2048,128]{1,0:T(8,128)S(1)}, f32[2048,128]{1,0:T(8,128)}, u32[]{:S(2)}) copy-start(f32[2048,128]{1,0:T(8,128)} %copy-done.1) | copy-start | bytes 3145732
  251.9 172.3 %all-to-all-start.2 = ((bf16[16,1,128,128]{3,2,1,0:T(8,128)(2,1)}), bf16[16,1,128,128]{3,2,1,0:T(8,128)(2,1)S(1)}, u32[]{:S(2)}, u32[]{:S(2)}) async-start(bf16[16,1,128,128]{3,2,1,0:T(8,128)(2,1)} %fusion.12), calls=%async_computation.4 | async-start | bytes 1048576 | tf_op jit(solution)/shard_map/all_to_all | solution.py:167
  261.5 161.4 %reduce-scatter.3.cloned.1.call-start = ((), (), s32[]{:S(2)}) async-start(), calls=%async_computation.6 | async-start | bytes 69632 | tf_op jit(solution)/shard_map/reduce_scatter | solution.py:159
Sparse Core Ops, SparseCore 0:
  57.4 34.6 all-gather.1
  185.4 63.9 reduce-scatter.4
  266.0 156.8 reduce-scatter.2
where the time goes:
time: 437 us; the launch traced here: 435 us
  waiting for transfers between devices  280 us (64%)
  matrix products  44.9 us (10%)
  local copies, waits for them, and re-layouts  44.3 us (10%)
  starting transfers between devices  27.1 us (6%)
  other arithmetic  23.5 us (5%)
  between operations  14.1 us (3%)
    reduce_scatter x1, waiting for transfers between devices, on_device(): lax.psum_scatter(query_acc.astype(jnp.bfloat16), 'pa', scatter_dimension=...  161 us
    reduce_scatter x1, waiting for transfers between devices, on_device(): lax.psum_scatter(emb_acc.astype(jnp.bfloat16), 'pb', scatter_dimension=0,...  63.7 us
    all_gather x1, waiting for transfers between devices, on_device(): backward_key_pieces = lax.all_gather(local_emb, 'pb', axis=0, tiled=True)  34.7 us
    all_to_all x1, waiting for transfers between devices, on_device(): lax.all_to_all(outgoing, 'pa', split_axis=0, concat_axis=0, tiled=True)  17.3 us
    dot_general x16, matrix products, backward_one_shard(): jnp.einsum('rk,rd->kd', coefficient, queries, preferred_element_type=jnp....  16.2 us
    dynamic_slice x16, local copies, waits for them, and re-layouts, forward_one_shard(): key_block = lax.dynamic_slice_in_dim(key_pieces, turn * PD, PD, 0)  15.6 us
    dynamic_slice x16, local copies, waits for them, and re-layouts, backward_one_shard(): key_block = lax.dynamic_slice_in_dim(backward_key_pieces, turn * PD, PD, 0)  15.5 us
    dot_general x16, matrix products, backward_one_shard(): jnp.dot(coefficient, key_block.reshape(PD * LEN, DIM), preferred_element_...  11.8 us
  transfers between devices with their start and end apart: 6, of which 5 were waited for; matrix products, arithmetic and copies ran while one was open for 2% of the time, Pallas kernels for 0%

commit v1 on v0

v1 whole, which is shorter than its diff:
```python
import math

import jax
import jax.numpy as jnp
from jax import lax
from jax.experimental import pallas as pl
from jax.experimental.pallas import tpu as pltpu
from jax.sharding import PartitionSpec as P

DIM = 128
H = 1024
QT = 32
LEN = 128
PD = 8
DEPTH = 100
CAP = 16
ROWS = CAP * LEN
GROUPS = 16
GR = 256
GQ = GR // QT

tau = 0.05
inv_temp = 20.0
rrf_offset = 60.0
norm_eps = 1e-06
log2_scale = inv_temp / math.log(2.0)

bf16 = jnp.bfloat16
f32 = jnp.float32
NT = (((1,), (1,)), ((), ()))
NN = (((1,), (0,)), ((), ()))
HIGH = lax.Precision.HIGHEST


def swap(value, axis, mask):
    return lax.ppermute(value, axis, [(i, i ^ mask) for i in range(16)])


def shift_x(value, by):
    return lax.ppermute(
        value, "pb", [(i, ((((i >> 2) + by) % 4) << 2) | (i & 3)) for i in range(16)]
    )


SHIFTS = (0, 1, -1, 2)


def gather_pb(value):
    pair = jnp.stack([value, swap(value, "pb", 2)])
    plane = jnp.stack([pair] + [shift_x(pair, by) for by in SHIFTS[1:]])
    return jnp.stack([plane, swap(plane, "pb", 1)])


def reduce_pb(parts):
    plane = (parts[0].astype(f32) + swap(parts[1], "pb", 1).astype(f32)).astype(bf16)
    got = [shift_x(plane[a], -SHIFTS[a]) for a in (1, 2, 3)]
    pair = plane[0].astype(f32)
    for one in got:
        pair = pair + one.astype(f32)
    return pair[0] + swap(pair[1].astype(bf16), "pb", 2).astype(f32)


def gather_pa(value):
    low = jnp.stack([value] + [swap(value, "pa", j) for j in (1, 2, 3)])
    return jnp.concatenate([low] + [swap(low, "pa", 4 * j) for j in (1, 2, 3)])


def reduce_pa(value, me):
    ids = jnp.arange(16, dtype=jnp.int32)
    order = (ids[None, :] == (ids[:, None] ^ me)).astype(bf16)
    blocks = lax.dot_general(
        order, value.astype(bf16).reshape(16, 16 * DIM), NN, preferred_element_type=f32
    ).astype(bf16)
    blocks = blocks.reshape(4, 4, 16, DIM)
    total = blocks[:, 0].astype(f32)
    for j in (1, 2, 3):
        total = total + swap(blocks[:, j], "pa", j).astype(f32)
    blocks = total.astype(bf16)
    total = total[0]
    for j in (1, 2, 3):
        total = total + swap(blocks[j], "pa", 4 * j).astype(f32)
    return total


def project_kernel(hid_ref, w_ref, proj_ref, emb_ref, emb_t_ref):
    proj = lax.dot_general(hid_ref[...], w_ref[...], NN, preferred_element_type=f32)
    scaling = lax.rsqrt(jnp.sum(proj * proj, axis=-1, keepdims=True) + norm_eps)
    unit = proj * scaling
    proj_ref[...] = proj
    emb_ref[...] = unit.astype(bf16)
    emb_t_ref[...] = unit.T.astype(bf16)


def project(hid, weight):
    step = 512
    return pl.pallas_call(
        project_kernel,
        grid=(ROWS // step,),
        in_specs=[
            pl.BlockSpec((step, H), lambda i: (i, 0)),
            pl.BlockSpec((H, DIM), lambda i: (0, 0)),
        ],
        out_specs=[
            pl.BlockSpec((step, DIM), lambda i: (i, 0)),
            pl.BlockSpec((step, DIM), lambda i: (i, 0)),
            pl.BlockSpec((DIM, step), lambda i: (0, i)),
        ],
        out_shape=[
            jax.ShapeDtypeStruct((ROWS, DIM), f32),
            jax.ShapeDtypeStruct((ROWS, DIM), bf16),
            jax.ShapeDtypeStruct((DIM, ROWS), bf16),
        ],
        compiler_params=pltpu.CompilerParams(vmem_limit_bytes=24 * 2**20),
        cost_estimate=pl.CostEstimate(
            flops=2 * ROWS * H * DIM, bytes_accessed=ROWS * (2 * H + 8 * DIM), transcendentals=0
        ),
        name="project",
    )(hid, weight)


def score_kernel(q_ref, emb_ref, emb_t_ref, pick_ref, target_ref, qg_ref, eg_ref, p_ref, c_ref):
    g = pl.program_id(0)

    @pl.when(g == 0)
    def _():
        eg_ref[...] = jnp.zeros_like(eg_ref)

    queries = q_ref[0, :GR, :]
    tops, sums = [], []
    for k in range(CAP):
        rows = slice(k * LEN, (k + 1) * LEN)
        raw = lax.dot_general(emb_ref[rows, :], queries, NT, preferred_element_type=f32)
        top = jnp.max(raw, axis=0, keepdims=True)
        p = jnp.exp2((raw - top) * log2_scale)
        p_ref[rows, :] = p
        tops.append(top)
        sums.append(jnp.sum(p, axis=0, keepdims=True))
    top = jnp.concatenate(tops, axis=0)
    total = jnp.concatenate(sums, axis=0)
    lse = inv_temp * top + jnp.log(total)
    row_q = lax.broadcasted_iota(jnp.int32, (GR, GR), 0) // QT
    col_q = lax.broadcasted_iota(jnp.int32, (GR, GR), 1) // QT
    same = (row_q == col_q).astype(f32)
    score = lax.dot_general(lse, same, NN, precision=HIGH, preferred_element_type=f32) * (tau / QT)
    wide = (
        lax.broadcasted_iota(jnp.int32, (LEN, GR), 0)
        == g * GQ + lax.broadcasted_iota(jnp.int32, (LEN, GR), 1) // QT
    ).astype(f32)
    pick = pick_ref[...]
    own = lax.dot_general(pick, target_ref[...], NN, precision=HIGH, preferred_element_type=f32)
    target = lax.dot_general(own, wide, NN, precision=HIGH, preferred_element_type=f32)
    residual = (score - target).astype(bf16).astype(f32) * jnp.sum(pick, axis=1, keepdims=True)
    factor = (residual / QT) / total
    for k in range(CAP):
        rows = slice(k * LEN, (k + 1) * LEN)
        c_ref[rows, :] = (p_ref[rows, :] * factor[k : k + 1, :]).astype(bf16)
    eg_ref[...] += lax.dot_general(c_ref[...], queries, NN, preferred_element_type=f32)
    qg = lax.dot_general(emb_t_ref[...], c_ref[...], NN, preferred_element_type=f32)
    qg_ref[0] = qg.T.astype(bf16)


def score_and_gradients(gathered, emb, emb_t, pick, target):
    height = gathered.shape[1]
    return pl.pallas_call(
        score_kernel,
        grid=(GROUPS,),
        in_specs=[
            pl.BlockSpec((1, height, DIM), lambda g: (g, 0, 0)),
            pl.BlockSpec((ROWS, DIM), lambda g: (0, 0)),
            pl.BlockSpec((DIM, ROWS), lambda g: (0, 0)),
            pl.BlockSpec((CAP, LEN), lambda g: (0, 0)),
            pl.BlockSpec((LEN, LEN), lambda g: (0, 0)),
        ],
        out_specs=[
            pl.BlockSpec((1, GR, DIM), lambda g: (g, 0, 0)),
            pl.BlockSpec((ROWS, DIM), lambda g: (0, 0)),
        ],
        out_shape=[
            jax.ShapeDtypeStruct((GROUPS, GR, DIM), bf16),
            jax.ShapeDtypeStruct((ROWS, DIM), f32),
        ],
        scratch_shapes=[pltpu.VMEM((ROWS, GR), f32), pltpu.VMEM((ROWS, GR), bf16)],
        compiler_params=pltpu.CompilerParams(vmem_limit_bytes=32 * 2**20),
        cost_estimate=pl.CostEstimate(
            flops=6 * GROUPS * GR * ROWS * DIM,
            bytes_accessed=5 * 2**20,
            transcendentals=GROUPS * GR * ROWS,
        ),
        name="score_and_gradients",
    )(gathered, emb, emb_t, pick, target)


def hidden_kernel(eg_ref, proj_ref, w_ref, out_ref):
    proj = proj_ref[...]
    scaling = lax.rsqrt(jnp.sum(proj * proj, axis=-1, keepdims=True) + norm_eps)
    unit = proj * scaling
    slot_grad = eg_ref[...].astype(bf16).astype(f32)
    inner = jnp.sum(unit * slot_grad, axis=-1, keepdims=True)
    proj_grad = ((slot_grad - unit * inner) * scaling).astype(bf16)
    out_ref[...] = lax.dot_general(
        proj_grad, w_ref[...], NT, preferred_element_type=f32
    ).astype(bf16)


def hidden_gradient(emb_grad, proj, weight):
    step = 512
    return pl.pallas_call(
        hidden_kernel,
        grid=(ROWS // step,),
        in_specs=[
            pl.BlockSpec((step, DIM), lambda i: (i, 0)),
            pl.BlockSpec((step, DIM), lambda i: (i, 0)),
            pl.BlockSpec((H, DIM), lambda i: (0, 0)),
        ],
        out_specs=pl.BlockSpec((step, H), lambda i: (i, 0)),
        out_shape=jax.ShapeDtypeStruct((ROWS, H), bf16),
        compiler_params=pltpu.CompilerParams(vmem_limit_bytes=24 * 2**20),
        cost_estimate=pl.CostEstimate(
            flops=2 * ROWS * H * DIM, bytes_accessed=ROWS * (2 * H + 8 * DIM), transcendentals=0
        ),
        name="hidden_gradient",
    )(emb_grad, proj, weight)


def rank_term(rank):
    return jnp.where(rank < DEPTH, rrf_offset / (rrf_offset + rank), 0.0)


def on_device(
    queries, encoder_outputs, proj_weight, bm25_rank, dense_rank, custodian_document_index
):
    me_pb, me_pa = lax.axis_index("pb"), lax.axis_index("pa")
    ids = jnp.arange(LEN, dtype=jnp.int32)
    slot_ids = custodian_document_index[0]
    place = jnp.where(slot_ids >= 0, slot_ids ^ (me_pa * PD), -1)
    pick = (place[:, None] == ids[None, :]).astype(f32)
    ranks = jnp.concatenate([bm25_rank[:, 0, :], dense_rank[:, 0, :]]).astype(bf16)
    gathered = gather_pb(jnp.concatenate([queries, ranks])).reshape(GROUPS, GR + 2 * GQ, DIM)
    proj, emb, emb_t = project(encoder_outputs.reshape(ROWS, H), proj_weight)
    own = (ids[None, :] == me_pb * PD + jnp.arange(PD, dtype=jnp.int32)[:, None]).astype(bf16)
    ranks = jnp.einsum("lm,grm->lgr", own, gathered[:, GR:, :], preferred_element_type=f32)
    target = rank_term(ranks[:, :, :GQ]) + rank_term(ranks[:, :, GQ:])
    target = gather_pa(target.reshape(PD, LEN)).reshape(LEN, LEN)
    query_parts, emb_grad = score_and_gradients(gathered, emb, emb_t, pick, target)
    own_sum = reduce_pb(query_parts.reshape(2, 4, 2, GR, DIM))
    query_grad = reduce_pa(own_sum, me_pa)
    hidden = hidden_gradient(emb_grad, proj, proj_weight)
    return (query_grad, hidden.reshape(1, CAP, LEN, H))


def solution(mesh):
    return jax.shard_map(
        on_device,
        mesh=mesh,
        in_specs=(
            P("pb", None),
            P("pb", "pa", None, None),
            P(),
            P("pb", "pa", None),
            P("pb", "pa", None),
            P("pb", "pa"),
        ),
        out_specs=(P(("pb", "pa"), None), P("pb", "pa", None, None)),
        check_vma=False,
    )
```

time: 437 us -> 111 us (0.25)
  waiting for transfers between devices: 280 us -> 29.3 us
  matrix products: 44.9 us -> 0.47 us
  local copies, waits for them, and re-layouts: 44.3 us -> 6.41 us
  Pallas kernels: 0 us -> 32.3 us
  other arithmetic: 23.5 us -> 3.42 us
  between operations: 14.1 us -> 0.89 us
  starting transfers between devices: 27.1 us -> 37.5 us
    reduce_scatter x2 -> x0, waiting for transfers between devices: 224 us -> none  [the longest x1 161 us: on_device(): lax.psum_scatter(query_acc.astype(jnp.bfloat16), 'pa', scatter_dimension=...]
    dot_general x66 -> x2, matrix products: 44.9 us -> 0.47 us  [the longest x1 0.27 us: on_device(): jnp.einsum('lm,grm->lgr', own, gathered[:, GR:, :], preferred_element_typ...]
    ppermute x0 -> x22, starting transfers between devices: none -> 37.5 us  [the longest x16 28.4 us: swap(): return lax.ppermute(value, axis, [(i, i ^ mask) for i in range(16)])]
    all_gather x1 -> x0, waiting for transfers between devices: 34.7 us -> none  [on_device(): backward_key_pieces = lax.all_gather(local_emb, 'pb', axis=0, tiled=True)]
    pallas_call x0 -> x3, Pallas kernels: none -> 32.3 us  [the longest x1 25.9 us: score_and_gradients(): pl.pallas_call(score_kernel, grid=(GROUPS,), in_specs=[pl.BlockSpec((1, h...]
    dynamic_slice x32 -> x0, local copies, waits for them, and re-layouts: 31 us -> none  [the longest x16 15.6 us: forward_one_shard(): key_block = lax.dynamic_slice_in_dim(key_pieces, turn * PD, PD, 0)]
    ppermute x0 -> x22, waiting for transfers between devices: none -> 29.3 us  [the longest x16 22.7 us: swap(): return lax.ppermute(value, axis, [(i, i ^ mask) for i in range(16)])]
    all_to_all x3 -> x0, starting transfers between devices: 27 us -> none  [the longest x1 11.2 us: on_device(): lax.all_to_all(labels.reshape(width_pa, sendable), 'pa', split_axis=0, co...]
  transfers between devices with their start and end apart: 6 -> 22, of which waited for: 5 -> 14; matrix products, arithmetic and copies ran while one was open for 2% -> 0% of each run, Pallas kernels for 0% -> 6%
where the time goes in v1:
time: 111 us; the launch traced here: 110 us
  starting transfers between devices  37.5 us (34%)
  Pallas kernels  32.3 us (29%)
  waiting for transfers between devices  29.3 us (26%)
  local copies, waits for them, and re-layouts  6.41 us (6%)
  other arithmetic  3.42 us (3%)
    ppermute x16, starting transfers between devices, swap(): return lax.ppermute(value, axis, [(i, i ^ mask) for i in range(16)])  28.4 us
    pallas_call x1, Pallas kernels, score_and_gradients(): pl.pallas_call(score_kernel, grid=(GROUPS,), in_specs=[pl.BlockSpec((1, h...  25.9 us
    ppermute x16, waiting for transfers between devices, swap(): return lax.ppermute(value, axis, [(i, i ^ mask) for i in range(16)])  22.7 us
    ppermute x6, starting transfers between devices, shift_x(): lax.ppermute(value, 'pb', [(i, ((i >> 2) + by) % 4 << 2 | i & 3) for i in...  9.05 us
    ppermute x6, waiting for transfers between devices, shift_x(): lax.ppermute(value, 'pb', [(i, ((i >> 2) + by) % 4 << 2 | i & 3) for i in...  6.66 us
    unnamed x26, local copies, waits for them, and re-layouts  5.9 us
    pallas_call x1, Pallas kernels, hidden_gradient(): pl.pallas_call(hidden_kernel, grid=(ROWS // step,), in_specs=[pl.BlockSpe...  3.97 us
    pallas_call x1, Pallas kernels, project(): pl.pallas_call(project_kernel, grid=(ROWS // step,), in_specs=[pl.BlockSp...  2.45 us
  transfers between devices with their start and end apart: 22, of which 14 were waited for; matrix products, arithmetic and copies ran while one was open for 0% of the time, Pallas kernels for 6%

profile of v1, /device:TPU:2, one launch (start us, length us, event | category | flops | bytes accessed | tf_op | source)
XLA Modules:
  0.0 110.3 jit_solution(9215589519268938114)
XLA Ops:
  0.6 0.7 convert.14
  1.3 0.7 convert.15
  2.0 0.9 fusion.20
  2.9 1.7 %collective-permute-start = (bf16[272,128]{1,0:T(8,128)(2,1)S(1)}, bf16[272,128]{1,0:T(8,128)(2,1)S(1)}, u32[]{:S(2)}, u32[]{:S(2)}) collective-permute-start(bf16[272,128]{1,0:T(8,128)(2,1)S(1)} %get-tuple-element.24), channel_id=1, source_target_pairs={{0,32},{16,48},{32,0},{48,16},{64,96},{80,112},{96,64},{112,80},{1... | collective-permute-start | bytes 208904 | tf_op jit(solution)/shard_map/ppermute | solution.py:36
  4.6 2.7 %collective-permute-done = bf16[272,128]{1,0:T(8,128)(2,1)S(1)} collective-permute-done((bf16[272,128]{1,0:T(8,128)(2,1)S(1)}, bf16[272,128]{1,0:T(8,128)(2,1)S(1)}, u32[]{:S(2)}, u32[]{:S(2)}) %collective-permute-start) | collective-permute-done | bytes 69664 | tf_op jit(solution)/shard_map/ppermute | solution.py:36
  7.3 2.3 %collective-permute-start.2 = (bf16[2,272,128]{2,1,0:T(8,128)(2,1)S(1)}, bf16[2,272,128]{2,1,0:T(8,128)(2,1)S(1)}, u32[]{:S(2)}, u32[]{:S(2)}) collective-permute-start(bf16[2,272,128]{2,1,0:T(8,128)(2,1)S(1)} %get-tuple-element.22), channel_id=1, source_target_pairs={{0,192},{16,208},{32,224},{48,240},{64,0},{80,16},{96,32},{112,48}... | collective-permute-start | bytes 417800 | tf_op jit(solution)/shard_map/ppermute | solution.py:40
  9.7 3.1 %collective-permute-start.3 = (bf16[2,272,128]{2,1,0:T(8,128)(2,1)S(1)}, bf16[2,272,128]{2,1,0:T(8,128)(2,1)S(1)}, u32[]{:S(2)}, u32[]{:S(2)}) collective-permute-start(bf16[2,272,128]{2,1,0:T(8,128)(2,1)S(1)} %get-tuple-element.22), channel_id=1, source_target_pairs={{0,128},{16,144},{32,160},{48,176},{64,192},{80,208},{96,224},{112... | collective-permute-start | bytes 417800 | tf_op jit(solution)/shard_map/ppermute | solution.py:40
  12.7 2.2 %copy-done = bf16[1,16,128,1024]{3,2,1,0:T(8,128)(2,1)S(1)} copy-done((bf16[1,16,128,1024]{3,2,1,0:T(8,128)(2,1)S(1)}, bf16[1,16,128,1024]{3,2,1,0:T(8,128)(2,1)}, u32[]{:S(2)}) %copy-start) | copy-done | bytes 4194328
  14.9 0.9 copy-done.1
  15.9 2.4 %project.1 = (f32[2048,128]{1,0:T(8,128)S(1)}, bf16[2048,128]{1,0:T(8,128)(2,1)S(1)}, bf16[128,2048]{1,0:T(8,128)(2,1)S(1)}) custom-call(bf16[2048,1024]{1,0:T(8,128)(2,1)S(1)} %bitcast.91, bf16[1024,128]{1,0:T(8,128)(2,1)S(1)} %copy-done.1), custom_call_target="tpu_custom_call" | custom-call | flops 536870912 | bytes 6291456 | tf_op jit(solution)/shard_map/project/pallas_call | solution.py:96
  18.6 0.4 copy-done.7
  19.1 1.4 %collective-permute-done.4 = bf16[4,2,272,128]{3,2,1,0:T(8,128)(2,1)S(1)} collective-permute-done((bf16[4,2,272,128]{3,2,1,0:T(8,128)(2,1)S(1)}, bf16[4,2,272,128]{3,2,1,0:T(8,128)(2,1)S(1)}, u32[]{:S(2)}, u32[]{:S(2)}) %collective-permute-start.4) | collective-permute-done | bytes 557088 | tf_op jit(solution)/shard_map/ppermute | solution.py:36
  20.7 0.3 fusion.7
  21.5 4.6 %collective-permute-start.7 = (f32[8,128]{1,0:T(8,128)S(1)}, f32[8,128]{1,0:T(8,128)S(1)}, u32[]{:S(2)}, u32[]{:S(2)}) collective-permute-start(f32[8,128]{1,0:T(8,128)S(1)} %reshape.65), channel_id=1, source_target_pairs={{0,3},{1,2},{2,1},{3,0},{4,7},{5,6},{6,5},{7,4},{8,11},{9,10},{10,... | collective-permute-start | bytes 12296 | tf_op jit(solution)/shard_map/ppermute | solution.py:36
  26.2 0.1 collective-permute-start.6
  26.3 0.6 collective-permute-start.5
  26.8 0.9 collective-permute-done.7
  27.8 2.0 %collective-permute-done.6 = f32[8,128]{1,0:T(8,128)S(1)} collective-permute-done((f32[8,128]{1,0:T(8,128)S(1)}, f32[8,128]{1,0:T(8,128)S(1)}, u32[]{:S(2)}, u32[]{:S(2)}) %collective-permute-start.6) | collective-permute-done | bytes 4128 | tf_op jit(solution)/shard_map/ppermute | solution.py:36
  29.8 1.6 %collective-permute-done.5 = f32[8,128]{1,0:T(8,128)S(1)} collective-permute-done((f32[8,128]{1,0:T(8,128)S(1)}, f32[8,128]{1,0:T(8,128)S(1)}, u32[]{:S(2)}, u32[]{:S(2)}) %collective-permute-start.5) | collective-permute-done | bytes 4128 | tf_op jit(solution)/shard_map/ppermute | solution.py:36
  31.4 6.3 %collective-permute-start.10 = (f32[4,8,128]{2,1,0:T(8,128)S(1)}, f32[4,8,128]{2,1,0:T(8,128)S(1)}, u32[]{:S(2)}, u32[]{:S(2)}) collective-permute-start(f32[4,8,128]{2,1,0:T(8,128)S(1)} %pad_maximum_fusion.4), channel_id=1, source_target_pairs={{0,12},{1,13},{2,14},{3,15},{4,8},{5,9},{6,10},{7,11},{8,4},{9,5},... | collective-permute-start | bytes 49160 | tf_op jit(solution)/shard_map/ppermute | solution.py:36
  37.7 0.9 collective-permute-start.9
  38.6 1.5 %collective-permute-start.8 = (f32[4,8,128]{2,1,0:T(8,128)S(1)}, f32[4,8,128]{2,1,0:T(8,128)S(1)}, u32[]{:S(2)}, u32[]{:S(2)}) collective-permute-start(f32[4,8,128]{2,1,0:T(8,128)S(1)} %pad_maximum_fusion.4), channel_id=1, source_target_pairs={{0,4},{1,5},{2,6},{3,7},{4,0},{5,1},{6,2},{7,3},{8,12},{9,13},{10,... | collective-permute-start | bytes 49160 | tf_op jit(solution)/shard_map/ppermute | solution.py:36
  40.1 3.2 %collective-permute-done.8 = f32[4,8,128]{2,1,0:T(8,128)S(1)} collective-permute-done((f32[4,8,128]{2,1,0:T(8,128)S(1)}, f32[4,8,128]{2,1,0:T(8,128)S(1)}, u32[]{:S(2)}, u32[]{:S(2)}) %collective-permute-start.8) | collective-permute-done | bytes 16416 | tf_op jit(solution)/shard_map/ppermute | solution.py:36
  43.2 2.1 %collective-permute-done.9 = f32[4,8,128]{2,1,0:T(8,128)S(1)} collective-permute-done((f32[4,8,128]{2,1,0:T(8,128)S(1)}, f32[4,8,128]{2,1,0:T(8,128)S(1)}, u32[]{:S(2)}, u32[]{:S(2)}) %collective-permute-start.9) | collective-permute-done | bytes 16416 | tf_op jit(solution)/shard_map/ppermute | solution.py:36
  45.4 1.0 copy-done.4
  46.4 1.0 copy-done.6
  47.4 25.9 %score_and_gradients.1 = (bf16[16,256,128]{2,1,0:T(8,128)(2,1)S(1)}, f32[2048,128]{1,0:T(8,128)S(1)}) custom-call(bf16[16,272,128]{2,1,0:T(8,128)(2,1)S(1)} %bitcast.93, bf16[2048,128]{1,0:T(8,128)(2,1)S(1)} %copy-done.4, bf16[128,2048]{1,0:T(8,128)(2,1)S(1)} %copy-done.6, f32[16,128]{1,0:T(8,128)S(1)} %fusion.14.pick_ref, f32[128,128]{1,0:T(8,128)S(1)} %bitcast.94), custom_call_target="tpu_custom_call" | custom-call | flops 6442450944 | bytes 5242880 | tf_op jit(solution)/shard_map/score_and_gradients/pallas_call | solution.py:164
  73.5 1.9 %collective-permute-done.11 = bf16[4,2,256,128]{3,2,1,0:T(8,128)(2,1)S(1)} collective-permute-done((bf16[4,2,256,128]{3,2,1,0:T(8,128)(2,1)S(1)}, bf16[4,2,256,128]{3,2,1,0:T(8,128)(2,1)S(1)}, u32[]{:S(2)}, u32[]{:S(2)}) %collective-permute-start.11) | collective-permute-done | bytes 524320 | tf_op jit(solution)/shard_map/ppermute | solution.py:36
  75.4 0.1 fusion.1
  75.6 0.5 collective-permute-start.12
  76.2 0.5 collective-permute-start.14
  76.7 2.5 %collective-permute-start.13 = (bf16[2,256,128]{2,1,0:T(8,128)(2,1)S(1)}, bf16[2,256,128]{2,1,0:T(8,128)(2,1)S(1)}, u32[]{:S(2)}, u32[]{:S(2)}) collective-permute-start(bf16[2,256,128]{2,1,0:T(8,128)(2,1)S(1)} %get-tuple-element.20), channel_id=1, source_target_pairs={{0,64},{16,80},{32,96},{48,112},{64,128},{80,144},{96,160},{112,17... | collective-permute-start | bytes 393224 | tf_op jit(solution)/shard_map/ppermute | solution.py:40
  79.2 4.8 %collective-permute-done.12 = bf16[2,256,128]{2,1,0:T(8,128)(2,1)S(1)} collective-permute-done((bf16[2,256,128]{2,1,0:T(8,128)(2,1)S(1)}, bf16[2,256,128]{2,1,0:T(8,128)(2,1)S(1)}, u32[]{:S(2)}, u32[]{:S(2)}) %collective-permute-start.12) | collective-permute-done | bytes 131104 | tf_op jit(solution)/shard_map/ppermute | solution.py:40
  84.1 1.8 %collective-permute-done.13 = bf16[2,256,128]{2,1,0:T(8,128)(2,1)S(1)} collective-permute-done((bf16[2,256,128]{2,1,0:T(8,128)(2,1)S(1)}, bf16[2,256,128]{2,1,0:T(8,128)(2,1)S(1)}, u32[]{:S(2)}, u32[]{:S(2)}) %collective-permute-start.13) | collective-permute-done | bytes 131104 | tf_op jit(solution)/shard_map/ppermute | solution.py:40
  86.0 0.9 collective-permute-start.15
  86.9 3.6 %collective-permute-done.15 = bf16[256,128]{1,0:T(8,128)(2,1)S(1)} collective-permute-done((bf16[256,128]{1,0:T(8,128)(2,1)S(1)}, bf16[256,128]{1,0:T(8,128)(2,1)S(1)}, u32[]{:S(2)}, u32[]{:S(2)}) %collective-permute-start.15) | collective-permute-done | bytes 65568 | tf_op jit(solution)/shard_map/ppermute | solution.py:36
  90.6 0.2 fusion
  90.8 0.6 collective-permute-start.16
  91.4 1.0 collective-permute-start.17
  92.4 3.5 %collective-permute-start.18 = (bf16[4,16,128]{2,1,0:T(8,128)(2,1)S(1)}, bf16[4,16,128]{2,1,0:T(8,128)(2,1)S(1)}, u32[]{:S(2)}, u32[]{:S(2)}) collective-permute-start(bf16[4,16,128]{2,1,0:T(8,128)(2,1)S(1)} %get-tuple-element.27), channel_id=1, source_target_pairs={{0,3},{1,2},{2,1},{3,0},{4,7},{5,6},{6,5},{7,4},{8,11},{9,10},{10,... | collective-permute-start | bytes 49160 | tf_op jit(solution)/shard_map/ppermute | solution.py:36
  95.9 0.2 collective-permute-done.16
  96.1 2.4 %collective-permute-done.18 = bf16[4,16,128]{2,1,0:T(8,128)(2,1)S(1)} collective-permute-done((bf16[4,16,128]{2,1,0:T(8,128)(2,1)S(1)}, bf16[4,16,128]{2,1,0:T(8,128)(2,1)S(1)}, u32[]{:S(2)}, u32[]{:S(2)}) %collective-permute-start.18) | collective-permute-done | bytes 16416 | tf_op jit(solution)/shard_map/ppermute | solution.py:36
  98.6 1.7 %collective-permute-start.19 = (bf16[16,128]{1,0:T(8,128)(2,1)S(1)}, bf16[16,128]{1,0:T(8,128)(2,1)S(1)}, u32[]{:S(2)}, u32[]{:S(2)}) collective-permute-start(bf16[16,128]{1,0:T(8,128)(2,1)S(1)} %get-tuple-element.30), channel_id=1, source_target_pairs={{0,4},{1,5},{2,6},{3,7},{4,0},{5,1},{6,2},{7,3},{8,12},{9,13},{10,... | collective-permute-start | bytes 12296 | tf_op jit(solution)/shard_map/ppermute | solution.py:36
  100.3 1.9 %collective-permute-start.21 = (bf16[16,128]{1,0:T(8,128)(2,1)S(1)}, bf16[16,128]{1,0:T(8,128)(2,1)S(1)}, u32[]{:S(2)}, u32[]{:S(2)}) collective-permute-start(bf16[16,128]{1,0:T(8,128)(2,1)S(1)} %get-tuple-element.31), channel_id=1, source_target_pairs={{0,12},{1,13},{2,14},{3,15},{4,8},{5,9},{6,10},{7,11},{8,4},{9,5},... | collective-permute-start | bytes 12296 | tf_op jit(solution)/shard_map/ppermute | solution.py:36
  102.2 3.0 %collective-permute-start.20 = (bf16[16,128]{1,0:T(8,128)(2,1)S(1)}, bf16[16,128]{1,0:T(8,128)(2,1)S(1)}, u32[]{:S(2)}, u32[]{:S(2)}) collective-permute-start(bf16[16,128]{1,0:T(8,128)(2,1)S(1)} %get-tuple-element.32), channel_id=1, source_target_pairs={{0,8},{1,9},{2,10},{3,11},{4,12},{5,13},{6,14},{7,15},{8,0},{9,1},... | collective-permute-start | bytes 12296 | tf_op jit(solution)/shard_map/ppermute | solution.py:36
  105.2 4.0 %hidden_gradient.1 = bf16[2048,1024]{1,0:T(8,128)(2,1)} custom-call(f32[2048,128]{1,0:T(8,128)S(1)} %get-tuple-element.10.eg_ref, f32[2048,128]{1,0:T(8,128)S(1)} %get-tuple-element.11.proj_ref, bf16[1024,128]{1,0:T(8,128)(2,1)S(1)} %copy-done.2), custom_call_target="tpu_custom_call" | custom-call | flops 536870912 | bytes 6291456 | tf_op jit(solution)/shard_map/hidden_gradient/pallas_call | solution.py:207
  109.2 0.5 collective-permute-done.20
  109.7 0.6 fusion.13
  (55 shorter events, 1.4 us)
Async XLA Ops:
  2.9 4.4 %collective-permute-start = (bf16[272,128]{1,0:T(8,128)(2,1)S(1)}, bf16[272,128]{1,0:T(8,128)(2,1)S(1)}, u32[]{:S(2)}, u32[]{:S(2)}) collective-permute-start(bf16[272,128]{1,0:T(8,128)(2,1)S(1)} %get-tuple-element.24), channel_id=1, source_target_pairs={{0,32},{16,48},{32,0},{48,16},{64,96},{80,112},{96,64},{112,80},{1... | collective-permute-start | bytes 208904 | tf_op jit(solution)/shard_map/ppermute | solution.py:36
  7.3 11.1 %collective-permute-start.2 = (bf16[2,272,128]{2,1,0:T(8,128)(2,1)S(1)}, bf16[2,272,128]{2,1,0:T(8,128)(2,1)S(1)}, u32[]{:S(2)}, u32[]{:S(2)}) collective-permute-start(bf16[2,272,128]{2,1,0:T(8,128)(2,1)S(1)} %get-tuple-element.22), channel_id=1, source_target_pairs={{0,192},{16,208},{32,224},{48,240},{64,0},{80,16},{96,32},{112,48}... | collective-permute-start | bytes 417800 | tf_op jit(solution)/shard_map/ppermute | solution.py:40
  9.7 8.7 %collective-permute-start.1 = (bf16[2,272,128]{2,1,0:T(8,128)(2,1)S(1)}, bf16[2,272,128]{2,1,0:T(8,128)(2,1)S(1)}, u32[]{:S(2)}, u32[]{:S(2)}) collective-permute-start(bf16[2,272,128]{2,1,0:T(8,128)(2,1)S(1)} %get-tuple-element.22), channel_id=1, source_target_pairs={{0,64},{16,80},{32,96},{48,112},{64,128},{80,144},{96,160},{112,17... | collective-permute-start | bytes 417800 | tf_op jit(solution)/shard_map/ppermute | solution.py:40
  9.7 8.7 %collective-permute-start.3 = (bf16[2,272,128]{2,1,0:T(8,128)(2,1)S(1)}, bf16[2,272,128]{2,1,0:T(8,128)(2,1)S(1)}, u32[]{:S(2)}, u32[]{:S(2)}) collective-permute-start(bf16[2,272,128]{2,1,0:T(8,128)(2,1)S(1)} %get-tuple-element.22), channel_id=1, source_target_pairs={{0,128},{16,144},{32,160},{48,176},{64,192},{80,208},{96,224},{112... | collective-permute-start | bytes 417800 | tf_op jit(solution)/shard_map/ppermute | solution.py:40
  12.7 2.2 %copy-start = (bf16[1,16,128,1024]{3,2,1,0:T(8,128)(2,1)S(1)}, bf16[1,16,128,1024]{3,2,1,0:T(8,128)(2,1)}, u32[]{:S(2)}) copy-start(bf16[1,16,128,1024]{3,2,1,0:T(8,128)(2,1)} %param.7) | copy-start | bytes 12582916
  14.9 0.9 copy-start.1
  18.3 2.3 %copy-start.3 = (bf16[2048,128]{1,0:T(8,128)(2,1)}, bf16[2048,128]{1,0:T(8,128)(2,1)S(1)}, u32[]{:S(2)}) copy-start(bf16[2048,128]{1,0:T(8,128)(2,1)S(1)} %get-tuple-element.7.emb_ref) | copy-start | bytes 1572868
  18.4 2.3 %copy-start.5 = (bf16[128,2048]{1,0:T(8,128)(2,1)}, bf16[128,2048]{1,0:T(8,128)(2,1)S(1)}, u32[]{:S(2)}) copy-start(bf16[128,2048]{1,0:T(8,128)(2,1)S(1)} %get-tuple-element.8.emb_t_ref) | copy-start | bytes 1572868
  18.4 0.7 copy-start.7
  18.5 2.0 %collective-permute-start.4 = (bf16[4,2,272,128]{3,2,1,0:T(8,128)(2,1)S(1)}, bf16[4,2,272,128]{3,2,1,0:T(8,128)(2,1)S(1)}, u32[]{:S(2)}, u32[]{:S(2)}) collective-permute-start(bf16[4,2,272,128]{3,2,1,0:T(8,128)(2,1)S(1)} %get-tuple-element.17), channel_id=1, source_target_pairs={{0,16},{16,0},{32,48},{48,32},{64,80},{80,64},{96,112},{112,96},{1... | collective-permute-start | bytes 1671176 | tf_op jit(solution)/shard_map/ppermute | solution.py:36
  21.5 6.2 %collective-permute-start.7 = (f32[8,128]{1,0:T(8,128)S(1)}, f32[8,128]{1,0:T(8,128)S(1)}, u32[]{:S(2)}, u32[]{:S(2)}) collective-permute-start(f32[8,128]{1,0:T(8,128)S(1)} %reshape.65), channel_id=1, source_target_pairs={{0,3},{1,2},{2,1},{3,0},{4,7},{5,6},{6,5},{7,4},{8,11},{9,10},{10,... | collective-permute-start | bytes 12296 | tf_op jit(solution)/shard_map/ppermute | solution.py:36
  26.2 3.6 %collective-permute-start.6 = (f32[8,128]{1,0:T(8,128)S(1)}, f32[8,128]{1,0:T(8,128)S(1)}, u32[]{:S(2)}, u32[]{:S(2)}) collective-permute-start(f32[8,128]{1,0:T(8,128)S(1)} %reshape.65), channel_id=1, source_target_pairs={{0,2},{1,3},{2,0},{3,1},{4,6},{5,7},{6,4},{7,5},{8,10},{9,11},{10,... | collective-permute-start | bytes 12296 | tf_op jit(solution)/shard_map/ppermute | solution.py:36
  26.3 5.1 %collective-permute-start.5 = (f32[8,128]{1,0:T(8,128)S(1)}, f32[8,128]{1,0:T(8,128)S(1)}, u32[]{:S(2)}, u32[]{:S(2)}) collective-permute-start(f32[8,128]{1,0:T(8,128)S(1)} %reshape.65), channel_id=1, source_target_pairs={{0,1},{1,0},{2,3},{3,2},{4,5},{5,4},{6,7},{7,6},{8,9},{9,8},{10,11... | collective-permute-start | bytes 12296 | tf_op jit(solution)/shard_map/ppermute | solution.py:36
  31.4 14.0 %collective-permute-start.10 = (f32[4,8,128]{2,1,0:T(8,128)S(1)}, f32[4,8,128]{2,1,0:T(8,128)S(1)}, u32[]{:S(2)}, u32[]{:S(2)}) collective-permute-start(f32[4,8,128]{2,1,0:T(8,128)S(1)} %pad_maximum_fusion.4), channel_id=1, source_target_pairs={{0,12},{1,13},{2,14},{3,15},{4,8},{5,9},{6,10},{7,11},{8,4},{9,5},... | collective-permute-start | bytes 49160 | tf_op jit(solution)/shard_map/ppermute | solution.py:36
  37.7 7.6 %collective-permute-start.9 = (f32[4,8,128]{2,1,0:T(8,128)S(1)}, f32[4,8,128]{2,1,0:T(8,128)S(1)}, u32[]{:S(2)}, u32[]{:S(2)}) collective-permute-start(f32[4,8,128]{2,1,0:T(8,128)S(1)} %pad_maximum_fusion.4), channel_id=1, source_target_pairs={{0,8},{1,9},{2,10},{3,11},{4,12},{5,13},{6,14},{7,15},{8,0},{9,1},... | collective-permute-start | bytes 49160 | tf_op jit(solution)/shard_map/ppermute | solution.py:36
  38.6 4.6 %collective-permute-start.8 = (f32[4,8,128]{2,1,0:T(8,128)S(1)}, f32[4,8,128]{2,1,0:T(8,128)S(1)}, u32[]{:S(2)}, u32[]{:S(2)}) collective-permute-start(f32[4,8,128]{2,1,0:T(8,128)S(1)} %pad_maximum_fusion.4), channel_id=1, source_target_pairs={{0,4},{1,5},{2,6},{3,7},{4,0},{5,1},{6,2},{7,3},{8,12},{9,13},{10,... | collective-permute-start | bytes 49160 | tf_op jit(solution)/shard_map/ppermute | solution.py:36
  45.4 1.0 copy-start.4
  46.4 1.0 copy-start.6
  73.4 2.0 %collective-permute-start.11 = (bf16[4,2,256,128]{3,2,1,0:T(8,128)(2,1)S(1)}, bf16[4,2,256,128]{3,2,1,0:T(8,128)(2,1)S(1)}, u32[]{:S(2)}, u32[]{:S(2)}) collective-permute-start(bf16[4,2,256,128]{3,2,1,0:T(8,128)(2,1)S(1)} %bitcast.98), channel_id=1, source_target_pairs={{0,16},{16,0},{32,48},{48,32},{64,80},{80,64},{96,112},{112,96},{1... | collective-permute-start | bytes 1572872 | tf_op jit(solution)/shard_map/ppermute | solution.py:36
  75.6 29.6 %copy-start.2 = (bf16[1024,128]{1,0:T(8,128)(2,1)S(1)}, bf16[1024,128]{1,0:T(8,128)(2,1)}, u32[]{:S(2)}) copy-start(bf16[1024,128]{1,0:T(8,128)(2,1)} %w_ref.3) | copy-start | bytes 786436
  75.6 8.4 %collective-permute-start.12 = (bf16[2,256,128]{2,1,0:T(8,128)(2,1)S(1)}, bf16[2,256,128]{2,1,0:T(8,128)(2,1)S(1)}, u32[]{:S(2)}, u32[]{:S(2)}) collective-permute-start(bf16[2,256,128]{2,1,0:T(8,128)(2,1)S(1)} %get-tuple-element.18), channel_id=1, source_target_pairs={{0,192},{16,208},{32,224},{48,240},{64,0},{80,16},{96,32},{112,48}... | collective-permute-start | bytes 393224 | tf_op jit(solution)/shard_map/ppermute | solution.py:40
  76.2 7.9 %collective-permute-start.14 = (bf16[2,256,128]{2,1,0:T(8,128)(2,1)S(1)}, bf16[2,256,128]{2,1,0:T(8,128)(2,1)S(1)}, u32[]{:S(2)}, u32[]{:S(2)}) collective-permute-start(bf16[2,256,128]{2,1,0:T(8,128)(2,1)S(1)} %get-tuple-element.19), channel_id=1, source_target_pairs={{0,128},{16,144},{32,160},{48,176},{64,192},{80,208},{96,224},{112... | collective-permute-start | bytes 393224 | tf_op jit(solution)/shard_map/ppermute | solution.py:40
  76.7 9.2 %collective-permute-start.13 = (bf16[2,256,128]{2,1,0:T(8,128)(2,1)S(1)}, bf16[2,256,128]{2,1,0:T(8,128)(2,1)S(1)}, u32[]{:S(2)}, u32[]{:S(2)}) collective-permute-start(bf16[2,256,128]{2,1,0:T(8,128)(2,1)S(1)} %get-tuple-element.20), channel_id=1, source_target_pairs={{0,64},{16,80},{32,96},{48,112},{64,128},{80,144},{96,160},{112,17... | collective-permute-start | bytes 393224 | tf_op jit(solution)/shard_map/ppermute | solution.py:40
  86.0 4.5 %collective-permute-start.15 = (bf16[256,128]{1,0:T(8,128)(2,1)S(1)}, bf16[256,128]{1,0:T(8,128)(2,1)S(1)}, u32[]{:S(2)}, u32[]{:S(2)}) collective-permute-start(bf16[256,128]{1,0:T(8,128)(2,1)S(1)} %fusion.6), channel_id=1, source_target_pairs={{0,32},{16,48},{32,0},{48,16},{64,96},{80,112},{96,64},{112,80},{1... | collective-permute-start | bytes 196616 | tf_op jit(solution)/shard_map/ppermute | solution.py:36
  90.8 5.3 %collective-permute-start.16 = (bf16[4,16,128]{2,1,0:T(8,128)(2,1)S(1)}, bf16[4,16,128]{2,1,0:T(8,128)(2,1)S(1)}, u32[]{:S(2)}, u32[]{:S(2)}) collective-permute-start(bf16[4,16,128]{2,1,0:T(8,128)(2,1)S(1)} %get-tuple-element.25), channel_id=1, source_target_pairs={{0,1},{1,0},{2,3},{3,2},{4,5},{5,4},{6,7},{7,6},{8,9},{9,8},{10,11... | collective-permute-start | bytes 49160 | tf_op jit(solution)/shard_map/ppermute | solution.py:36
  91.4 4.7 %collective-permute-start.17 = (bf16[4,16,128]{2,1,0:T(8,128)(2,1)S(1)}, bf16[4,16,128]{2,1,0:T(8,128)(2,1)S(1)}, u32[]{:S(2)}, u32[]{:S(2)}) collective-permute-start(bf16[4,16,128]{2,1,0:T(8,128)(2,1)S(1)} %get-tuple-element.26), channel_id=1, source_target_pairs={{0,2},{1,3},{2,0},{3,1},{4,6},{5,7},{6,4},{7,5},{8,10},{9,11},{10,... | collective-permute-start | bytes 49160 | tf_op jit(solution)/shard_map/ppermute | solution.py:36
  92.4 6.1 %collective-permute-start.18 = (bf16[4,16,128]{2,1,0:T(8,128)(2,1)S(1)}, bf16[4,16,128]{2,1,0:T(8,128)(2,1)S(1)}, u32[]{:S(2)}, u32[]{:S(2)}) collective-permute-start(bf16[4,16,128]{2,1,0:T(8,128)(2,1)S(1)} %get-tuple-element.27), channel_id=1, source_target_pairs={{0,3},{1,2},{2,1},{3,0},{4,7},{5,6},{6,5},{7,4},{8,11},{9,10},{10,... | collective-permute-start | bytes 49160 | tf_op jit(solution)/shard_map/ppermute | solution.py:36
  98.6 10.6 %collective-permute-start.19 = (bf16[16,128]{1,0:T(8,128)(2,1)S(1)}, bf16[16,128]{1,0:T(8,128)(2,1)S(1)}, u32[]{:S(2)}, u32[]{:S(2)}) collective-permute-start(bf16[16,128]{1,0:T(8,128)(2,1)S(1)} %get-tuple-element.30), channel_id=1, source_target_pairs={{0,4},{1,5},{2,6},{3,7},{4,0},{5,1},{6,2},{7,3},{8,12},{9,13},{10,... | collective-permute-start | bytes 12296 | tf_op jit(solution)/shard_map/ppermute | solution.py:36
  100.3 8.9 %collective-permute-start.21 = (bf16[16,128]{1,0:T(8,128)(2,1)S(1)}, bf16[16,128]{1,0:T(8,128)(2,1)S(1)}, u32[]{:S(2)}, u32[]{:S(2)}) collective-permute-start(bf16[16,128]{1,0:T(8,128)(2,1)S(1)} %get-tuple-element.31), channel_id=1, source_target_pairs={{0,12},{1,13},{2,14},{3,15},{4,8},{5,9},{6,10},{7,11},{8,4},{9,5},... | collective-permute-start | bytes 12296 | tf_op jit(solution)/shard_map/ppermute | solution.py:36
  102.2 7.5 %collective-permute-start.20 = (bf16[16,128]{1,0:T(8,128)(2,1)S(1)}, bf16[16,128]{1,0:T(8,128)(2,1)S(1)}, u32[]{:S(2)}, u32[]{:S(2)}) collective-permute-start(bf16[16,128]{1,0:T(8,128)(2,1)S(1)} %get-tuple-element.32), channel_id=1, source_target_pairs={{0,8},{1,9},{2,10},{3,11},{4,12},{5,13},{6,14},{7,15},{8,0},{9,1},... | collective-permute-start | bytes 12296 | tf_op jit(solution)/shard_map/ppermute | solution.py:36

commit v2 on v1

v2 whole, which is shorter than its diff:
```python
import functools
import math

import jax
import jax.numpy as jnp
from jax import lax
from jax.experimental import pallas as pl
from jax.experimental.pallas import tpu as pltpu
from jax.sharding import PartitionSpec as P

DIM = 128
H = 1024
QT = 32
LEN = 128
PD = 8
DEPTH = 100
CAP = 16
ROWS = CAP * LEN
GROUPS = 16
GR = 256
GQ = GR // QT

tau = 0.05
inv_temp = 20.0
rrf_offset = 60.0
norm_eps = 1e-06
log2_scale = inv_temp / math.log(2.0)

bf16 = jnp.bfloat16
f32 = jnp.float32
NT = (((1,), (1,)), ((), ()))
NN = (((1,), (0,)), ((), ()))
HIGH = lax.Precision.HIGHEST


def swap(value, axis, mask):
    return lax.ppermute(value, axis, [(i, i ^ mask) for i in range(16)])


def shift_x(value, by):
    return lax.ppermute(
        value, "pb", [(i, ((((i >> 2) + by) % 4) << 2) | (i & 3)) for i in range(16)]
    )


SHIFTS = (0, 1, -1, 2)


def reduce_pa(value, me):
    ids = jnp.arange(16, dtype=jnp.int32)
    order = (ids[None, :] == (ids[:, None] ^ me)).astype(bf16)
    blocks = lax.dot_general(
        order, value.astype(bf16).reshape(16, 16 * DIM), NN, preferred_element_type=f32
    ).astype(bf16)
    blocks = blocks.reshape(4, 4, 16, DIM)
    total = blocks[:, 0].astype(f32)
    for j in (1, 2, 3):
        total = total + swap(blocks[:, j], "pa", j).astype(f32)
    blocks = total.astype(bf16)
    total = total[0]
    for j in (1, 2, 3):
        total = total + swap(blocks[j], "pa", 4 * j).astype(f32)
    return total


def project_kernel(hid_ref, w_ref, proj_ref, emb_ref, emb_t_ref):
    proj = lax.dot_general(hid_ref[...], w_ref[...], NN, preferred_element_type=f32)
    scaling = lax.rsqrt(jnp.sum(proj * proj, axis=-1, keepdims=True) + norm_eps)
    unit = proj * scaling
    proj_ref[...] = proj
    emb_ref[...] = unit.astype(bf16)
    emb_t_ref[...] = unit.T.astype(bf16)


def project(hid, weight):
    step = 512
    return pl.pallas_call(
        project_kernel,
        grid=(ROWS // step,),
        in_specs=[
            pl.BlockSpec((step, H), lambda i: (i, 0)),
            pl.BlockSpec((H, DIM), lambda i: (0, 0)),
        ],
        out_specs=[
            pl.BlockSpec((step, DIM), lambda i: (i, 0)),
            pl.BlockSpec((step, DIM), lambda i: (i, 0)),
            pl.BlockSpec((DIM, step), lambda i: (0, i)),
        ],
        out_shape=[
            jax.ShapeDtypeStruct((ROWS, DIM), f32),
            jax.ShapeDtypeStruct((ROWS, DIM), bf16),
            jax.ShapeDtypeStruct((DIM, ROWS), bf16),
        ],
        compiler_params=pltpu.CompilerParams(vmem_limit_bytes=6 * 2**20),
        cost_estimate=pl.CostEstimate(
            flops=2 * ROWS * H * DIM, bytes_accessed=ROWS * (2 * H + 8 * DIM), transcendentals=0
        ),
        name="project",
    )(hid, weight)


def token_sums(value):
    high = value.astype(bf16)
    rest = value - high.astype(f32)
    middle = rest.astype(bf16)
    low = (rest - middle.astype(f32)).astype(bf16)
    row_q = lax.broadcasted_iota(jnp.int32, (GR, GR), 0) // QT
    col_q = lax.broadcasted_iota(jnp.int32, (GR, GR), 1) // QT
    same = (row_q == col_q).astype(f32).astype(bf16)
    parts = [lax.dot_general(v, same, NN, preferred_element_type=f32) for v in (high, middle, low)]
    return parts[0] + (parts[1] + parts[2])


def forward_kernel(q_ref, emb_ref, p_ref, lse_ref, total_ref):
    queries = q_ref[0, :GR, :]
    tops, sums = [], []
    for k in range(CAP):
        rows = slice(k * LEN, (k + 1) * LEN)
        raw = lax.dot_general(emb_ref[rows, :], queries, NT, preferred_element_type=f32)
        top = jnp.max(raw, axis=0, keepdims=True)
        p = jnp.exp2((raw - top) * log2_scale)
        p_ref[0, rows, :] = p.astype(bf16)
        tops.append(top)
        sums.append(jnp.sum(p, axis=0, keepdims=True))
    top = jnp.concatenate(tops, axis=0)
    total = jnp.concatenate(sums, axis=0)
    lse_ref[0] = inv_temp * top + jnp.log(total)
    total_ref[0] = total


def forward(gathered, start, count, emb):
    height = gathered.shape[1]
    return pl.pallas_call(
        forward_kernel,
        grid=(count,),
        in_specs=[
            pl.BlockSpec((1, height, DIM), lambda g: (g + start, 0, 0)),
            pl.BlockSpec((ROWS, DIM), lambda g: (0, 0)),
        ],
        out_specs=[
            pl.BlockSpec((1, ROWS, GR), lambda g: (g, 0, 0)),
            pl.BlockSpec((1, CAP, GR), lambda g: (g, 0, 0)),
            pl.BlockSpec((1, CAP, GR), lambda g: (g, 0, 0)),
        ],
        out_shape=[
            jax.ShapeDtypeStruct((count, ROWS, GR), bf16),
            jax.ShapeDtypeStruct((count, CAP, GR), f32),
            jax.ShapeDtypeStruct((count, CAP, GR), f32),
        ],
        compiler_params=pltpu.CompilerParams(vmem_limit_bytes=6 * 2**20),
        cost_estimate=pl.CostEstimate(
            flops=2 * count * GR * ROWS * DIM,
            bytes_accessed=count * 2 * GR * ROWS,
            transcendentals=count * GR * ROWS,
        ),
        name="forward",
    )(gathered, emb)


def backward_kernel(
    first, half, q_at, q_ref, p_ref, lse_ref, total_ref, emb_t_ref, pick_ref, *rest
):
    target_refs = rest[:4]
    qg_ref, eg_ref, c_ref, own_ref, score_ref = rest[-5:]
    g = pl.program_id(0)
    pick = pick_ref[...]

    @pl.when(g == 0)
    def _():
        eg_ref[...] = jnp.zeros_like(eg_ref) if first else rest[4][...]
        own = jnp.zeros((CAP, LEN), f32)
        for j in range(4):
            part = target_refs[j][:, :, half * LEN : (half + 1) * LEN].reshape(QT, LEN)
            own += lax.dot_general(
                pick[:, j * QT : (j + 1) * QT], part, NN, precision=HIGH, preferred_element_type=f32
            )
        own_ref[...] = own
        score = token_sums(lse_ref[...].reshape(-1, GR)) * (tau / QT)
        score_ref[...] = score.reshape(score_ref.shape)

    queries = q_ref[0, :GR, :]
    held = jnp.sum(pick, axis=1, keepdims=True)
    own = own_ref[...]
    lane = lax.broadcasted_iota(jnp.int32, (CAP, LEN), 1) // QT
    factors = []
    for k in range(2):
        lanes = slice(k * LEN, (k + 1) * LEN)
        at = lane + ((g + q_at) * 2 * GQ + k * (GQ // 2))
        target = jnp.take_along_axis(own, at, axis=1, mode="promise_in_bounds")
        residual = (score_ref[g, :, lanes] - target).astype(bf16).astype(f32) * held
        factors.append((residual / QT) / total_ref[0, :, lanes])
    factor = jnp.concatenate(factors, axis=1)
    for k in range(CAP):
        rows = slice(k * LEN, (k + 1) * LEN)
        c_ref[rows, :] = (p_ref[0, rows, :].astype(f32) * factor[k : k + 1, :]).astype(bf16)
    eg_ref[...] += lax.dot_general(c_ref[...], queries, NN, preferred_element_type=f32)
    qg = lax.dot_general(emb_t_ref[...], c_ref[...], NN, preferred_element_type=f32)
    qg_ref[0] = qg.T.astype(bf16)


def backward(gathered, start, half, kept, emb_t, pick, targets, emb_grad=None):
    height = gathered.shape[1]
    p, lse, total = kept
    count = p.shape[0]
    first = emb_grad is None
    whole = lambda g: (0, 0)
    step = lambda g: (g, 0, 0)
    in_specs = [
        pl.BlockSpec((1, height, DIM), lambda g: (g + start, 0, 0)),
        pl.BlockSpec((1, ROWS, GR), step),
        pl.BlockSpec((count, CAP, GR), lambda g: (0, 0, 0)),
        pl.BlockSpec((1, CAP, GR), step),
        pl.BlockSpec((DIM, ROWS), whole),
        pl.BlockSpec((CAP, LEN), whole),
    ] + [pl.BlockSpec((4, PD, 2 * LEN), lambda g: (0, 0, 0))] * 4
    args = [gathered, p, lse, total, emb_t, pick, *targets]
    if not first:
        in_specs.append(pl.BlockSpec((ROWS, DIM), whole))
        args.append(emb_grad)
    return pl.pallas_call(
        functools.partial(backward_kernel, first, half, start),
        grid=(count,),
        in_specs=in_specs,
        out_specs=[pl.BlockSpec((1, GR, DIM), step), pl.BlockSpec((ROWS, DIM), whole)],
        out_shape=[
            jax.ShapeDtypeStruct((count, GR, DIM), bf16),
            jax.ShapeDtypeStruct((ROWS, DIM), f32),
        ],
        scratch_shapes=[pltpu.VMEM((ROWS, GR), bf16), pltpu.VMEM((CAP, LEN), f32), pltpu.VMEM((count, CAP, GR), f32)],
        compiler_params=pltpu.CompilerParams(vmem_limit_bytes=11 * 2**20),
        cost_estimate=pl.CostEstimate(
            flops=4 * count * GR * ROWS * DIM,
            bytes_accessed=count * 2 * GR * ROWS,
            transcendentals=0,
        ),
        name="backward",
    )(*args)


def hidden_kernel(eg_ref, proj_ref, w_ref, out_ref):
    proj = proj_ref[...]
    scaling = lax.rsqrt(jnp.sum(proj * proj, axis=-1, keepdims=True) + norm_eps)
    unit = proj * scaling
    slot_grad = eg_ref[...].astype(bf16).astype(f32)
    inner = jnp.sum(unit * slot_grad, axis=-1, keepdims=True)
    proj_grad = ((slot_grad - unit * inner) * scaling).astype(bf16)
    out_ref[...] = lax.dot_general(
        proj_grad, w_ref[...], NT, preferred_element_type=f32
    ).astype(bf16)


def hidden_gradient(emb_grad, proj, weight):
    step = 512
    return pl.pallas_call(
        hidden_kernel,
        grid=(ROWS // step,),
        in_specs=[
            pl.BlockSpec((step, DIM), lambda i: (i, 0)),
            pl.BlockSpec((step, DIM), lambda i: (i, 0)),
            pl.BlockSpec((H, DIM), lambda i: (0, 0)),
        ],
        out_specs=pl.BlockSpec((step, H), lambda i: (i, 0)),
        out_shape=jax.ShapeDtypeStruct((ROWS, H), bf16),
        compiler_params=pltpu.CompilerParams(vmem_limit_bytes=8 * 2**20),
        cost_estimate=pl.CostEstimate(
            flops=2 * ROWS * H * DIM, bytes_accessed=ROWS * (2 * H + 8 * DIM), transcendentals=0
        ),
        name="hidden_gradient",
    )(emb_grad, proj, weight)


def target_kernel(me_ref, near_ref, far_ref, out_ref):
    row = lax.broadcasted_iota(jnp.int32, (2 * PD, LEN), 0) + me_ref[0] * PD
    own = (row == lax.broadcasted_iota(jnp.int32, (2 * PD, LEN), 1)).astype(f32).astype(bf16)
    for half, ref in enumerate((near_ref, far_ref)):
        ranks = ref[...].reshape(LEN, LEN)
        rank = lax.dot_general(own, ranks, NT, preferred_element_type=f32)[:PD]
        term = rank_term(rank)
        out_ref[:, half * LEN : (half + 1) * LEN] = term + pltpu.roll(term, LEN - GQ, 1)


def targets_of(me_pb, near, far):
    rows = pl.BlockSpec((8, 2 * GQ, DIM), lambda i: (0, GR // (2 * GQ), 0))
    return pl.pallas_call(
        target_kernel,
        grid=(1,),
        in_specs=[pl.BlockSpec(memory_space=pltpu.SMEM), rows, rows],
        out_specs=pl.BlockSpec((PD, 2 * LEN), lambda i: (0, 0)),
        out_shape=jax.ShapeDtypeStruct((PD, 2 * LEN), f32),
        compiler_params=pltpu.CompilerParams(vmem_limit_bytes=2 * 2**20),
        name="targets",
    )(me_pb.reshape(1), near, far)


def rank_term(rank):
    return jnp.where(rank < DEPTH, rrf_offset / (rrf_offset + rank), 0.0)


def on_device(
    queries, encoder_outputs, proj_weight, bm25_rank, dense_rank, custodian_document_index
):
    me_pb, me_pa = lax.axis_index("pb"), lax.axis_index("pa")
    ids = jnp.arange(LEN, dtype=jnp.int32)
    slot_ids = custodian_document_index[0]
    place = jnp.where(slot_ids >= 0, slot_ids ^ (me_pa * PD), -1)
    pick = (place[:, None] == ids[None, :]).astype(f32)
    ranks = jnp.concatenate([bm25_rank[:, 0, :], dense_rank[:, 0, :]]).astype(bf16)
    mine = jnp.concatenate([queries, ranks])
    other = swap(mine, "pb", 2)
    proj, emb, emb_t = project(encoder_outputs.reshape(ROWS, H), proj_weight)
    pair = jnp.stack([mine, other])
    got = [shift_x(pair, by) for by in SHIFTS[1:]]
    kept_d = forward(pair, 0, 2, emb)
    got, kept_d = lax.optimization_barrier((got, kept_d))
    plane = jnp.concatenate([pair] + got)
    far = swap(plane, "pb", 1)
    kept_b = forward(plane, 2, 6, emb)
    far, kept_b = lax.optimization_barrier((far, kept_b))
    target = targets_of(me_pb, plane, far)
    low = [swap(target, "pa", j) for j in (1, 2, 3)]
    kept_a = forward(far, 2, 6, emb)
    low, kept_a = lax.optimization_barrier((low, kept_a))
    low = jnp.stack([target] + low)
    high = [swap(low, "pa", 4 * j) for j in (1, 2, 3)]
    kept_c = forward(far, 0, 2, emb)
    high, kept_c = lax.optimization_barrier((high, kept_c))
    own_args = (emb_t, pick, [low] + high)
    qg_a, eg = backward(far, 2, 1, kept_a, *own_args)
    from_core = swap(qg_a, "pb", 1)
    qg_b, eg = backward(plane, 2, 0, kept_b, *own_args, eg)
    sent = (qg_b.astype(f32) + from_core.astype(f32)).astype(bf16).reshape(3, 2, GR, DIM)
    from_x = [shift_x(sent[a - 1], -SHIFTS[a]) for a in (1, 2, 3)]
    qg_c, eg = backward(far, 0, 1, kept_c, *own_args, eg)
    from_core = swap(qg_c, "pb", 1)
    qg_d, eg = backward(pair, 0, 0, kept_d, *own_args, eg)
    hidden = hidden_gradient(eg, proj, proj_weight)
    from_x, hidden = lax.optimization_barrier((from_x, hidden))
    both = qg_d.astype(f32) + from_core.astype(f32)
    for one in from_x:
        both = both + one.astype(f32)
    from_y = swap(both[1].astype(bf16), "pb", 2)
    query_grad = reduce_pa(both[0] + from_y.astype(f32), me_pa)
    return (query_grad, hidden.reshape(1, CAP, LEN, H))


def solution(mesh):
    return jax.shard_map(
        on_device,
        mesh=mesh,
        in_specs=(
            P("pb", None),
            P("pb", "pa", None, None),
            P(),
            P("pb", "pa", None),
            P("pb", "pa", None),
            P("pb", "pa"),
        ),
        out_specs=(P(("pb", "pa"), None), P("pb", "pa", None, None)),
        check_vma=False,
    )
```

time: 111 us -> 98.4 us (0.89)
  waiting for transfers between devices: 29.3 us -> 20.3 us
  local copies, waits for them, and re-layouts: 6.41 us -> 4.63 us
  Pallas kernels: 32.3 us -> 31 us
    ppermute x16 -> x17, waiting for transfers between devices: 22.7 us -> 17.6 us  [swap(): return lax.ppermute(value, axis, [(i, i ^ mask) for i in range(16)])]
    ppermute x6, waiting for transfers between devices: 6.66 us -> 2.73 us  [shift_x(): lax.ppermute(value, 'pb', [(i, ((i >> 2) + by) % 4 << 2 | i & 3) for i in...]
    another operation x7 -> x3, other arithmetic: 2.47 us -> 0.88 us  [the longest x2 0.87 us: on_device(): pair = jnp.stack([mine, other])]
    unnamed x26 -> x16, local copies, waits for them, and re-layouts: 5.9 us -> 4.53 us
    pallas_call x1 -> x9, Pallas kernels: 25.9 us -> 24.6 us  [the longest x4 12.9 us: backward(): pl.pallas_call(functools.partial(backward_kernel, first, half, start), gr...]
    ppermute x16 -> x17, starting transfers between devices: 28.4 us -> 28 us  [swap(): return lax.ppermute(value, axis, [(i, i ^ mask) for i in range(16)])]
  transfers between devices with their start and end apart: 22 -> 23, of which waited for: 14 -> 10; matrix products, arithmetic and copies ran while one was open for 0% -> 1% of each run, Pallas kernels for 6% -> 27%
where the time goes in v2:
time: 98.4 us; the launch traced here: 97 us
  starting transfers between devices  36.5 us (37%)
  Pallas kernels  31 us (32%)
  waiting for transfers between devices  20.3 us (21%)
  local copies, waits for them, and re-layouts  4.63 us (5%)
  other arithmetic  3.34 us (3%)
    ppermute x17, starting transfers between devices, swap(): return lax.ppermute(value, axis, [(i, i ^ mask) for i in range(16)])  28 us
    ppermute x17, waiting for transfers between devices, swap(): return lax.ppermute(value, axis, [(i, i ^ mask) for i in range(16)])  17.6 us
    pallas_call x4, Pallas kernels, backward(): pl.pallas_call(functools.partial(backward_kernel, first, half, start), gr...  12.9 us
    pallas_call x4, Pallas kernels, forward(): pl.pallas_call(forward_kernel, grid=(count,), in_specs=[pl.BlockSpec((1,...  11.5 us
    ppermute x6, starting transfers between devices, shift_x(): lax.ppermute(value, 'pb', [(i, ((i >> 2) + by) % 4 << 2 | i & 3) for i in...  8.45 us
    unnamed x16, local copies, waits for them, and re-layouts  4.53 us
    pallas_call x1, Pallas kernels, hidden_gradient(): pl.pallas_call(hidden_kernel, grid=(ROWS // step,), in_specs=[pl.BlockSpe...  4 us
    ppermute x6, waiting for transfers between devices, shift_x(): lax.ppermute(value, 'pb', [(i, ((i >> 2) + by) % 4 << 2 | i & 3) for i in...  2.73 us
  transfers between devices with their start and end apart: 23, of which 10 were waited for; matrix products, arithmetic and copies ran while one was open for 1% of the time, Pallas kernels for 27%

profile of v2, /device:TPU:2, one launch (start us, length us, event | category | flops | bytes accessed | tf_op | source)
XLA Modules:
  0.0 97.0 jit_solution(10192842296432363810)
XLA Ops:
  0.6 0.7 convert_bitcast_fusion
  1.4 0.9 fusion.12
  2.2 1.7 %collective-permute-start = (bf16[272,128]{1,0:T(8,128)(2,1)S(1)}, bf16[272,128]{1,0:T(8,128)(2,1)S(1)}, u32[]{:S(2)}, u32[]{:S(2)}) collective-permute-start(bf16[272,128]{1,0:T(8,128)(2,1)S(1)} %get-tuple-element.106), channel_id=1, source_target_pairs={{0,32},{16,48},{32,0},{48,16},{64,96},{80,112},{96,64},{112,80},{1... | collective-permute-start | bytes 208904 | tf_op jit(solution)/shard_map/ppermute | solution.py:37
  3.9 0.8 constant_dynamic-update-slice_fusion.4
  4.7 2.2 %copy-done = bf16[1,16,128,1024]{3,2,1,0:T(8,128)(2,1)S(1)} copy-done((bf16[1,16,128,1024]{3,2,1,0:T(8,128)(2,1)S(1)}, bf16[1,16,128,1024]{3,2,1,0:T(8,128)(2,1)}, u32[]{:S(2)}) %copy-start) | copy-done | bytes 4194328
  6.9 0.9 copy-done.3
  7.9 2.4 %project.1 = (f32[2048,128]{1,0:T(8,128)S(1)}, bf16[2048,128]{1,0:T(8,128)(2,1)S(1)}, bf16[128,2048]{1,0:T(8,128)(2,1)S(1)}) custom-call(bf16[2048,1024]{1,0:T(8,128)(2,1)S(1)} %bitcast.67, bf16[1024,128]{1,0:T(8,128)(2,1)S(1)} %copy-done.3), custom_call_target="tpu_custom_call" | custom-call | flops 536870912 | bytes 6291456 | tf_op jit(solution)/shard_map/project/pallas_call | solution.py:77
  10.3 2.2 %collective-permute-start.3 = (bf16[2,272,128]{2,1,0:T(8,128)(2,1)S(1)}, bf16[2,272,128]{2,1,0:T(8,128)(2,1)S(1)}, u32[]{:S(2)}, u32[]{:S(2)}) collective-permute-start(bf16[2,272,128]{2,1,0:T(8,128)(2,1)S(1)} %pad_maximum_fusion.q_ref), channel_id=1, source_target_pairs={{0,128},{16,144},{32,160},{48,176},{64,192},{80,208},{96,224},{112... | collective-permute-start | bytes 417800 | tf_op jit(solution)/shard_map/ppermute | solution.py:41
  12.6 1.4 %collective-permute-start.2 = (bf16[2,272,128]{2,1,0:T(8,128)(2,1)S(1)}, bf16[2,272,128]{2,1,0:T(8,128)(2,1)S(1)}, u32[]{:S(2)}, u32[]{:S(2)}) collective-permute-start(bf16[2,272,128]{2,1,0:T(8,128)(2,1)S(1)} %pad_maximum_fusion.q_ref), channel_id=1, source_target_pairs={{0,192},{16,208},{32,224},{48,240},{64,0},{80,16},{96,32},{112,48}... | collective-permute-start | bytes 417800 | tf_op jit(solution)/shard_map/ppermute | solution.py:41
  14.0 0.6 collective-permute-start.1
  14.6 1.4 %forward.4 = (bf16[2,2048,256]{2,1,0:T(8,128)(2,1)S(1)}, f32[2,16,256]{2,1,0:T(8,128)S(1)}, f32[2,16,256]{2,1,0:T(8,128)S(1)}) custom-call(bf16[2,272,128]{2,1,0:T(8,128)(2,1)S(1)} %pad_maximum_fusion.q_ref, bf16[2048,128]{1,0:T(8,128)(2,1)S(1)} %get-tuple-element.51.emb_ref), custom_call_target="tpu_custom_call" | custom-call | flops 268435456 | bytes 2097152 | tf_op jit(solution)/shard_map/forward/pallas_call | solution.py:133
  16.0 1.3 %copy-done.1 = bf16[2,2048,256]{2,1,0:T(8,128)(2,1)} copy-done((bf16[2,2048,256]{2,1,0:T(8,128)(2,1)}, bf16[2,2048,256]{2,1,0:T(8,128)(2,1)S(1)}, u32[]{:S(2)}) %copy-start.1) | copy-done | bytes 2097176
  17.4 1.2 %collective-permute-done.3 = bf16[2,272,128]{2,1,0:T(8,128)(2,1)S(1)} collective-permute-done((bf16[2,272,128]{2,1,0:T(8,128)(2,1)S(1)}, bf16[2,272,128]{2,1,0:T(8,128)(2,1)S(1)}, u32[]{:S(2)}, u32[]{:S(2)}) %collective-permute-start.3) | collective-permute-done | bytes 139296 | tf_op jit(solution)/shard_map/ppermute | solution.py:41
  18.5 1.5 %collective-permute-done.2 = bf16[2,272,128]{2,1,0:T(8,128)(2,1)S(1)} collective-permute-done((bf16[2,272,128]{2,1,0:T(8,128)(2,1)S(1)}, bf16[2,272,128]{2,1,0:T(8,128)(2,1)S(1)}, u32[]{:S(2)}, u32[]{:S(2)}) %collective-permute-start.2) | collective-permute-done | bytes 139296 | tf_op jit(solution)/shard_map/ppermute | solution.py:41
  20.3 4.3 %forward.5 = (bf16[6,2048,256]{2,1,0:T(8,128)(2,1)S(1)}, f32[6,16,256]{2,1,0:T(8,128)S(1)}, f32[6,16,256]{2,1,0:T(8,128)S(1)}) custom-call(bf16[8,272,128]{2,1,0:T(8,128)(2,1)S(1)} %constant_dynamic-update-slice_fusion.q_ref.near_ref, bf16[2048,128]{1,0:T(8,128)(2,1)S(1)} %get-tuple-element.51.emb_ref), custom_call_target="tpu_custom_call" | custom-call | flops 805306368 | bytes 6291456 | tf_op jit(solution)/shard_map/forward/pallas_call | solution.py:133
  24.6 0.2 targets.1
  24.8 4.3 %collective-permute-start.7 = (f32[8,256]{1,0:T(8,128)S(1)}, f32[8,256]{1,0:T(8,128)S(1)}, u32[]{:S(2)}, u32[]{:S(2)}) collective-permute-start(f32[8,256]{1,0:T(8,128)S(1)} %targets.1), channel_id=1, source_target_pairs={{0,3},{1,2},{2,1},{3,0},{4,7},{5,6},{6,5},{7,4},{8,11},{9,10},{10,... | collective-permute-start | bytes 24584 | tf_op jit(solution)/shard_map/ppermute | solution.py:37
  29.2 0.6 collective-permute-start.5
  29.9 4.3 %forward.6 = (bf16[6,2048,256]{2,1,0:T(8,128)(2,1)S(1)}, f32[6,16,256]{2,1,0:T(8,128)S(1)}, f32[6,16,256]{2,1,0:T(8,128)S(1)}) custom-call(bf16[8,272,128]{2,1,0:T(8,128)(2,1)S(1)} %collective-permute-done.4.far_ref.q_ref, bf16[2048,128]{1,0:T(8,128)(2,1)S(1)} %get-tuple-element.51.emb_ref), custom_call_target="tpu_custom_call" | custom-call | flops 805306368 | bytes 6291456 | tf_op jit(solution)/shard_map/forward/pallas_call | solution.py:133
  34.4 6.3 %collective-permute-start.10 = (f32[4,8,256]{2,1,0:T(8,128)S(1)}, f32[4,8,256]{2,1,0:T(8,128)S(1)}, u32[]{:S(2)}, u32[]{:S(2)}) collective-permute-start(f32[4,8,256]{2,1,0:T(8,128)S(1)} %pad_maximum_fusion.2.rest_0_), channel_id=1, source_target_pairs={{0,12},{1,13},{2,14},{3,15},{4,8},{5,9},{6,10},{7,11},{8,4},{9,5},... | collective-permute-start | bytes 98312 | tf_op jit(solution)/shard_map/ppermute | solution.py:37
  40.7 1.0 collective-permute-start.9
  41.7 1.5 %collective-permute-start.8 = (f32[4,8,256]{2,1,0:T(8,128)S(1)}, f32[4,8,256]{2,1,0:T(8,128)S(1)}, u32[]{:S(2)}, u32[]{:S(2)}) collective-permute-start(f32[4,8,256]{2,1,0:T(8,128)S(1)} %pad_maximum_fusion.2.rest_0_), channel_id=1, source_target_pairs={{0,4},{1,5},{2,6},{3,7},{4,0},{5,1},{6,2},{7,3},{8,12},{9,13},{10,... | collective-permute-start | bytes 98312 | tf_op jit(solution)/shard_map/ppermute | solution.py:37
  43.2 1.4 %forward.7 = (bf16[2,2048,256]{2,1,0:T(8,128)(2,1)S(1)}, f32[2,16,256]{2,1,0:T(8,128)S(1)}, f32[2,16,256]{2,1,0:T(8,128)S(1)}) custom-call(bf16[8,272,128]{2,1,0:T(8,128)(2,1)S(1)} %collective-permute-done.4.far_ref.q_ref, bf16[2048,128]{1,0:T(8,128)(2,1)S(1)} %get-tuple-element.51.emb_ref), custom_call_target="tpu_custom_call" | custom-call | flops 268435456 | bytes 2097152 | tf_op jit(solution)/shard_map/forward/pallas_call | solution.py:133
  44.7 4.1 %collective-permute-done.9.rest_2_ = f32[4,8,256]{2,1,0:T(8,128)S(1)} collective-permute-done((f32[4,8,256]{2,1,0:T(8,128)S(1)}, f32[4,8,256]{2,1,0:T(8,128)S(1)}, u32[]{:S(2)}, u32[]{:S(2)}) %collective-permute-start.9) | collective-permute-done | bytes 32800 | tf_op jit(solution)/shard_map/ppermute | solution.py:37
  48.7 4.7 %backward.4 = (bf16[6,256,128]{2,1,0:T(8,128)(2,1)S(1)}, f32[2048,128]{1,0:T(8,128)S(1)}) custom-call(bf16[8,272,128]{2,1,0:T(8,128)(2,1)S(1)} %collective-permute-done.4.far_ref.q_ref, bf16[6,2048,256]{2,1,0:T(8,128)(2,1)S(1)} %get-tuple-element.84.p_ref, f32[6,16,256]{2,1,0:T(8,128)S(1)} %get-tuple-element.85.lse_ref, ...), custom_call_target="tpu_custom_call" | custom-call | flops 1610612736 | bytes 6291456 | tf_op jit(solution)/shard_map/backward/pallas_call | solution.py:220
  53.4 0.3 collective-permute-start.12
  53.7 4.7 %backward.5 = (bf16[6,256,128]{2,1,0:T(8,128)(2,1)S(1)}, f32[2048,128]{1,0:T(8,128)S(1)}) custom-call(bf16[8,272,128]{2,1,0:T(8,128)(2,1)S(1)} %constant_dynamic-update-slice_fusion.q_ref.near_ref, bf16[6,2048,256]{2,1,0:T(8,128)(2,1)S(1)} %get-tuple-element.81.p_ref, f32[6,16,256]{2,1,0:T(8,128)S(1)} %get-tuple-element.82.lse_ref, ...), custom_call_target="tpu_custom_call" | custom-call | flops 1610612736 | bytes 6291456 | tf_op jit(solution)/shard_map/backward/pallas_call | solution.py:220
  58.5 2.2 %collective-permute-start.15 = (bf16[2,256,128]{2,1,0:T(8,128)(2,1)S(1)}, bf16[2,256,128]{2,1,0:T(8,128)(2,1)S(1)}, u32[]{:S(2)}, u32[]{:S(2)}) collective-permute-start(bf16[2,256,128]{2,1,0:T(8,128)(2,1)S(1)} %get-tuple-element.102), channel_id=1, source_target_pairs={{0,128},{16,144},{32,160},{48,176},{64,192},{80,208},{96,224},{112... | collective-permute-start | bytes 393224 | tf_op jit(solution)/shard_map/ppermute | solution.py:41
  60.7 0.7 collective-permute-start.14
  61.4 1.3 %collective-permute-start.13 = (bf16[2,256,128]{2,1,0:T(8,128)(2,1)S(1)}, bf16[2,256,128]{2,1,0:T(8,128)(2,1)S(1)}, u32[]{:S(2)}, u32[]{:S(2)}) collective-permute-start(bf16[2,256,128]{2,1,0:T(8,128)(2,1)S(1)} %get-tuple-element.104), channel_id=1, source_target_pairs={{0,192},{16,208},{32,224},{48,240},{64,0},{80,16},{96,32},{112,48}... | collective-permute-start | bytes 393224 | tf_op jit(solution)/shard_map/ppermute | solution.py:41
  62.7 1.8 %backward.6 = (bf16[2,256,128]{2,1,0:T(8,128)(2,1)S(1)}, f32[2048,128]{1,0:T(8,128)S(1)}) custom-call(bf16[8,272,128]{2,1,0:T(8,128)(2,1)S(1)} %collective-permute-done.4.far_ref.q_ref, bf16[2,2048,256]{2,1,0:T(8,128)(2,1)S(1)} %get-tuple-element.78.p_ref, f32[2,16,256]{2,1,0:T(8,128)S(1)} %get-tuple-element.79.lse_ref, ...), custom_call_target="tpu_custom_call" | custom-call | flops 536870912 | bytes 2097152 | tf_op jit(solution)/shard_map/backward/pallas_call | solution.py:220
  64.6 1.8 %backward.7 = (bf16[2,256,128]{2,1,0:T(8,128)(2,1)S(1)}, f32[2048,128]{1,0:T(8,128)S(1)}) custom-call(bf16[2,272,128]{2,1,0:T(8,128)(2,1)S(1)} %pad_maximum_fusion.q_ref, bf16[2,2048,256]{2,1,0:T(8,128)(2,1)S(1)} %copy-done.2, f32[2,16,256]{2,1,0:T(8,128)S(1)} %get-tuple-element.56.lse_ref, f32[2,16,256]{2,1,0:T(8,128)S(1)} %get-tuple-element.57.total_ref, ...), custom_call_target="tpu_custom_call" | custom-call | flops 536870912 | bytes 2097152 | tf_op jit(solution)/shard_map/backward/pallas_call | solution.py:220
  66.4 4.0 %hidden_gradient.1 = bf16[2048,1024]{1,0:T(8,128)(2,1)} custom-call(f32[2048,128]{1,0:T(8,128)S(1)} %get-tuple-element.94.eg_ref, f32[2048,128]{1,0:T(8,128)S(1)} %get-tuple-element.95.proj_ref, bf16[1024,128]{1,0:T(8,128)(2,1)S(1)} %copy-done.4), custom_call_target="tpu_custom_call" | custom-call | flops 536870912 | bytes 6291456 | tf_op jit(solution)/shard_map/hidden_gradient/pallas_call | solution.py:254
  70.5 0.5 collective-permute-start.16
  71.0 4.0 %collective-permute-done.16 = bf16[256,128]{1,0:T(8,128)(2,1)S(1)} collective-permute-done((bf16[256,128]{1,0:T(8,128)(2,1)S(1)}, bf16[256,128]{1,0:T(8,128)(2,1)S(1)}, u32[]{:S(2)}, u32[]{:S(2)}) %collective-permute-start.16) | collective-permute-done | bytes 65568 | tf_op jit(solution)/shard_map/ppermute | solution.py:37
  75.1 0.2 fusion
  75.4 2.9 %collective-permute-start.17 = (bf16[4,16,128]{2,1,0:T(8,128)(2,1)S(1)}, bf16[4,16,128]{2,1,0:T(8,128)(2,1)S(1)}, u32[]{:S(2)}, u32[]{:S(2)}) collective-permute-start(bf16[4,16,128]{2,1,0:T(8,128)(2,1)S(1)} %get-tuple-element.107), channel_id=1, source_target_pairs={{0,1},{1,0},{2,3},{3,2},{4,5},{5,4},{6,7},{7,6},{8,9},{9,8},{10,11... | collective-permute-start | bytes 49160 | tf_op jit(solution)/shard_map/ppermute | solution.py:37
  78.3 1.2 %collective-permute-start.18 = (bf16[4,16,128]{2,1,0:T(8,128)(2,1)S(1)}, bf16[4,16,128]{2,1,0:T(8,128)(2,1)S(1)}, u32[]{:S(2)}, u32[]{:S(2)}) collective-permute-start(bf16[4,16,128]{2,1,0:T(8,128)(2,1)S(1)} %get-tuple-element.108), channel_id=1, source_target_pairs={{0,2},{1,3},{2,0},{3,1},{4,6},{5,7},{6,4},{7,5},{8,10},{9,11},{10,... | collective-permute-start | bytes 49160 | tf_op jit(solution)/shard_map/ppermute | solution.py:37
  79.5 1.0 collective-permute-start.19
  80.5 0.2 collective-permute-done.17
  80.7 1.4 %collective-permute-done.18 = bf16[4,16,128]{2,1,0:T(8,128)(2,1)S(1)} collective-permute-done((bf16[4,16,128]{2,1,0:T(8,128)(2,1)S(1)}, bf16[4,16,128]{2,1,0:T(8,128)(2,1)S(1)}, u32[]{:S(2)}, u32[]{:S(2)}) %collective-permute-start.18) | collective-permute-done | bytes 16416 | tf_op jit(solution)/shard_map/ppermute | solution.py:37
  82.1 3.6 %collective-permute-done.19 = bf16[4,16,128]{2,1,0:T(8,128)(2,1)S(1)} collective-permute-done((bf16[4,16,128]{2,1,0:T(8,128)(2,1)S(1)}, bf16[4,16,128]{2,1,0:T(8,128)(2,1)S(1)}, u32[]{:S(2)}, u32[]{:S(2)}) %collective-permute-start.19) | collective-permute-done | bytes 16416 | tf_op jit(solution)/shard_map/ppermute | solution.py:37
  85.7 1.5 %collective-permute-start.20 = (bf16[16,128]{1,0:T(8,128)(2,1)S(1)}, bf16[16,128]{1,0:T(8,128)(2,1)S(1)}, u32[]{:S(2)}, u32[]{:S(2)}) collective-permute-start(bf16[16,128]{1,0:T(8,128)(2,1)S(1)} %get-tuple-element.110), channel_id=1, source_target_pairs={{0,4},{1,5},{2,6},{3,7},{4,0},{5,1},{6,2},{7,3},{8,12},{9,13},{10,... | collective-permute-start | bytes 12296 | tf_op jit(solution)/shard_map/ppermute | solution.py:37
  87.2 1.7 %collective-permute-start.22 = (bf16[16,128]{1,0:T(8,128)(2,1)S(1)}, bf16[16,128]{1,0:T(8,128)(2,1)S(1)}, u32[]{:S(2)}, u32[]{:S(2)}) collective-permute-start(bf16[16,128]{1,0:T(8,128)(2,1)S(1)} %get-tuple-element.111), channel_id=1, source_target_pairs={{0,12},{1,13},{2,14},{3,15},{4,8},{5,9},{6,10},{7,11},{8,4},{9,5},... | collective-permute-start | bytes 12296 | tf_op jit(solution)/shard_map/ppermute | solution.py:37
  88.8 3.4 %collective-permute-start.21 = (bf16[16,128]{1,0:T(8,128)(2,1)S(1)}, bf16[16,128]{1,0:T(8,128)(2,1)S(1)}, u32[]{:S(2)}, u32[]{:S(2)}) collective-permute-start(bf16[16,128]{1,0:T(8,128)(2,1)S(1)} %get-tuple-element.112), channel_id=1, source_target_pairs={{0,8},{1,9},{2,10},{3,11},{4,12},{5,13},{6,14},{7,15},{8,0},{9,1},... | collective-permute-start | bytes 12296 | tf_op jit(solution)/shard_map/ppermute | solution.py:37
  92.2 0.6 collective-permute-done.22
  92.9 3.5 %collective-permute-done.21 = bf16[16,128]{1,0:T(8,128)(2,1)S(1)} collective-permute-done((bf16[16,128]{1,0:T(8,128)(2,1)S(1)}, bf16[16,128]{1,0:T(8,128)(2,1)S(1)}, u32[]{:S(2)}, u32[]{:S(2)}) %collective-permute-start.21) | collective-permute-done | bytes 4128 | tf_op jit(solution)/shard_map/ppermute | solution.py:37
  96.4 0.6 fusion.8
  (45 shorter events, 1.0 us)
Async XLA Ops:
  0.6 19.6 %copy-start.5 = (s32[1,16]{1,0:T(1,128)S(1)}, s32[1,16]{1,0:T(1,128)}, u32[]{:S(2)}) copy-start(s32[1,16]{1,0:T(1,128)} %param.11) | copy-start | bytes 196
  2.2 8.1 %collective-permute-start = (bf16[272,128]{1,0:T(8,128)(2,1)S(1)}, bf16[272,128]{1,0:T(8,128)(2,1)S(1)}, u32[]{:S(2)}, u32[]{:S(2)}) collective-permute-start(bf16[272,128]{1,0:T(8,128)(2,1)S(1)} %get-tuple-element.106), channel_id=1, source_target_pairs={{0,32},{16,48},{32,0},{48,16},{64,96},{80,112},{96,64},{112,80},{1... | collective-permute-start | bytes 208904 | tf_op jit(solution)/shard_map/ppermute | solution.py:37
  4.7 2.2 %copy-start = (bf16[1,16,128,1024]{3,2,1,0:T(8,128)(2,1)S(1)}, bf16[1,16,128,1024]{3,2,1,0:T(8,128)(2,1)}, u32[]{:S(2)}) copy-start(bf16[1,16,128,1024]{3,2,1,0:T(8,128)(2,1)} %param.7) | copy-start | bytes 12582916
  6.9 0.9 copy-start.3
  10.3 8.2 %collective-permute-start.3 = (bf16[2,272,128]{2,1,0:T(8,128)(2,1)S(1)}, bf16[2,272,128]{2,1,0:T(8,128)(2,1)S(1)}, u32[]{:S(2)}, u32[]{:S(2)}) collective-permute-start(bf16[2,272,128]{2,1,0:T(8,128)(2,1)S(1)} %pad_maximum_fusion.q_ref), channel_id=1, source_target_pairs={{0,128},{16,144},{32,160},{48,176},{64,192},{80,208},{96,224},{112... | collective-permute-start | bytes 417800 | tf_op jit(solution)/shard_map/ppermute | solution.py:41
  12.6 7.5 %collective-permute-start.2 = (bf16[2,272,128]{2,1,0:T(8,128)(2,1)S(1)}, bf16[2,272,128]{2,1,0:T(8,128)(2,1)S(1)}, u32[]{:S(2)}, u32[]{:S(2)}) collective-permute-start(bf16[2,272,128]{2,1,0:T(8,128)(2,1)S(1)} %pad_maximum_fusion.q_ref), channel_id=1, source_target_pairs={{0,192},{16,208},{32,224},{48,240},{64,0},{80,16},{96,32},{112,48}... | collective-permute-start | bytes 417800 | tf_op jit(solution)/shard_map/ppermute | solution.py:41
  14.0 6.1 %collective-permute-start.1 = (bf16[2,272,128]{2,1,0:T(8,128)(2,1)S(1)}, bf16[2,272,128]{2,1,0:T(8,128)(2,1)S(1)}, u32[]{:S(2)}, u32[]{:S(2)}) collective-permute-start(bf16[2,272,128]{2,1,0:T(8,128)(2,1)S(1)} %pad_maximum_fusion.q_ref), channel_id=1, source_target_pairs={{0,64},{16,80},{32,96},{48,112},{64,128},{80,144},{96,160},{112,17... | collective-permute-start | bytes 417800 | tf_op jit(solution)/shard_map/ppermute | solution.py:41
  16.0 1.3 %copy-start.1 = (bf16[2,2048,256]{2,1,0:T(8,128)(2,1)}, bf16[2,2048,256]{2,1,0:T(8,128)(2,1)S(1)}, u32[]{:S(2)}) copy-start(bf16[2,2048,256]{2,1,0:T(8,128)(2,1)S(1)} %get-tuple-element.55.p_ref) | copy-start | bytes 6291460
  20.2 4.5 %collective-permute-start.4 = (bf16[8,272,128]{2,1,0:T(8,128)(2,1)S(1)}, bf16[8,272,128]{2,1,0:T(8,128)(2,1)S(1)}, u32[]{:S(2)}, u32[]{:S(2)}) collective-permute-start(bf16[8,272,128]{2,1,0:T(8,128)(2,1)S(1)} %constant_dynamic-update-slice_fusion.q_ref.near_ref), channel_id=1, source_target_pairs={{0,16},{16,0},{32,48},{48,32},{64,80},{80,64},{96,112},{112,96},{1... | collective-permute-start | bytes 1671176 | tf_op jit(solution)/shard_map/ppermute | solution.py:37
  24.8 9.4 %collective-permute-start.7 = (f32[8,256]{1,0:T(8,128)S(1)}, f32[8,256]{1,0:T(8,128)S(1)}, u32[]{:S(2)}, u32[]{:S(2)}) collective-permute-start(f32[8,256]{1,0:T(8,128)S(1)} %targets.1), channel_id=1, source_target_pairs={{0,3},{1,2},{2,1},{3,0},{4,7},{5,6},{6,5},{7,4},{8,11},{9,10},{10,... | collective-permute-start | bytes 24584 | tf_op jit(solution)/shard_map/ppermute | solution.py:37
  29.1 5.1 %collective-permute-start.6 = (f32[8,256]{1,0:T(8,128)S(1)}, f32[8,256]{1,0:T(8,128)S(1)}, u32[]{:S(2)}, u32[]{:S(2)}) collective-permute-start(f32[8,256]{1,0:T(8,128)S(1)} %targets.1), channel_id=1, source_target_pairs={{0,2},{1,3},{2,0},{3,1},{4,6},{5,7},{6,4},{7,5},{8,10},{9,11},{10,... | collective-permute-start | bytes 24584 | tf_op jit(solution)/shard_map/ppermute | solution.py:37
  29.2 5.2 %collective-permute-start.5 = (f32[8,256]{1,0:T(8,128)S(1)}, f32[8,256]{1,0:T(8,128)S(1)}, u32[]{:S(2)}, u32[]{:S(2)}) collective-permute-start(f32[8,256]{1,0:T(8,128)S(1)} %targets.1), channel_id=1, source_target_pairs={{0,1},{1,0},{2,3},{3,2},{4,5},{5,4},{6,7},{7,6},{8,9},{9,8},{10,11... | collective-permute-start | bytes 24584 | tf_op jit(solution)/shard_map/ppermute | solution.py:37
  34.4 10.2 %collective-permute-start.10 = (f32[4,8,256]{2,1,0:T(8,128)S(1)}, f32[4,8,256]{2,1,0:T(8,128)S(1)}, u32[]{:S(2)}, u32[]{:S(2)}) collective-permute-start(f32[4,8,256]{2,1,0:T(8,128)S(1)} %pad_maximum_fusion.2.rest_0_), channel_id=1, source_target_pairs={{0,12},{1,13},{2,14},{3,15},{4,8},{5,9},{6,10},{7,11},{8,4},{9,5},... | collective-permute-start | bytes 98312 | tf_op jit(solution)/shard_map/ppermute | solution.py:37
  40.7 8.0 %collective-permute-start.9 = (f32[4,8,256]{2,1,0:T(8,128)S(1)}, f32[4,8,256]{2,1,0:T(8,128)S(1)}, u32[]{:S(2)}, u32[]{:S(2)}) collective-permute-start(f32[4,8,256]{2,1,0:T(8,128)S(1)} %pad_maximum_fusion.2.rest_0_), channel_id=1, source_target_pairs={{0,8},{1,9},{2,10},{3,11},{4,12},{5,13},{6,14},{7,15},{8,0},{9,1},... | collective-permute-start | bytes 98312 | tf_op jit(solution)/shard_map/ppermute | solution.py:37
  41.7 7.1 %collective-permute-start.8 = (f32[4,8,256]{2,1,0:T(8,128)S(1)}, f32[4,8,256]{2,1,0:T(8,128)S(1)}, u32[]{:S(2)}, u32[]{:S(2)}) collective-permute-start(f32[4,8,256]{2,1,0:T(8,128)S(1)} %pad_maximum_fusion.2.rest_0_), channel_id=1, source_target_pairs={{0,4},{1,5},{2,6},{3,7},{4,0},{5,1},{6,2},{7,3},{8,12},{9,13},{10,... | collective-permute-start | bytes 98312 | tf_op jit(solution)/shard_map/ppermute | solution.py:37
  53.4 5.0 %collective-permute-start.12 = (bf16[6,256,128]{2,1,0:T(8,128)(2,1)S(1)}, bf16[6,256,128]{2,1,0:T(8,128)(2,1)S(1)}, u32[]{:S(2)}, u32[]{:S(2)}) collective-permute-start(bf16[6,256,128]{2,1,0:T(8,128)(2,1)S(1)} %get-tuple-element.93), channel_id=1, source_target_pairs={{0,16},{16,0},{32,48},{48,32},{64,80},{80,64},{96,112},{112,96},{1... | collective-permute-start | bytes 1179656 | tf_op jit(solution)/shard_map/ppermute | solution.py:37
  58.3 6.3 %copy-start.2 = (bf16[2,2048,256]{2,1,0:T(8,128)(2,1)S(1)}, bf16[2,2048,256]{2,1,0:T(8,128)(2,1)}, u32[]{:S(2)}) copy-start(bf16[2,2048,256]{2,1,0:T(8,128)(2,1)} %copy-done.1) | copy-start | bytes 6291460
  58.5 11.9 %collective-permute-start.15 = (bf16[2,256,128]{2,1,0:T(8,128)(2,1)S(1)}, bf16[2,256,128]{2,1,0:T(8,128)(2,1)S(1)}, u32[]{:S(2)}, u32[]{:S(2)}) collective-permute-start(bf16[2,256,128]{2,1,0:T(8,128)(2,1)S(1)} %get-tuple-element.102), channel_id=1, source_target_pairs={{0,128},{16,144},{32,160},{48,176},{64,192},{80,208},{96,224},{112... | collective-permute-start | bytes 393224 | tf_op jit(solution)/shard_map/ppermute | solution.py:41
  60.7 9.7 %collective-permute-start.14 = (bf16[2,256,128]{2,1,0:T(8,128)(2,1)S(1)}, bf16[2,256,128]{2,1,0:T(8,128)(2,1)S(1)}, u32[]{:S(2)}, u32[]{:S(2)}) collective-permute-start(bf16[2,256,128]{2,1,0:T(8,128)(2,1)S(1)} %get-tuple-element.103), channel_id=1, source_target_pairs={{0,64},{16,80},{32,96},{48,112},{64,128},{80,144},{96,160},{112,17... | collective-permute-start | bytes 393224 | tf_op jit(solution)/shard_map/ppermute | solution.py:41
  61.4 9.0 %collective-permute-start.13 = (bf16[2,256,128]{2,1,0:T(8,128)(2,1)S(1)}, bf16[2,256,128]{2,1,0:T(8,128)(2,1)S(1)}, u32[]{:S(2)}, u32[]{:S(2)}) collective-permute-start(bf16[2,256,128]{2,1,0:T(8,128)(2,1)S(1)} %get-tuple-element.104), channel_id=1, source_target_pairs={{0,192},{16,208},{32,224},{48,240},{64,0},{80,16},{96,32},{112,48}... | collective-permute-start | bytes 393224 | tf_op jit(solution)/shard_map/ppermute | solution.py:41
  62.7 3.7 %copy-start.4 = (bf16[1024,128]{1,0:T(8,128)(2,1)S(1)}, bf16[1024,128]{1,0:T(8,128)(2,1)}, u32[]{:S(2)}) copy-start(bf16[1024,128]{1,0:T(8,128)(2,1)} %w_ref.3) | copy-start | bytes 786436
  64.5 5.9 %collective-permute-start.11 = (bf16[2,256,128]{2,1,0:T(8,128)(2,1)S(1)}, bf16[2,256,128]{2,1,0:T(8,128)(2,1)S(1)}, u32[]{:S(2)}, u32[]{:S(2)}) collective-permute-start(bf16[2,256,128]{2,1,0:T(8,128)(2,1)S(1)} %get-tuple-element.91), channel_id=1, source_target_pairs={{0,16},{16,0},{32,48},{48,32},{64,80},{80,64},{96,112},{112,96},{1... | collective-permute-start | bytes 393224 | tf_op jit(solution)/shard_map/ppermute | solution.py:37
  70.5 4.6 %collective-permute-start.16 = (bf16[256,128]{1,0:T(8,128)(2,1)S(1)}, bf16[256,128]{1,0:T(8,128)(2,1)S(1)}, u32[]{:S(2)}, u32[]{:S(2)}) collective-permute-start(bf16[256,128]{1,0:T(8,128)(2,1)S(1)} %fusion.3), channel_id=1, source_target_pairs={{0,32},{16,48},{32,0},{48,16},{64,96},{80,112},{96,64},{112,80},{1... | collective-permute-start | bytes 196616 | tf_op jit(solution)/shard_map/ppermute | solution.py:37
  75.4 5.3 %collective-permute-start.17 = (bf16[4,16,128]{2,1,0:T(8,128)(2,1)S(1)}, bf16[4,16,128]{2,1,0:T(8,128)(2,1)S(1)}, u32[]{:S(2)}, u32[]{:S(2)}) collective-permute-start(bf16[4,16,128]{2,1,0:T(8,128)(2,1)S(1)} %get-tuple-element.107), channel_id=1, source_target_pairs={{0,1},{1,0},{2,3},{3,2},{4,5},{5,4},{6,7},{7,6},{8,9},{9,8},{10,11... | collective-permute-start | bytes 49160 | tf_op jit(solution)/shard_map/ppermute | solution.py:37
  78.3 3.7 %collective-permute-start.18 = (bf16[4,16,128]{2,1,0:T(8,128)(2,1)S(1)}, bf16[4,16,128]{2,1,0:T(8,128)(2,1)S(1)}, u32[]{:S(2)}, u32[]{:S(2)}) collective-permute-start(bf16[4,16,128]{2,1,0:T(8,128)(2,1)S(1)} %get-tuple-element.108), channel_id=1, source_target_pairs={{0,2},{1,3},{2,0},{3,1},{4,6},{5,7},{6,4},{7,5},{8,10},{9,11},{10,... | collective-permute-start | bytes 49160 | tf_op jit(solution)/shard_map/ppermute | solution.py:37
  79.5 6.1 %collective-permute-start.19 = (bf16[4,16,128]{2,1,0:T(8,128)(2,1)S(1)}, bf16[4,16,128]{2,1,0:T(8,128)(2,1)S(1)}, u32[]{:S(2)}, u32[]{:S(2)}) collective-permute-start(bf16[4,16,128]{2,1,0:T(8,128)(2,1)S(1)} %get-tuple-element.109), channel_id=1, source_target_pairs={{0,3},{1,2},{2,1},{3,0},{4,7},{5,6},{6,5},{7,4},{8,11},{9,10},{10,... | collective-permute-start | bytes 49160 | tf_op jit(solution)/shard_map/ppermute | solution.py:37
  85.7 6.6 %collective-permute-start.20 = (bf16[16,128]{1,0:T(8,128)(2,1)S(1)}, bf16[16,128]{1,0:T(8,128)(2,1)S(1)}, u32[]{:S(2)}, u32[]{:S(2)}) collective-permute-start(bf16[16,128]{1,0:T(8,128)(2,1)S(1)} %get-tuple-element.110), channel_id=1, source_target_pairs={{0,4},{1,5},{2,6},{3,7},{4,0},{5,1},{6,2},{7,3},{8,12},{9,13},{10,... | collective-permute-start | bytes 12296 | tf_op jit(solution)/shard_map/ppermute | solution.py:37
  87.2 5.7 %collective-permute-start.22 = (bf16[16,128]{1,0:T(8,128)(2,1)S(1)}, bf16[16,128]{1,0:T(8,128)(2,1)S(1)}, u32[]{:S(2)}, u32[]{:S(2)}) collective-permute-start(bf16[16,128]{1,0:T(8,128)(2,1)S(1)} %get-tuple-element.111), channel_id=1, source_target_pairs={{0,12},{1,13},{2,14},{3,15},{4,8},{5,9},{6,10},{7,11},{8,4},{9,5},... | collective-permute-start | bytes 12296 | tf_op jit(solution)/shard_map/ppermute | solution.py:37
  88.8 7.5 %collective-permute-start.21 = (bf16[16,128]{1,0:T(8,128)(2,1)S(1)}, bf16[16,128]{1,0:T(8,128)(2,1)S(1)}, u32[]{:S(2)}, u32[]{:S(2)}) collective-permute-start(bf16[16,128]{1,0:T(8,128)(2,1)S(1)} %get-tuple-element.112), channel_id=1, source_target_pairs={{0,8},{1,9},{2,10},{3,11},{4,12},{5,13},{6,14},{7,15},{8,0},{9,1},... | collective-permute-start | bytes 12296 | tf_op jit(solution)/shard_map/ppermute | solution.py:37

commit v3 on v2

--- a/solution.py
+++ b/solution.py
@@ -46,21 +46,49 @@
 SHIFTS = (0, 1, -1, 2)
 
 
-def reduce_pa(value, me):
-    ids = jnp.arange(16, dtype=jnp.int32)
-    order = (ids[None, :] == (ids[:, None] ^ me)).astype(bf16)
-    blocks = lax.dot_general(
-        order, value.astype(bf16).reshape(16, 16 * DIM), NN, preferred_element_type=f32
-    ).astype(bf16)
-    blocks = blocks.reshape(4, 4, 16, DIM)
-    total = blocks[:, 0].astype(f32)
-    for j in (1, 2, 3):
-        total = total + swap(blocks[:, j], "pa", j).astype(f32)
-    blocks = total.astype(bf16)
-    total = total[0]
-    for j in (1, 2, 3):
-        total = total + swap(blocks[j], "pa", 4 * j).astype(f32)
-    return total
+def shift_z(value, by):
+    return lax.ppermute(
+        value, "pa", [(i, ((((i >> 1) + by) % 8) << 1) | (i & 1)) for i in range(16)]
+    )
+
+
+Z_PLACE = (0, 2, 7, 6, 4, 3, 5, 1)
+Z_OFFSETS = (0, 1, 7, 3, 4, 2, 5, 6)
+
+
+def swap_y(value, low, high):
+    pairs = [(i, i ^ (32 * low + high)) for i in range(256)]
+    return lax.ppermute(value, ("pb", "pa"), pairs)
+
+
+def order_of(me):
+    j = jnp.arange(16, dtype=jnp.int32)[:, None]
+    offset = jnp.zeros_like(j)
+    for place, one in enumerate(Z_OFFSETS):
+        offset = jnp.where((j & 7) == place, one, offset)
+    block = ((((me >> 1) + offset) & 7) << 1) + ((me & 1) ^ (j >> 3))
+    return (block == jnp.arange(16, dtype=jnp.int32)[None, :]).astype(bf16)
+
+
+def reduce_y_z(value, order):
+    blocks = [
+        lax.dot_general(
+            order, rows.astype(bf16).reshape(16, 16 * DIM), NN, preferred_element_type=f32
+        )
+        .astype(bf16)
+        .reshape(2, 8, 16, DIM)
+        for rows in value
+    ]
+    got = [swap_y(blocks[1][1], 1, 1), swap_y(blocks[0][1], 0, 1), swap_y(blocks[1][0], 1, 0)]
+    blocks = blocks[0][0].astype(f32)
+    for one in got:
+        blocks = blocks + one.astype(f32)
+    up = shift_z(blocks[3:6].astype(bf16), 3).astype(f32)
+    down = shift_z(blocks[6:].astype(bf16), -3).astype(f32)
+    near_up = (blocks[1] + up[1] + down[1]).astype(bf16)
+    near_down = (blocks[2] + up[2]).astype(bf16)
+    up_one, down_one = shift_z(near_up, 1), shift_z(near_down, -1)
+    return blocks[0] + up[0] + down[0] + up_one.astype(f32) + down_one.astype(f32)
 
 
 def project_kernel(hid_ref, w_ref, proj_ref, emb_ref, emb_t_ref):
@@ -96,7 +124,7 @@
             flops=2 * ROWS * H * DIM, bytes_accessed=ROWS * (2 * H + 8 * DIM), transcendentals=0
         ),
         name="project",
-    )(hid, weight)
+    )(*(pltpu.with_memory_space_constraint(x, pltpu.HBM) for x in (hid, weight)))
 
 
 def token_sums(value):
@@ -160,42 +188,45 @@
 def backward_kernel(
     first, half, q_at, q_ref, p_ref, lse_ref, total_ref, emb_t_ref, pick_ref, *rest
 ):
-    target_refs = rest[:4]
+    target_refs = rest[:3]
     qg_ref, eg_ref, c_ref, own_ref, score_ref = rest[-5:]
     g = pl.program_id(0)
-    pick = pick_ref[...]
 
     @pl.when(g == 0)
     def _():
-        eg_ref[...] = jnp.zeros_like(eg_ref) if first else rest[4][...]
+        eg_ref[...] = jnp.zeros_like(eg_ref) if first else rest[3][...]
         own = jnp.zeros((CAP, LEN), f32)
-        for j in range(4):
-            part = target_refs[j][:, :, half * LEN : (half + 1) * LEN].reshape(QT, LEN)
+        for j in range(3):
+            part = target_refs[j][:, :, half * LEN : (half + 1) * LEN].reshape(6 * PD, LEN)
             own += lax.dot_general(
-                pick[:, j * QT : (j + 1) * QT], part, NN, precision=HIGH, preferred_element_type=f32
+                pick_ref[j], part, NN, precision=HIGH, preferred_element_type=f32
             )
         own_ref[...] = own
         score = token_sums(lse_ref[...].reshape(-1, GR)) * (tau / QT)
         score_ref[...] = score.reshape(score_ref.shape)
 
-    queries = q_ref[0, :GR, :]
-    held = jnp.sum(pick, axis=1, keepdims=True)
+    queries = q_ref[:, :GR, :].reshape(2 * GR, DIM)
+    pick = pick_ref[...]
+    held = jnp.sum(pick[0] + pick[1] + pick[2], axis=1, keepdims=True)
     own = own_ref[...]
     lane = lax.broadcasted_iota(jnp.int32, (CAP, LEN), 1) // QT
-    factors = []
-    for k in range(2):
-        lanes = slice(k * LEN, (k + 1) * LEN)
-        at = lane + ((g + q_at) * 2 * GQ + k * (GQ // 2))
-        target = jnp.take_along_axis(own, at, axis=1, mode="promise_in_bounds")
-        residual = (score_ref[g, :, lanes] - target).astype(bf16).astype(f32) * held
-        factors.append((residual / QT) / total_ref[0, :, lanes])
-    factor = jnp.concatenate(factors, axis=1)
-    for k in range(CAP):
-        rows = slice(k * LEN, (k + 1) * LEN)
-        c_ref[rows, :] = (p_ref[0, rows, :].astype(f32) * factor[k : k + 1, :]).astype(bf16)
+    for u in range(2):
+        factors = []
+        for k in range(2):
+            lanes = slice(k * LEN, (k + 1) * LEN)
+            at = lane + ((2 * g + u + q_at) * 2 * GQ + k * (GQ // 2))
+            target = jnp.take_along_axis(own, at, axis=1, mode="promise_in_bounds")
+            residual = (score_ref[2 * g + u, :, lanes] - target).astype(bf16).astype(f32) * held
+            factors.append((residual / QT) / total_ref[u, :, lanes])
+        factor = jnp.concatenate(factors, axis=1)
+        for k in range(CAP):
+            rows = slice(k * LEN, (k + 1) * LEN)
+            c_ref[rows, u * GR : (u + 1) * GR] = (
+                p_ref[u, rows, :].astype(f32) * factor[k : k + 1, :]
+            ).astype(bf16)
     eg_ref[...] += lax.dot_general(c_ref[...], queries, NN, preferred_element_type=f32)
     qg = lax.dot_general(emb_t_ref[...], c_ref[...], NN, preferred_element_type=f32)
-    qg_ref[0] = qg.T.astype(bf16)
+    qg_ref[...] = qg.T.astype(bf16).reshape(2, GR, DIM)
 
 
 def backward(gathered, start, half, kept, emb_t, pick, targets, emb_grad=None):
@@ -205,29 +236,34 @@
     first = emb_grad is None
     whole = lambda g: (0, 0)
     step = lambda g: (g, 0, 0)
+    fixed = lambda g: (0, 0, 0)
     in_specs = [
-        pl.BlockSpec((1, height, DIM), lambda g: (g + start, 0, 0)),
-        pl.BlockSpec((1, ROWS, GR), step),
-        pl.BlockSpec((count, CAP, GR), lambda g: (0, 0, 0)),
-        pl.BlockSpec((1, CAP, GR), step),
+        pl.BlockSpec((2, height, DIM), lambda g: (g + start // 2, 0, 0)),
+        pl.BlockSpec((2, ROWS, GR), step),
+        pl.BlockSpec((count, CAP, GR), fixed),
+        pl.BlockSpec((2, CAP, GR), step),
         pl.BlockSpec((DIM, ROWS), whole),
-        pl.BlockSpec((CAP, LEN), whole),
-    ] + [pl.BlockSpec((4, PD, 2 * LEN), lambda g: (0, 0, 0))] * 4
+        pl.BlockSpec((3, CAP, 6 * PD), fixed),
+    ] + [pl.BlockSpec((6, PD, 2 * LEN), fixed)] * 3
     args = [gathered, p, lse, total, emb_t, pick, *targets]
     if not first:
         in_specs.append(pl.BlockSpec((ROWS, DIM), whole))
         args.append(emb_grad)
     return pl.pallas_call(
         functools.partial(backward_kernel, first, half, start),
-        grid=(count,),
+        grid=(count // 2,),
         in_specs=in_specs,
-        out_specs=[pl.BlockSpec((1, GR, DIM), step), pl.BlockSpec((ROWS, DIM), whole)],
+        out_specs=[pl.BlockSpec((2, GR, DIM), step), pl.BlockSpec((ROWS, DIM), whole)],
         out_shape=[
             jax.ShapeDtypeStruct((count, GR, DIM), bf16),
             jax.ShapeDtypeStruct((ROWS, DIM), f32),
         ],
-        scratch_shapes=[pltpu.VMEM((ROWS, GR), bf16), pltpu.VMEM((CAP, LEN), f32), pltpu.VMEM((count, CAP, GR), f32)],
-        compiler_params=pltpu.CompilerParams(vmem_limit_bytes=11 * 2**20),
+        scratch_shapes=[
+            pltpu.VMEM((ROWS, 2 * GR), bf16),
+            pltpu.VMEM((CAP, LEN), f32),
+            pltpu.VMEM((count, CAP, GR), f32),
+        ],
+        compiler_params=pltpu.CompilerParams(vmem_limit_bytes=14 * 2**20),
         cost_estimate=pl.CostEstimate(
             flops=4 * count * GR * ROWS * DIM,
             bytes_accessed=count * 2 * GR * ROWS,
@@ -269,8 +305,8 @@
     )(emb_grad, proj, weight)
 
 
-def target_kernel(me_ref, near_ref, far_ref, out_ref):
-    row = lax.broadcasted_iota(jnp.int32, (2 * PD, LEN), 0) + me_ref[0] * PD
+def target_kernel(first_ref, near_ref, far_ref, out_ref):
+    row = lax.broadcasted_iota(jnp.int32, (2 * PD, LEN), 0) + first_ref[0]
     own = (row == lax.broadcasted_iota(jnp.int32, (2 * PD, LEN), 1)).astype(f32).astype(bf16)
     for half, ref in enumerate((near_ref, far_ref)):
         ranks = ref[...].reshape(LEN, LEN)
@@ -279,7 +315,7 @@
         out_ref[:, half * LEN : (half + 1) * LEN] = term + pltpu.roll(term, LEN - GQ, 1)
 
 
-def targets_of(me_pb, near, far):
+def targets_of(first_row, near, far):
     rows = pl.BlockSpec((8, 2 * GQ, DIM), lambda i: (0, GR // (2 * GQ), 0))
     return pl.pallas_call(
         target_kernel,
@@ -289,7 +325,7 @@
         out_shape=jax.ShapeDtypeStruct((PD, 2 * LEN), f32),
         compiler_params=pltpu.CompilerParams(vmem_limit_bytes=2 * 2**20),
         name="targets",
-    )(me_pb.reshape(1), near, far)
+    )(first_row, near, far)
 
 
 def rank_term(rank):
@@ -300,14 +336,24 @@
     queries, encoder_outputs, proj_weight, bm25_rank, dense_rank, custodian_document_index
 ):
     me_pb, me_pa = lax.axis_index("pb"), lax.axis_index("pa")
-    ids = jnp.arange(LEN, dtype=jnp.int32)
     slot_ids = custodian_document_index[0]
-    place = jnp.where(slot_ids >= 0, slot_ids ^ (me_pa * PD), -1)
-    pick = (place[:, None] == ids[None, :]).astype(f32)
+    shard = slot_ids >> 3
+    offset = ((shard >> 1) - (me_pa >> 1)) & 7
+    place = jnp.zeros_like(offset)
+    for at, one in enumerate(Z_PLACE):
+        place = jnp.where(offset == at, one, place)
+    place = (place * 2 + ((shard ^ me_pa) & 1)) * PD + (slot_ids & 7)
+    place = jnp.where(slot_ids >= 0, place, -1)
+    rows = jnp.arange(18 * PD, dtype=jnp.int32).reshape(3, 1, 6 * PD)
+    pick = (place[None, :, None] == rows).astype(f32)
     ranks = jnp.concatenate([bm25_rank[:, 0, :], dense_rank[:, 0, :]]).astype(bf16)
     mine = jnp.concatenate([queries, ranks])
     other = swap(mine, "pb", 2)
-    proj, emb, emb_t = project(encoder_outputs.reshape(ROWS, H), proj_weight)
+    first_row, order = (me_pb * PD).reshape(1), order_of(me_pa)
+    other, late_weight, pick, order, first_row = lax.optimization_barrier(
+        (other, proj_weight, pick, order, first_row)
+    )
+    proj, emb, emb_t = project(encoder_outputs.reshape(ROWS, H), late_weight)
     pair = jnp.stack([mine, other])
     got = [shift_x(pair, by) for by in SHIFTS[1:]]
     kept_d = forward(pair, 0, 2, emb)
@@ -316,17 +362,23 @@
     far = swap(plane, "pb", 1)
     kept_b = forward(plane, 2, 6, emb)
     far, kept_b = lax.optimization_barrier((far, kept_b))
-    target = targets_of(me_pb, plane, far)
-    low = [swap(target, "pa", j) for j in (1, 2, 3)]
-    kept_a = forward(far, 2, 6, emb)
-    low, kept_a = lax.optimization_barrier((low, kept_a))
-    low = jnp.stack([target] + low)
-    high = [swap(low, "pa", 4 * j) for j in (1, 2, 3)]
+    target = targets_of(first_row, plane, far)
+    from_y = swap(target, "pa", 1)
     kept_c = forward(far, 0, 2, emb)
-    high, kept_c = lax.optimization_barrier((high, kept_c))
-    own_args = (emb_t, pick, [low] + high)
-    qg_a, eg = backward(far, 2, 1, kept_a, *own_args)
-    from_core = swap(qg_a, "pb", 1)
+    from_y, kept_c = lax.optimization_barrier((from_y, kept_c))
+    targets = jnp.stack([target, from_y])
+    from_z = [shift_z(targets, 1), shift_z(targets, -1)]
+    kept_a = forward(far, 2, 2, emb)
+    from_z, kept_a = lax.optimization_barrier((from_z, kept_a))
+    targets = jnp.concatenate([targets] + from_z)
+    from_z = [shift_z(targets, 3), shift_z(targets, -3)]
+    kept_e = forward(far, 4, 4, emb)
+    from_z, kept_e = lax.optimization_barrier((from_z, kept_e))
+    own_args = (emb_t, pick, [targets] + from_z)
+    qg_e, eg = backward(far, 4, 1, kept_e, *own_args)
+    from_core = [swap(qg_e, "pb", 1)]
+    qg_a, eg = backward(far, 2, 1, kept_a, *own_args, eg)
+    from_core = jnp.concatenate([swap(qg_a, "pb", 1)] + from_core)
     qg_b, eg = backward(plane, 2, 0, kept_b, *own_args, eg)
     sent = (qg_b.astype(f32) + from_core.astype(f32)).astype(bf16).reshape(3, 2, GR, DIM)
     from_x = [shift_x(sent[a - 1], -SHIFTS[a]) for a in (1, 2, 3)]
@@ -338,8 +390,7 @@
     both = qg_d.astype(f32) + from_core.astype(f32)
     for one in from_x:
         both = both + one.astype(f32)
-    from_y = swap(both[1].astype(bf16), "pb", 2)
-    query_grad = reduce_pa(both[0] + from_y.astype(f32), me_pa)
+    query_grad = reduce_y_z(both, order)
     return (query_grad, hidden.reshape(1, CAP, LEN, H))
 
 

time: 98.4 us -> 90 us (0.915); the launches traced: 97 us -> 89.7 us
  waiting for transfers between devices: 20.3 us -> 15.4 us
  local copies, waits for them, and re-layouts: 4.63 us -> 0.22 us
  starting transfers between devices: 36.5 us -> 38.2 us
    ppermute x0 -> x11, starting transfers between devices: none -> 23.3 us  [the longest x8 18.6 us: shift_z(): lax.ppermute(value, 'pa', [(i, ((i >> 1) + by) % 8 << 1 | i & 1) for i in...]
    ppermute x17 -> x6, starting transfers between devices: 28 us -> 5.92 us  [swap(): return lax.ppermute(value, axis, [(i, i ^ mask) for i in range(16)])]
    ppermute x17 -> x6, waiting for transfers between devices: 17.6 us -> 1.6 us  [swap(): return lax.ppermute(value, axis, [(i, i ^ mask) for i in range(16)])]
    ppermute x0 -> x11, waiting for transfers between devices: none -> 13.7 us  [the longest x8 9.11 us: shift_z(): lax.ppermute(value, 'pa', [(i, ((i >> 1) + by) % 8 << 1 | i & 1) for i in...]
    unnamed x16 -> x5, local copies, waits for them, and re-layouts: 4.53 us -> 0.06 us
    ppermute x6, waiting for transfers between devices: 2.73 us -> 0.02 us  [shift_x(): lax.ppermute(value, 'pb', [(i, ((i >> 2) + by) % 4 << 2 | i & 3) for i in...]
    pallas_call x4 -> x5, Pallas kernels: 12.9 us -> 10.6 us  [backward(): pl.pallas_call(functools.partial(backward_kernel, first, half, start), gr...]
    pallas_call x1, Pallas kernels: 2.45 us -> 4.41 us  [project(): pl.pallas_call(project_kernel, grid=(ROWS // step,), in_specs=[pl.BlockSp...]
  transfers between devices with their start and end apart: 23 -> 23, of which waited for: 10 -> 11; matrix products, arithmetic and copies ran while one was open for 1% -> 2% of each run, Pallas kernels for 27% -> 31%
where the time goes in v3:
time: 90 us; the launch traced here: 89.7 us
  starting transfers between devices  38.2 us (42%)
  Pallas kernels  30.6 us (34%)
  waiting for transfers between devices  15.4 us (17%)
  other arithmetic  4.11 us (5%)
  between operations  0.96 us (1%)
    ppermute x8, starting transfers between devices, shift_z(): lax.ppermute(value, 'pa', [(i, ((i >> 1) + by) % 8 << 1 | i & 1) for i in...  18.6 us
    pallas_call x5, Pallas kernels, forward(): pl.pallas_call(forward_kernel, grid=(count,), in_specs=[pl.BlockSpec((1,...  11.4 us
    pallas_call x5, Pallas kernels, backward(): pl.pallas_call(functools.partial(backward_kernel, first, half, start), gr...  10.6 us
    ppermute x8, waiting for transfers between devices, shift_z(): lax.ppermute(value, 'pa', [(i, ((i >> 1) + by) % 8 << 1 | i & 1) for i in...  9.11 us
    ppermute x6, starting transfers between devices, shift_x(): lax.ppermute(value, 'pb', [(i, ((i >> 2) + by) % 4 << 2 | i & 3) for i in...  8.95 us
    ppermute x6, starting transfers between devices, swap(): return lax.ppermute(value, axis, [(i, i ^ mask) for i in range(16)])  5.92 us
    ppermute x3, starting transfers between devices, swap_y(): return lax.ppermute(value, ('pb', 'pa'), pairs)  4.68 us
    ppermute x3, waiting for transfers between devices, swap_y(): return lax.ppermute(value, ('pb', 'pa'), pairs)  4.62 us
  transfers between devices with their start and end apart: 23, of which 11 were waited for; matrix products, arithmetic and copies ran while one was open for 2% of the time, Pallas kernels for 31%

profile of v3, /device:TPU:2, one launch (start us, length us, event | category | flops | bytes accessed | tf_op | source)
XLA Modules:
  0.0 89.7 jit_solution(1774541543320053427)
XLA Ops:
  0.6 0.7 convert_bitcast_fusion
  1.3 0.9 fusion.17
  2.2 1.7 %collective-permute-start = (bf16[272,128]{1,0:T(8,128)(2,1)S(1)}, bf16[272,128]{1,0:T(8,128)(2,1)S(1)}, u32[]{:S(2)}, u32[]{:S(2)}) collective-permute-start(bf16[272,128]{1,0:T(8,128)(2,1)S(1)} %get-tuple-element.134), channel_id=1, source_target_pairs={{0,32},{16,48},{32,0},{48,16},{64,96},{80,112},{96,64},{112,80},{1... | collective-permute-start | bytes 208904 | tf_op jit(solution)/shard_map/ppermute | solution.py:37
  3.9 0.7 bitcast_select_fusion
  4.7 0.8 constant_dynamic-update-slice_fusion.4
  5.5 1.1 %collective-permute-done = bf16[272,128]{1,0:T(8,128)(2,1)S(1)} collective-permute-done((bf16[272,128]{1,0:T(8,128)(2,1)S(1)}, bf16[272,128]{1,0:T(8,128)(2,1)S(1)}, u32[]{:S(2)}, u32[]{:S(2)}) %collective-permute-start) | collective-permute-done | bytes 69664 | tf_op jit(solution)/shard_map/ppermute | solution.py:37
  6.6 2.2 %collective-permute-start.3 = (bf16[2,272,128]{2,1,0:T(8,128)(2,1)S(1)}, bf16[2,272,128]{2,1,0:T(8,128)(2,1)S(1)}, u32[]{:S(2)}, u32[]{:S(2)}) collective-permute-start(bf16[2,272,128]{2,1,0:T(8,128)(2,1)S(1)} %pad_maximum_fusion.q_ref), channel_id=1, source_target_pairs={{0,128},{16,144},{32,160},{48,176},{64,192},{80,208},{96,224},{112... | collective-permute-start | bytes 417800 | tf_op jit(solution)/shard_map/ppermute | solution.py:41
  8.8 1.4 %collective-permute-start.2 = (bf16[2,272,128]{2,1,0:T(8,128)(2,1)S(1)}, bf16[2,272,128]{2,1,0:T(8,128)(2,1)S(1)}, u32[]{:S(2)}, u32[]{:S(2)}) collective-permute-start(bf16[2,272,128]{2,1,0:T(8,128)(2,1)S(1)} %pad_maximum_fusion.q_ref), channel_id=1, source_target_pairs={{0,192},{16,208},{32,224},{48,240},{64,0},{80,16},{96,32},{112,48}... | collective-permute-start | bytes 417800 | tf_op jit(solution)/shard_map/ppermute | solution.py:41
  10.3 0.6 collective-permute-start.1
  10.9 4.4 %project.1 = (f32[2048,128]{1,0:T(8,128)S(1)}, bf16[2048,128]{1,0:T(8,128)(2,1)S(1)}, bf16[128,2048]{1,0:T(8,128)(2,1)S(1)}) custom-call(bf16[2048,1024]{1,0:T(8,128)(2,1)} %bitcast.47, bf16[1024,128]{1,0:T(8,128)(2,1)} %w_ref.2), custom_call_target="tpu_custom_call" | custom-call | flops 536870912 | bytes 6291456 | tf_op jit(solution)/shard_map/project/pallas_call | solution.py:105
  15.3 1.4 %forward.5 = (bf16[2,2048,256]{2,1,0:T(8,128)(2,1)S(1)}, f32[2,16,256]{2,1,0:T(8,128)S(1)}, f32[2,16,256]{2,1,0:T(8,128)S(1)}) custom-call(bf16[2,272,128]{2,1,0:T(8,128)(2,1)S(1)} %pad_maximum_fusion.q_ref, bf16[2048,128]{1,0:T(8,128)(2,1)S(1)} %get-tuple-element.66.emb_ref), custom_call_target="tpu_custom_call" | custom-call | flops 268435456 | bytes 2097152 | tf_op jit(solution)/shard_map/forward/pallas_call | solution.py:161
  17.0 4.3 %forward.6 = (bf16[6,2048,256]{2,1,0:T(8,128)(2,1)S(1)}, f32[6,16,256]{2,1,0:T(8,128)S(1)}, f32[6,16,256]{2,1,0:T(8,128)S(1)}) custom-call(bf16[8,272,128]{2,1,0:T(8,128)(2,1)S(1)} %constant_dynamic-update-slice_fusion.q_ref.near_ref, bf16[2048,128]{1,0:T(8,128)(2,1)S(1)} %get-tuple-element.66.emb_ref), custom_call_target="tpu_custom_call" | custom-call | flops 805306368 | bytes 6291456 | tf_op jit(solution)/shard_map/forward/pallas_call | solution.py:161
  21.3 0.2 targets.1
  21.5 3.2 %collective-permute-start.5 = (f32[8,256]{1,0:T(8,128)S(1)}, f32[8,256]{1,0:T(8,128)S(1)}, u32[]{:S(2)}, u32[]{:S(2)}) collective-permute-start(f32[8,256]{1,0:T(8,128)S(1)} %targets.1), channel_id=1, source_target_pairs={{0,1},{1,0},{2,3},{3,2},{4,5},{5,4},{6,7},{7,6},{8,9},{9,8},{10,11... | collective-permute-start | bytes 24584 | tf_op jit(solution)/shard_map/ppermute | solution.py:37
  24.7 1.4 %forward.7 = (bf16[2,2048,256]{2,1,0:T(8,128)(2,1)S(1)}, f32[2,16,256]{2,1,0:T(8,128)S(1)}, f32[2,16,256]{2,1,0:T(8,128)S(1)}) custom-call(bf16[8,272,128]{2,1,0:T(8,128)(2,1)S(1)} %collective-permute-done.4.far_ref.q_ref, bf16[2048,128]{1,0:T(8,128)(2,1)S(1)} %get-tuple-element.66.emb_ref), custom_call_target="tpu_custom_call" | custom-call | flops 268435456 | bytes 2097152 | tf_op jit(solution)/shard_map/forward/pallas_call | solution.py:161
  26.1 0.5 collective-permute-done.5
  26.7 5.8 %collective-permute-start.7 = (f32[2,8,256]{2,1,0:T(8,128)S(1)}, f32[2,8,256]{2,1,0:T(8,128)S(1)}, u32[]{:S(2)}, u32[]{:S(2)}) collective-permute-start(f32[2,8,256]{2,1,0:T(8,128)S(1)} %pad_maximum_fusion.3), channel_id=1, source_target_pairs={{0,14},{1,15},{2,0},{3,1},{4,2},{5,3},{6,4},{7,5},{8,6},{9,7},{10,... | collective-permute-start | bytes 49160 | tf_op jit(solution)/shard_map/ppermute | solution.py:50
  32.5 1.4 %forward.8 = (bf16[2,2048,256]{2,1,0:T(8,128)(2,1)S(1)}, f32[2,16,256]{2,1,0:T(8,128)S(1)}, f32[2,16,256]{2,1,0:T(8,128)S(1)}) custom-call(bf16[8,272,128]{2,1,0:T(8,128)(2,1)S(1)} %collective-permute-done.4.far_ref.q_ref, bf16[2048,128]{1,0:T(8,128)(2,1)S(1)} %get-tuple-element.66.emb_ref), custom_call_target="tpu_custom_call" | custom-call | flops 268435456 | bytes 2097152 | tf_op jit(solution)/shard_map/forward/pallas_call | solution.py:161
  33.9 3.5 %collective-permute-done.6 = f32[2,8,256]{2,1,0:T(8,128)S(1)} collective-permute-done((f32[2,8,256]{2,1,0:T(8,128)S(1)}, f32[2,8,256]{2,1,0:T(8,128)S(1)}, u32[]{:S(2)}, u32[]{:S(2)}) %collective-permute-start.6) | collective-permute-done | bytes 16416 | tf_op jit(solution)/shard_map/ppermute | solution.py:50
  37.5 0.7 collective-permute-start.9
  38.2 3.1 %collective-permute-start.8 = (f32[6,8,256]{2,1,0:T(8,128)S(1)}, f32[6,8,256]{2,1,0:T(8,128)S(1)}, u32[]{:S(2)}, u32[]{:S(2)}) collective-permute-start(f32[6,8,256]{2,1,0:T(8,128)S(1)} %pad_maximum_fusion.2.rest_0_), channel_id=1, source_target_pairs={{0,6},{1,7},{2,8},{3,9},{4,10},{5,11},{6,12},{7,13},{8,14},{9,15},... | collective-permute-start | bytes 147464 | tf_op jit(solution)/shard_map/ppermute | solution.py:50
  41.3 2.8 %forward.9 = (bf16[4,2048,256]{2,1,0:T(8,128)(2,1)S(1)}, f32[4,16,256]{2,1,0:T(8,128)S(1)}, f32[4,16,256]{2,1,0:T(8,128)S(1)}) custom-call(bf16[8,272,128]{2,1,0:T(8,128)(2,1)S(1)} %collective-permute-done.4.far_ref.q_ref, bf16[2048,128]{1,0:T(8,128)(2,1)S(1)} %get-tuple-element.66.emb_ref), custom_call_target="tpu_custom_call" | custom-call | flops 536870912 | bytes 4194304 | tf_op jit(solution)/shard_map/forward/pallas_call | solution.py:161
  44.1 1.7 %collective-permute-done.8.rest_1_ = f32[6,8,256]{2,1,0:T(8,128)S(1)} collective-permute-done((f32[6,8,256]{2,1,0:T(8,128)S(1)}, f32[6,8,256]{2,1,0:T(8,128)S(1)}, u32[]{:S(2)}, u32[]{:S(2)}) %collective-permute-start.8) | collective-permute-done | bytes 49184 | tf_op jit(solution)/shard_map/ppermute | solution.py:50
  45.9 2.6 %backward.5 = (bf16[4,256,128]{2,1,0:T(8,128)(2,1)S(1)}, f32[2048,128]{1,0:T(8,128)S(1)}) custom-call(bf16[8,272,128]{2,1,0:T(8,128)(2,1)S(1)} %collective-permute-done.4.far_ref.q_ref, bf16[4,2048,256]{2,1,0:T(8,128)(2,1)S(1)} %get-tuple-element.106.p_ref, f32[4,16,256]{2,1,0:T(8,128)S(1)} %get-tuple-element.107.lse_ref, ...), custom_call_target="tpu_custom_call" | custom-call | flops 1073741824 | bytes 4194304 | tf_op jit(solution)/shard_map/backward/pallas_call | solution.py:252
  48.5 0.3 collective-permute-start.12
  48.8 1.4 %backward.6 = (bf16[2,256,128]{2,1,0:T(8,128)(2,1)S(1)}, f32[2048,128]{1,0:T(8,128)S(1)}) custom-call(bf16[8,272,128]{2,1,0:T(8,128)(2,1)S(1)} %collective-permute-done.4.far_ref.q_ref, bf16[2,2048,256]{2,1,0:T(8,128)(2,1)S(1)} %get-tuple-element.103.p_ref, f32[2,16,256]{2,1,0:T(8,128)S(1)} %get-tuple-element.104.lse_ref, ...), custom_call_target="tpu_custom_call" | custom-call | flops 536870912 | bytes 2097152 | tf_op jit(solution)/shard_map/backward/pallas_call | solution.py:252
  50.2 0.6 collective-permute-start.11
  50.8 3.8 %backward.7 = (bf16[6,256,128]{2,1,0:T(8,128)(2,1)S(1)}, f32[2048,128]{1,0:T(8,128)S(1)}) custom-call(bf16[8,272,128]{2,1,0:T(8,128)(2,1)S(1)} %constant_dynamic-update-slice_fusion.q_ref.near_ref, bf16[6,2048,256]{2,1,0:T(8,128)(2,1)S(1)} %get-tuple-element.100.p_ref, f32[6,16,256]{2,1,0:T(8,128)S(1)} %get-tuple-element.101.lse_ref, ...), custom_call_target="tpu_custom_call" | custom-call | flops 1610612736 | bytes 6291456 | tf_op jit(solution)/shard_map/backward/pallas_call | solution.py:252
  54.7 2.7 %collective-permute-start.15 = (bf16[2,256,128]{2,1,0:T(8,128)(2,1)S(1)}, bf16[2,256,128]{2,1,0:T(8,128)(2,1)S(1)}, u32[]{:S(2)}, u32[]{:S(2)}) collective-permute-start(bf16[2,256,128]{2,1,0:T(8,128)(2,1)S(1)} %get-tuple-element.126), channel_id=1, source_target_pairs={{0,128},{16,144},{32,160},{48,176},{64,192},{80,208},{96,224},{112... | collective-permute-start | bytes 393224 | tf_op jit(solution)/shard_map/ppermute | solution.py:41
  57.4 0.3 collective-permute-start.14
  57.7 1.7 %collective-permute-start.13 = (bf16[2,256,128]{2,1,0:T(8,128)(2,1)S(1)}, bf16[2,256,128]{2,1,0:T(8,128)(2,1)S(1)}, u32[]{:S(2)}, u32[]{:S(2)}) collective-permute-start(bf16[2,256,128]{2,1,0:T(8,128)(2,1)S(1)} %get-tuple-element.128), channel_id=1, source_target_pairs={{0,192},{16,208},{32,224},{48,240},{64,0},{80,16},{96,32},{112,48}... | collective-permute-start | bytes 393224 | tf_op jit(solution)/shard_map/ppermute | solution.py:41
  59.4 1.4 %backward.8 = (bf16[2,256,128]{2,1,0:T(8,128)(2,1)S(1)}, f32[2048,128]{1,0:T(8,128)S(1)}) custom-call(bf16[8,272,128]{2,1,0:T(8,128)(2,1)S(1)} %collective-permute-done.4.far_ref.q_ref, bf16[2,2048,256]{2,1,0:T(8,128)(2,1)S(1)} %get-tuple-element.97.p_ref, f32[2,16,256]{2,1,0:T(8,128)S(1)} %get-tuple-element.98.lse_ref, ...), custom_call_target="tpu_custom_call" | custom-call | flops 536870912 | bytes 2097152 | tf_op jit(solution)/shard_map/backward/pallas_call | solution.py:252
  60.9 1.4 %backward.9 = (bf16[2,256,128]{2,1,0:T(8,128)(2,1)S(1)}, f32[2048,128]{1,0:T(8,128)S(1)}) custom-call(bf16[2,272,128]{2,1,0:T(8,128)(2,1)S(1)} %pad_maximum_fusion.q_ref, bf16[2,2048,256]{2,1,0:T(8,128)(2,1)S(1)} %get-tuple-element.70.p_ref, f32[2,16,256]{2,1,0:T(8,128)S(1)} %get-tuple-element.71.lse_ref, f32[2,16,256]{2,1,0:T(8,128)S(1)} %get-tuple-element.72.total_ref, ...), custom_call_target="tpu_custom_call" | custom-call | flops 536870912 | bytes 2097152 | tf_op jit(solution)/shard_map/backward/pallas_call | solution.py:252
  62.4 4.0 %hidden_gradient.1 = bf16[2048,1024]{1,0:T(8,128)(2,1)} custom-call(f32[2048,128]{1,0:T(8,128)S(1)} %get-tuple-element.118.eg_ref, f32[2048,128]{1,0:T(8,128)S(1)} %get-tuple-element.119.proj_ref, bf16[1024,128]{1,0:T(8,128)(2,1)S(1)} %copy-done), custom_call_target="tpu_custom_call" | custom-call | flops 536870912 | bytes 6291456 | tf_op jit(solution)/shard_map/hidden_gradient/pallas_call | solution.py:290
  66.7 3.4 %collective-permute-start.17 = (bf16[8,16,128]{2,1,0:T(8,128)(2,1)S(1)}, bf16[8,16,128]{2,1,0:T(8,128)(2,1)S(1)}, u32[]{:S(2)}, u32[]{:S(2)}) collective-permute-start(bf16[8,16,128]{2,1,0:T(8,128)(2,1)S(1)} %copy.12), channel_id=1, source_target_pairs={{0,1},{1,0},{2,3},{3,2},{4,5},{5,4},{6,7},{7,6},{8,9},{9,8},{10,11... | collective-permute-start | bytes 98312 | tf_op jit(solution)/shard_map/ppermute | solution.py:61
  70.4 0.8 collective-permute-start.18
  71.1 0.5 collective-permute-start.16
  71.6 0.6 collective-permute-done.17
  72.2 2.1 %collective-permute-done.18 = bf16[8,16,128]{2,1,0:T(8,128)(2,1)S(1)} collective-permute-done((bf16[8,16,128]{2,1,0:T(8,128)(2,1)S(1)}, bf16[8,16,128]{2,1,0:T(8,128)(2,1)S(1)}, u32[]{:S(2)}, u32[]{:S(2)}) %collective-permute-start.18) | collective-permute-done | bytes 32800 | tf_op jit(solution)/shard_map/ppermute | solution.py:61
  74.4 1.9 %collective-permute-done.16 = bf16[8,16,128]{2,1,0:T(8,128)(2,1)S(1)} collective-permute-done((bf16[8,16,128]{2,1,0:T(8,128)(2,1)S(1)}, bf16[8,16,128]{2,1,0:T(8,128)(2,1)S(1)}, u32[]{:S(2)}, u32[]{:S(2)}) %collective-permute-start.16) | collective-permute-done | bytes 32800 | tf_op jit(solution)/shard_map/ppermute | solution.py:61
  76.3 1.3 %collective-permute-start.19 = (bf16[3,16,128]{2,1,0:T(8,128)(2,1)S(1)}, bf16[3,16,128]{2,1,0:T(8,128)(2,1)S(1)}, u32[]{:S(2)}, u32[]{:S(2)}) collective-permute-start(bf16[3,16,128]{2,1,0:T(8,128)(2,1)S(1)} %slice.85), channel_id=1, source_target_pairs={{0,6},{1,7},{2,8},{3,9},{4,10},{5,11},{6,12},{7,13},{8,14},{9,15},... | collective-permute-start | bytes 36872 | tf_op jit(solution)/shard_map/ppermute | solution.py:50
  77.5 3.9 %collective-permute-start.20 = (bf16[2,16,128]{2,1,0:T(8,128)(2,1)S(1)}, bf16[2,16,128]{2,1,0:T(8,128)(2,1)S(1)}, u32[]{:S(2)}, u32[]{:S(2)}) collective-permute-start(bf16[2,16,128]{2,1,0:T(8,128)(2,1)S(1)} %slice.87), channel_id=1, source_target_pairs={{0,10},{1,11},{2,12},{3,13},{4,14},{5,15},{6,0},{7,1},{8,2},{9,3},... | collective-permute-start | bytes 24584 | tf_op jit(solution)/shard_map/ppermute | solution.py:50
  81.4 1.6 %collective-permute-done.20 = bf16[2,16,128]{2,1,0:T(8,128)(2,1)S(1)} collective-permute-done((bf16[2,16,128]{2,1,0:T(8,128)(2,1)S(1)}, bf16[2,16,128]{2,1,0:T(8,128)(2,1)S(1)}, u32[]{:S(2)}, u32[]{:S(2)}) %collective-permute-start.20) | collective-permute-done | bytes 8224 | tf_op jit(solution)/shard_map/ppermute | solution.py:50
  83.1 2.4 %collective-permute-start.21 = (bf16[16,128]{1,0:T(8,128)(2,1)S(1)}, bf16[16,128]{1,0:T(8,128)(2,1)S(1)}, u32[]{:S(2)}, u32[]{:S(2)}) collective-permute-start(bf16[16,128]{1,0:T(8,128)(2,1)S(1)} %get-tuple-element.131), channel_id=1, source_target_pairs={{0,2},{1,3},{2,4},{3,5},{4,6},{5,7},{6,8},{7,9},{8,10},{9,11},{10,... | collective-permute-start | bytes 12296 | tf_op jit(solution)/shard_map/ppermute | solution.py:50
  85.5 1.4 %collective-permute-start.22 = (bf16[16,128]{1,0:T(8,128)(2,1)S(1)}, bf16[16,128]{1,0:T(8,128)(2,1)S(1)}, u32[]{:S(2)}, u32[]{:S(2)}) collective-permute-start(bf16[16,128]{1,0:T(8,128)(2,1)S(1)} %get-tuple-element.132), channel_id=1, source_target_pairs={{0,14},{1,15},{2,0},{3,1},{4,2},{5,3},{6,4},{7,5},{8,6},{9,7},{10,... | collective-permute-start | bytes 12296 | tf_op jit(solution)/shard_map/ppermute | solution.py:50
  87.0 1.5 %collective-permute-done.21 = bf16[16,128]{1,0:T(8,128)(2,1)S(1)} collective-permute-done((bf16[16,128]{1,0:T(8,128)(2,1)S(1)}, bf16[16,128]{1,0:T(8,128)(2,1)S(1)}, u32[]{:S(2)}, u32[]{:S(2)}) %collective-permute-start.21) | collective-permute-done | bytes 4128 | tf_op jit(solution)/shard_map/ppermute | solution.py:50
  88.4 0.7 collective-permute-done.22
  89.1 0.6 fusion.7
  (47 shorter events, 1.2 us)
Async XLA Ops:
  2.2 4.4 %collective-permute-start = (bf16[272,128]{1,0:T(8,128)(2,1)S(1)}, bf16[272,128]{1,0:T(8,128)(2,1)S(1)}, u32[]{:S(2)}, u32[]{:S(2)}) collective-permute-start(bf16[272,128]{1,0:T(8,128)(2,1)S(1)} %get-tuple-element.134), channel_id=1, source_target_pairs={{0,32},{16,48},{32,0},{48,16},{64,96},{80,112},{96,64},{112,80},{1... | collective-permute-start | bytes 208904 | tf_op jit(solution)/shard_map/ppermute | solution.py:37
  6.6 10.1 %collective-permute-start.3 = (bf16[2,272,128]{2,1,0:T(8,128)(2,1)S(1)}, bf16[2,272,128]{2,1,0:T(8,128)(2,1)S(1)}, u32[]{:S(2)}, u32[]{:S(2)}) collective-permute-start(bf16[2,272,128]{2,1,0:T(8,128)(2,1)S(1)} %pad_maximum_fusion.q_ref), channel_id=1, source_target_pairs={{0,128},{16,144},{32,160},{48,176},{64,192},{80,208},{96,224},{112... | collective-permute-start | bytes 417800 | tf_op jit(solution)/shard_map/ppermute | solution.py:41
  8.8 7.9 %collective-permute-start.2 = (bf16[2,272,128]{2,1,0:T(8,128)(2,1)S(1)}, bf16[2,272,128]{2,1,0:T(8,128)(2,1)S(1)}, u32[]{:S(2)}, u32[]{:S(2)}) collective-permute-start(bf16[2,272,128]{2,1,0:T(8,128)(2,1)S(1)} %pad_maximum_fusion.q_ref), channel_id=1, source_target_pairs={{0,192},{16,208},{32,224},{48,240},{64,0},{80,16},{96,32},{112,48}... | collective-permute-start | bytes 417800 | tf_op jit(solution)/shard_map/ppermute | solution.py:41
  10.3 6.5 %collective-permute-start.1 = (bf16[2,272,128]{2,1,0:T(8,128)(2,1)S(1)}, bf16[2,272,128]{2,1,0:T(8,128)(2,1)S(1)}, u32[]{:S(2)}, u32[]{:S(2)}) collective-permute-start(bf16[2,272,128]{2,1,0:T(8,128)(2,1)S(1)} %pad_maximum_fusion.q_ref), channel_id=1, source_target_pairs={{0,64},{16,80},{32,96},{48,112},{64,128},{80,144},{96,160},{112,17... | collective-permute-start | bytes 417800 | tf_op jit(solution)/shard_map/ppermute | solution.py:41
  16.9 4.4 %collective-permute-start.4 = (bf16[8,272,128]{2,1,0:T(8,128)(2,1)S(1)}, bf16[8,272,128]{2,1,0:T(8,128)(2,1)S(1)}, u32[]{:S(2)}, u32[]{:S(2)}) collective-permute-start(bf16[8,272,128]{2,1,0:T(8,128)(2,1)S(1)} %constant_dynamic-update-slice_fusion.q_ref.near_ref), channel_id=1, source_target_pairs={{0,16},{16,0},{32,48},{48,32},{64,80},{80,64},{96,112},{112,96},{1... | collective-permute-start | bytes 1671176 | tf_op jit(solution)/shard_map/ppermute | solution.py:37
  21.5 5.2 %collective-permute-start.5 = (f32[8,256]{1,0:T(8,128)S(1)}, f32[8,256]{1,0:T(8,128)S(1)}, u32[]{:S(2)}, u32[]{:S(2)}) collective-permute-start(f32[8,256]{1,0:T(8,128)S(1)} %targets.1), channel_id=1, source_target_pairs={{0,1},{1,0},{2,3},{3,2},{4,5},{5,4},{6,7},{7,6},{8,9},{9,8},{10,11... | collective-permute-start | bytes 24584 | tf_op jit(solution)/shard_map/ppermute | solution.py:37
  26.7 7.3 %collective-permute-start.7 = (f32[2,8,256]{2,1,0:T(8,128)S(1)}, f32[2,8,256]{2,1,0:T(8,128)S(1)}, u32[]{:S(2)}, u32[]{:S(2)}) collective-permute-start(f32[2,8,256]{2,1,0:T(8,128)S(1)} %pad_maximum_fusion.3), channel_id=1, source_target_pairs={{0,14},{1,15},{2,0},{3,1},{4,2},{5,3},{6,4},{7,5},{8,6},{9,7},{10,... | collective-permute-start | bytes 49160 | tf_op jit(solution)/shard_map/ppermute | solution.py:50
  32.5 4.9 %collective-permute-start.6 = (f32[2,8,256]{2,1,0:T(8,128)S(1)}, f32[2,8,256]{2,1,0:T(8,128)S(1)}, u32[]{:S(2)}, u32[]{:S(2)}) collective-permute-start(f32[2,8,256]{2,1,0:T(8,128)S(1)} %pad_maximum_fusion.3), channel_id=1, source_target_pairs={{0,2},{1,3},{2,4},{3,5},{4,6},{5,7},{6,8},{7,9},{8,10},{9,11},{10,... | collective-permute-start | bytes 49160 | tf_op jit(solution)/shard_map/ppermute | solution.py:50
  37.5 6.7 %collective-permute-start.9 = (f32[6,8,256]{2,1,0:T(8,128)S(1)}, f32[6,8,256]{2,1,0:T(8,128)S(1)}, u32[]{:S(2)}, u32[]{:S(2)}) collective-permute-start(f32[6,8,256]{2,1,0:T(8,128)S(1)} %pad_maximum_fusion.2.rest_0_), channel_id=1, source_target_pairs={{0,10},{1,11},{2,12},{3,13},{4,14},{5,15},{6,0},{7,1},{8,2},{9,3},... | collective-permute-start | bytes 147464 | tf_op jit(solution)/shard_map/ppermute | solution.py:50
  38.2 7.7 %collective-permute-start.8 = (f32[6,8,256]{2,1,0:T(8,128)S(1)}, f32[6,8,256]{2,1,0:T(8,128)S(1)}, u32[]{:S(2)}, u32[]{:S(2)}) collective-permute-start(f32[6,8,256]{2,1,0:T(8,128)S(1)} %pad_maximum_fusion.2.rest_0_), channel_id=1, source_target_pairs={{0,6},{1,7},{2,8},{3,9},{4,10},{5,11},{6,12},{7,13},{8,14},{9,15},... | collective-permute-start | bytes 147464 | tf_op jit(solution)/shard_map/ppermute | solution.py:50
  48.5 6.0 %collective-permute-start.12 = (bf16[4,256,128]{2,1,0:T(8,128)(2,1)S(1)}, bf16[4,256,128]{2,1,0:T(8,128)(2,1)S(1)}, u32[]{:S(2)}, u32[]{:S(2)}) collective-permute-start(bf16[4,256,128]{2,1,0:T(8,128)(2,1)S(1)} %get-tuple-element.117), channel_id=1, source_target_pairs={{0,16},{16,0},{32,48},{48,32},{64,80},{80,64},{96,112},{112,96},{1... | collective-permute-start | bytes 786440 | tf_op jit(solution)/shard_map/ppermute | solution.py:37
  50.2 4.4 %collective-permute-start.11 = (bf16[2,256,128]{2,1,0:T(8,128)(2,1)S(1)}, bf16[2,256,128]{2,1,0:T(8,128)(2,1)S(1)}, u32[]{:S(2)}, u32[]{:S(2)}) collective-permute-start(bf16[2,256,128]{2,1,0:T(8,128)(2,1)S(1)} %get-tuple-element.116), channel_id=1, source_target_pairs={{0,16},{16,0},{32,48},{48,32},{64,80},{80,64},{96,112},{112,96},{1... | collective-permute-start | bytes 393224 | tf_op jit(solution)/shard_map/ppermute | solution.py:37
  54.7 11.6 %collective-permute-start.15 = (bf16[2,256,128]{2,1,0:T(8,128)(2,1)S(1)}, bf16[2,256,128]{2,1,0:T(8,128)(2,1)S(1)}, u32[]{:S(2)}, u32[]{:S(2)}) collective-permute-start(bf16[2,256,128]{2,1,0:T(8,128)(2,1)S(1)} %get-tuple-element.126), channel_id=1, source_target_pairs={{0,128},{16,144},{32,160},{48,176},{64,192},{80,208},{96,224},{112... | collective-permute-start | bytes 393224 | tf_op jit(solution)/shard_map/ppermute | solution.py:41
  57.4 9.0 %collective-permute-start.14 = (bf16[2,256,128]{2,1,0:T(8,128)(2,1)S(1)}, bf16[2,256,128]{2,1,0:T(8,128)(2,1)S(1)}, u32[]{:S(2)}, u32[]{:S(2)}) collective-permute-start(bf16[2,256,128]{2,1,0:T(8,128)(2,1)S(1)} %get-tuple-element.127), channel_id=1, source_target_pairs={{0,64},{16,80},{32,96},{48,112},{64,128},{80,144},{96,160},{112,17... | collective-permute-start | bytes 393224 | tf_op jit(solution)/shard_map/ppermute | solution.py:41
  57.7 8.7 %collective-permute-start.13 = (bf16[2,256,128]{2,1,0:T(8,128)(2,1)S(1)}, bf16[2,256,128]{2,1,0:T(8,128)(2,1)S(1)}, u32[]{:S(2)}, u32[]{:S(2)}) collective-permute-start(bf16[2,256,128]{2,1,0:T(8,128)(2,1)S(1)} %get-tuple-element.128), channel_id=1, source_target_pairs={{0,192},{16,208},{32,224},{48,240},{64,0},{80,16},{96,32},{112,48}... | collective-permute-start | bytes 393224 | tf_op jit(solution)/shard_map/ppermute | solution.py:41
  59.4 2.9 %copy-start = (bf16[1024,128]{1,0:T(8,128)(2,1)S(1)}, bf16[1024,128]{1,0:T(8,128)(2,1)}, u32[]{:S(2)}) copy-start(bf16[1024,128]{1,0:T(8,128)(2,1)} %w_ref.2) | copy-start | bytes 786436
  60.8 5.5 %collective-permute-start.10 = (bf16[2,256,128]{2,1,0:T(8,128)(2,1)S(1)}, bf16[2,256,128]{2,1,0:T(8,128)(2,1)S(1)}, u32[]{:S(2)}, u32[]{:S(2)}) collective-permute-start(bf16[2,256,128]{2,1,0:T(8,128)(2,1)S(1)} %get-tuple-element.114), channel_id=1, source_target_pairs={{0,16},{16,0},{32,48},{48,32},{64,80},{80,64},{96,112},{112,96},{1... | collective-permute-start | bytes 393224 | tf_op jit(solution)/shard_map/ppermute | solution.py:37
  66.7 5.5 %collective-permute-start.17 = (bf16[8,16,128]{2,1,0:T(8,128)(2,1)S(1)}, bf16[8,16,128]{2,1,0:T(8,128)(2,1)S(1)}, u32[]{:S(2)}, u32[]{:S(2)}) collective-permute-start(bf16[8,16,128]{2,1,0:T(8,128)(2,1)S(1)} %copy.12), channel_id=1, source_target_pairs={{0,1},{1,0},{2,3},{3,2},{4,5},{5,4},{6,7},{7,6},{8,9},{9,8},{10,11... | collective-permute-start | bytes 98312 | tf_op jit(solution)/shard_map/ppermute | solution.py:61
  70.4 4.0 %collective-permute-start.18 = (bf16[8,16,128]{2,1,0:T(8,128)(2,1)S(1)}, bf16[8,16,128]{2,1,0:T(8,128)(2,1)S(1)}, u32[]{:S(2)}, u32[]{:S(2)}) collective-permute-start(bf16[8,16,128]{2,1,0:T(8,128)(2,1)S(1)} %copy.13), channel_id=1, source_target_pairs={{0,32},{1,33},{2,34},{3,35},{4,36},{5,37},{6,38},{7,39},{8,40},{9,... | collective-permute-start | bytes 98312 | tf_op jit(solution)/shard_map/ppermute | solution.py:61
  71.1 5.1 %collective-permute-start.16 = (bf16[8,16,128]{2,1,0:T(8,128)(2,1)S(1)}, bf16[8,16,128]{2,1,0:T(8,128)(2,1)S(1)}, u32[]{:S(2)}, u32[]{:S(2)}) collective-permute-start(bf16[8,16,128]{2,1,0:T(8,128)(2,1)S(1)} %copy.10), channel_id=1, source_target_pairs={{0,33},{1,32},{2,35},{3,34},{4,37},{5,36},{6,39},{7,38},{8,41},{9,... | collective-permute-start | bytes 98312 | tf_op jit(solution)/shard_map/ppermute | solution.py:61
  76.3 6.8 %collective-permute-start.19 = (bf16[3,16,128]{2,1,0:T(8,128)(2,1)S(1)}, bf16[3,16,128]{2,1,0:T(8,128)(2,1)S(1)}, u32[]{:S(2)}, u32[]{:S(2)}) collective-permute-start(bf16[3,16,128]{2,1,0:T(8,128)(2,1)S(1)} %slice.85), channel_id=1, source_target_pairs={{0,6},{1,7},{2,8},{3,9},{4,10},{5,11},{6,12},{7,13},{8,14},{9,15},... | collective-permute-start | bytes 36872 | tf_op jit(solution)/shard_map/ppermute | solution.py:50
  77.5 5.4 %collective-permute-start.20 = (bf16[2,16,128]{2,1,0:T(8,128)(2,1)S(1)}, bf16[2,16,128]{2,1,0:T(8,128)(2,1)S(1)}, u32[]{:S(2)}, u32[]{:S(2)}) collective-permute-start(bf16[2,16,128]{2,1,0:T(8,128)(2,1)S(1)} %slice.87), channel_id=1, source_target_pairs={{0,10},{1,11},{2,12},{3,13},{4,14},{5,15},{6,0},{7,1},{8,2},{9,3},... | collective-permute-start | bytes 24584 | tf_op jit(solution)/shard_map/ppermute | solution.py:50
  83.1 5.4 %collective-permute-start.21 = (bf16[16,128]{1,0:T(8,128)(2,1)S(1)}, bf16[16,128]{1,0:T(8,128)(2,1)S(1)}, u32[]{:S(2)}, u32[]{:S(2)}) collective-permute-start(bf16[16,128]{1,0:T(8,128)(2,1)S(1)} %get-tuple-element.131), channel_id=1, source_target_pairs={{0,2},{1,3},{2,4},{3,5},{4,6},{5,7},{6,8},{7,9},{8,10},{9,11},{10,... | collective-permute-start | bytes 12296 | tf_op jit(solution)/shard_map/ppermute | solution.py:50
  85.5 3.6 %collective-permute-start.22 = (bf16[16,128]{1,0:T(8,128)(2,1)S(1)}, bf16[16,128]{1,0:T(8,128)(2,1)S(1)}, u32[]{:S(2)}, u32[]{:S(2)}) collective-permute-start(bf16[16,128]{1,0:T(8,128)(2,1)S(1)} %get-tuple-element.132), channel_id=1, source_target_pairs={{0,14},{1,15},{2,0},{3,1},{4,2},{5,3},{6,4},{7,5},{8,6},{9,7},{10,... | collective-permute-start | bytes 12296 | tf_op jit(solution)/shard_map/ppermute | solution.py:50

commit v4 on v3

--- a/solution.py
+++ b/solution.py
@@ -101,7 +101,7 @@
 
 
 def project(hid, weight):
-    step = 512
+    step = 1024
     return pl.pallas_call(
         project_kernel,
         grid=(ROWS // step,),
@@ -119,7 +119,7 @@
             jax.ShapeDtypeStruct((ROWS, DIM), bf16),
             jax.ShapeDtypeStruct((DIM, ROWS), bf16),
         ],
-        compiler_params=pltpu.CompilerParams(vmem_limit_bytes=6 * 2**20),
+        compiler_params=pltpu.CompilerParams(vmem_limit_bytes=12 * 2**20),
         cost_estimate=pl.CostEstimate(
             flops=2 * ROWS * H * DIM, bytes_accessed=ROWS * (2 * H + 8 * DIM), transcendentals=0
         ),
@@ -139,7 +139,8 @@
     return parts[0] + (parts[1] + parts[2])
 
 
-def forward_kernel(q_ref, emb_ref, p_ref, lse_ref, total_ref):
+def forward_kernel(q_ref, emb_ref, *rest):
+    p_ref, lse_ref, total_ref = rest[-3:]
     queries = q_ref[0, :GR, :]
     tops, sums = [], []
     for k in range(CAP):
@@ -156,33 +157,36 @@
     total_ref[0] = total
 
 
-def forward(gathered, start, count, emb):
+def forward(gathered, start, count, emb, place, size, kept=(), after=()):
     height = gathered.shape[1]
+    step = lambda g: (g + place, 0, 0)
     return pl.pallas_call(
         forward_kernel,
         grid=(count,),
         in_specs=[
             pl.BlockSpec((1, height, DIM), lambda g: (g + start, 0, 0)),
             pl.BlockSpec((ROWS, DIM), lambda g: (0, 0)),
-        ],
+        ]
+        + [pl.BlockSpec(memory_space=pl.ANY)] * (len(kept) + len(after)),
         out_specs=[
-            pl.BlockSpec((1, ROWS, GR), lambda g: (g, 0, 0)),
-            pl.BlockSpec((1, CAP, GR), lambda g: (g, 0, 0)),
-            pl.BlockSpec((1, CAP, GR), lambda g: (g, 0, 0)),
+            pl.BlockSpec((1, ROWS, GR), step),
+            pl.BlockSpec((1, CAP, GR), step),
+            pl.BlockSpec((1, CAP, GR), step),
         ],
         out_shape=[
-            jax.ShapeDtypeStruct((count, ROWS, GR), bf16),
-            jax.ShapeDtypeStruct((count, CAP, GR), f32),
-            jax.ShapeDtypeStruct((count, CAP, GR), f32),
-        ],
+            jax.ShapeDtypeStruct((size, ROWS, GR), bf16),
+            jax.ShapeDtypeStruct((size, CAP, GR), f32),
+            jax.ShapeDtypeStruct((size, CAP, GR), f32),
+        ],
+        input_output_aliases={2 + i: i for i in range(len(kept))},
         compiler_params=pltpu.CompilerParams(vmem_limit_bytes=6 * 2**20),
         cost_estimate=pl.CostEstimate(
-            flops=2 * count * GR * ROWS * DIM,
-            bytes_accessed=count * 2 * GR * ROWS,
-            transcendentals=count * GR * ROWS,
+            flops=2 * count * GR * ROWS * DIM // 4,
+            bytes_accessed=count * 2 * GR * ROWS // 4,
+            transcendentals=count * GR * ROWS // 4,
         ),
         name="forward",
-    )(gathered, emb)
+    )(gathered, emb, *kept, *after)
 
 
 def backward_kernel(
@@ -286,7 +290,7 @@
 
 
 def hidden_gradient(emb_grad, proj, weight):
-    step = 512
+    step = 1024
     return pl.pallas_call(
         hidden_kernel,
         grid=(ROWS // step,),
@@ -297,7 +301,7 @@
         ],
         out_specs=pl.BlockSpec((step, H), lambda i: (i, 0)),
         out_shape=jax.ShapeDtypeStruct((ROWS, H), bf16),
-        compiler_params=pltpu.CompilerParams(vmem_limit_bytes=8 * 2**20),
+        compiler_params=pltpu.CompilerParams(vmem_limit_bytes=12 * 2**20),
         cost_estimate=pl.CostEstimate(
             flops=2 * ROWS * H * DIM, bytes_accessed=ROWS * (2 * H + 8 * DIM), transcendentals=0
         ),
@@ -356,38 +360,35 @@
     proj, emb, emb_t = project(encoder_outputs.reshape(ROWS, H), late_weight)
     pair = jnp.stack([mine, other])
     got = [shift_x(pair, by) for by in SHIFTS[1:]]
-    kept_d = forward(pair, 0, 2, emb)
+    kept_d = forward(pair, 0, 2, emb, 0, 2)
     got, kept_d = lax.optimization_barrier((got, kept_d))
     plane = jnp.concatenate([pair] + got)
     far = swap(plane, "pb", 1)
-    kept_b = forward(plane, 2, 6, emb)
+    kept_b = forward(plane, 2, 4, emb, 0, 6)
     far, kept_b = lax.optimization_barrier((far, kept_b))
     target = targets_of(first_row, plane, far)
     from_y = swap(target, "pa", 1)
-    kept_c = forward(far, 0, 2, emb)
-    from_y, kept_c = lax.optimization_barrier((from_y, kept_c))
+    kept_b = forward(plane, 6, 2, emb, 4, 6, kept_b, [target])
+    kept_f = forward(far, 0, 2, emb, 0, 8, after=[target])
+    from_y, kept_b, kept_f = lax.optimization_barrier((from_y, kept_b, kept_f))
     targets = jnp.stack([target, from_y])
     from_z = [shift_z(targets, 1), shift_z(targets, -1)]
-    kept_a = forward(far, 2, 2, emb)
-    from_z, kept_a = lax.optimization_barrier((from_z, kept_a))
+    kept_f = forward(far, 2, 2, emb, 2, 8, kept_f)
+    from_z, kept_f = lax.optimization_barrier((from_z, kept_f))
     targets = jnp.concatenate([targets] + from_z)
     from_z = [shift_z(targets, 3), shift_z(targets, -3)]
-    kept_e = forward(far, 4, 4, emb)
-    from_z, kept_e = lax.optimization_barrier((from_z, kept_e))
+    kept_f = forward(far, 4, 4, emb, 4, 8, kept_f)
+    from_z, kept_f = lax.optimization_barrier((from_z, kept_f))
     own_args = (emb_t, pick, [targets] + from_z)
-    qg_e, eg = backward(far, 4, 1, kept_e, *own_args)
-    from_core = [swap(qg_e, "pb", 1)]
-    qg_a, eg = backward(far, 2, 1, kept_a, *own_args, eg)
-    from_core = jnp.concatenate([swap(qg_a, "pb", 1)] + from_core)
+    qg_f, eg = backward(far, 0, 1, kept_f, *own_args)
+    from_core = swap(qg_f, "pb", 1)
     qg_b, eg = backward(plane, 2, 0, kept_b, *own_args, eg)
-    sent = (qg_b.astype(f32) + from_core.astype(f32)).astype(bf16).reshape(3, 2, GR, DIM)
+    sent = (qg_b.astype(f32) + from_core[2:].astype(f32)).astype(bf16).reshape(3, 2, GR, DIM)
     from_x = [shift_x(sent[a - 1], -SHIFTS[a]) for a in (1, 2, 3)]
-    qg_c, eg = backward(far, 0, 1, kept_c, *own_args, eg)
-    from_core = swap(qg_c, "pb", 1)
     qg_d, eg = backward(pair, 0, 0, kept_d, *own_args, eg)
     hidden = hidden_gradient(eg, proj, proj_weight)
     from_x, hidden = lax.optimization_barrier((from_x, hidden))
-    both = qg_d.astype(f32) + from_core.astype(f32)
+    both = qg_d.astype(f32) + from_core[:2].astype(f32)
     for one in from_x:
         both = both + one.astype(f32)
     query_grad = reduce_y_z(both, order)

time: 90 us -> 86.4 us (0.960)
  waiting for transfers between devices: 15.4 us -> 12.7 us
  Pallas kernels: 30.6 us -> 28.7 us
    ppermute x8, starting transfers between devices: 18.6 us -> 20.1 us  [shift_z(): lax.ppermute(value, 'pa', [(i, ((i >> 1) + by) % 8 << 1 | i & 1) for i in...]
    ppermute x8, waiting for transfers between devices: 9.11 us -> 7.85 us  [shift_z(): lax.ppermute(value, 'pa', [(i, ((i >> 1) + by) % 8 << 1 | i & 1) for i in...]
    ppermute x6 -> x4, starting transfers between devices: 5.92 us -> 4.89 us  [swap(): return lax.ppermute(value, axis, [(i, i ^ mask) for i in range(16)])]
    ppermute x3, starting transfers between devices: 4.68 us -> 3.66 us  [swap_y(): return lax.ppermute(value, ('pb', 'pa'), pairs)]
    pallas_call x1, Pallas kernels: 4.41 us -> 3.5 us  [project(): pl.pallas_call(project_kernel, grid=(ROWS // step,), in_specs=[pl.BlockSp...]
    pallas_call x5 -> x3, Pallas kernels: 10.6 us -> 10 us  [backward(): pl.pallas_call(functools.partial(backward_kernel, first, half, start), gr...]
    pallas_call x5 -> x6, Pallas kernels: 11.4 us -> 11.4 us  [forward(): pl.pallas_call(forward_kernel, grid=(count,), in_specs=[pl.BlockSpec((1,...]
  transfers between devices with their start and end apart: 23 -> 21, of which waited for: 11 -> 8; matrix products, arithmetic and copies ran while one was open for 2% -> 2% of each run, Pallas kernels for 31% -> 28%
where the time goes in v4:
time: 86.4 us; the launch traced here: 85.3 us
  starting transfers between devices  38.3 us (44%)
  Pallas kernels  28.7 us (33%)
  waiting for transfers between devices  12.7 us (15%)
  other arithmetic  4.11 us (5%)
  between operations  0.95 us (1%)
    ppermute x8, starting transfers between devices, shift_z(): lax.ppermute(value, 'pa', [(i, ((i >> 1) + by) % 8 << 1 | i & 1) for i in...  20.1 us
    pallas_call x6, Pallas kernels, forward(): pl.pallas_call(forward_kernel, grid=(count,), in_specs=[pl.BlockSpec((1,...  11.4 us
    pallas_call x3, Pallas kernels, backward(): pl.pallas_call(functools.partial(backward_kernel, first, half, start), gr...  10 us
    ppermute x6, starting transfers between devices, shift_x(): lax.ppermute(value, 'pb', [(i, ((i >> 2) + by) % 4 << 2 | i & 3) for i in...  9.59 us
    ppermute x8, waiting for transfers between devices, shift_z(): lax.ppermute(value, 'pa', [(i, ((i >> 1) + by) % 8 << 1 | i & 1) for i in...  7.85 us
    ppermute x4, starting transfers between devices, swap(): return lax.ppermute(value, axis, [(i, i ^ mask) for i in range(16)])  4.89 us
    ppermute x3, waiting for transfers between devices, swap_y(): return lax.ppermute(value, ('pb', 'pa'), pairs)  3.77 us
    ppermute x3, starting transfers between devices, swap_y(): return lax.ppermute(value, ('pb', 'pa'), pairs)  3.66 us
  transfers between devices with their start and end apart: 21, of which 8 were waited for; matrix products, arithmetic and copies ran while one was open for 2% of the time, Pallas kernels for 28%

profile of v4, /device:TPU:2, one launch (start us, length us, event | category | flops | bytes accessed | tf_op | source)
XLA Modules:
  0.0 85.3 jit_solution(13061473906782416052)
XLA Ops:
  0.6 0.7 convert_bitcast_fusion
  1.3 0.9 %fusion.17 = (bf16[1,272,128]{2,1,0:T(8,128)(2,1)S(1)}, bf16[272,128]{1,0:T(8,128)(2,1)S(1)}) fusion(bf16[8,128]{1,0:T(8,128)(2,1)S(1)} %get-tuple-element.143, bf16[8,128]{1,0:T(8,128)(2,1)S(1)} %get-tuple-element.144, bf16[256,128]{1,0:T(8,128)(2,1)} %param.6), kind=kLoop, calls=%fused_computation.60 | loop fusion | flops 208896 | bytes 208896 | tf_op jit(solution)/shard_map/stack | solution.py:361
  2.2 1.7 %collective-permute-start = (bf16[272,128]{1,0:T(8,128)(2,1)S(1)}, bf16[272,128]{1,0:T(8,128)(2,1)S(1)}, u32[]{:S(2)}, u32[]{:S(2)}) collective-permute-start(bf16[272,128]{1,0:T(8,128)(2,1)S(1)} %get-tuple-element.138), channel_id=1, source_target_pairs={{0,32},{16,48},{32,0},{48,16},{64,96},{80,112},{96,64},{112,80},{1... | collective-permute-start | bytes 208904 | tf_op jit(solution)/shard_map/ppermute | solution.py:37
  3.9 0.7 bitcast_select_fusion
  4.7 0.8 constant_dynamic-update-slice_fusion.4
  5.5 1.1 %collective-permute-done = bf16[272,128]{1,0:T(8,128)(2,1)S(1)} collective-permute-done((bf16[272,128]{1,0:T(8,128)(2,1)S(1)}, bf16[272,128]{1,0:T(8,128)(2,1)S(1)}, u32[]{:S(2)}, u32[]{:S(2)}) %collective-permute-start) | collective-permute-done | bytes 69664 | tf_op jit(solution)/shard_map/ppermute | solution.py:37
  6.6 1.6 %collective-permute-start.1 = (bf16[2,272,128]{2,1,0:T(8,128)(2,1)S(1)}, bf16[2,272,128]{2,1,0:T(8,128)(2,1)S(1)}, u32[]{:S(2)}, u32[]{:S(2)}) collective-permute-start(bf16[2,272,128]{2,1,0:T(8,128)(2,1)S(1)} %pad_maximum_fusion.q_ref), channel_id=1, source_target_pairs={{0,64},{16,80},{32,96},{48,112},{64,128},{80,144},{96,160},{112,17... | collective-permute-start | bytes 417800 | tf_op jit(solution)/shard_map/ppermute | solution.py:41
  8.2 0.9 %collective-permute-start.2 = (bf16[2,272,128]{2,1,0:T(8,128)(2,1)S(1)}, bf16[2,272,128]{2,1,0:T(8,128)(2,1)S(1)}, u32[]{:S(2)}, u32[]{:S(2)}) collective-permute-start(bf16[2,272,128]{2,1,0:T(8,128)(2,1)S(1)} %pad_maximum_fusion.q_ref), channel_id=1, source_target_pairs={{0,192},{16,208},{32,224},{48,240},{64,0},{80,16},{96,32},{112,48}... | collective-permute-start | bytes 417800 | tf_op jit(solution)/shard_map/ppermute | solution.py:41
  9.1 2.0 %collective-permute-start.3 = (bf16[2,272,128]{2,1,0:T(8,128)(2,1)S(1)}, bf16[2,272,128]{2,1,0:T(8,128)(2,1)S(1)}, u32[]{:S(2)}, u32[]{:S(2)}) collective-permute-start(bf16[2,272,128]{2,1,0:T(8,128)(2,1)S(1)} %pad_maximum_fusion.q_ref), channel_id=1, source_target_pairs={{0,128},{16,144},{32,160},{48,176},{64,192},{80,208},{96,224},{112... | collective-permute-start | bytes 417800 | tf_op jit(solution)/shard_map/ppermute | solution.py:41
  11.0 3.5 %project.1 = (f32[2048,128]{1,0:T(8,128)S(1)}, bf16[2048,128]{1,0:T(8,128)(2,1)S(1)}, bf16[128,2048]{1,0:T(8,128)(2,1)S(1)}) custom-call(bf16[2048,1024]{1,0:T(8,128)(2,1)} %bitcast.47, bf16[1024,128]{1,0:T(8,128)(2,1)} %w_ref.2), custom_call_target="tpu_custom_call" | custom-call | flops 536870912 | bytes 6291456 | tf_op jit(solution)/shard_map/project/pallas_call | solution.py:105
  14.5 1.4 %forward.6 = (bf16[2,2048,256]{2,1,0:T(8,128)(2,1)S(1)}, f32[2,16,256]{2,1,0:T(8,128)S(1)}, f32[2,16,256]{2,1,0:T(8,128)S(1)}) custom-call(bf16[2,272,128]{2,1,0:T(8,128)(2,1)S(1)} %pad_maximum_fusion.q_ref, bf16[2048,128]{1,0:T(8,128)(2,1)S(1)} %get-tuple-element.68.emb_ref), custom_call_target="tpu_custom_call" | custom-call | flops 67108864 | bytes 524288 | tf_op jit(solution)/shard_map/forward/pallas_call | solution.py:163
  16.1 0.1 collective-permute-start.4
  16.2 2.9 %forward.7 = (bf16[6,2048,256]{2,1,0:T(8,128)(2,1)S(1)}, f32[6,16,256]{2,1,0:T(8,128)S(1)}, f32[6,16,256]{2,1,0:T(8,128)S(1)}) custom-call(bf16[8,272,128]{2,1,0:T(8,128)(2,1)S(1)} %constant_dynamic-update-slice_fusion.q_ref.near_ref, bf16[2048,128]{1,0:T(8,128)(2,1)S(1)} %get-tuple-element.68.emb_ref), custom_call_target="tpu_custom_call" | custom-call | flops 134217728 | bytes 1048576 | tf_op jit(solution)/shard_map/forward/pallas_call | solution.py:163
  19.1 0.2 targets.1.rest_3_.rest_0_
  19.3 3.0 %collective-permute-start.5 = (f32[8,256]{1,0:T(8,128)S(1)}, f32[8,256]{1,0:T(8,128)S(1)}, u32[]{:S(2)}, u32[]{:S(2)}) collective-permute-start(f32[8,256]{1,0:T(8,128)S(1)} %targets.1.rest_3_.rest_0_), channel_id=1, source_target_pairs={{0,1},{1,0},{2,3},{3,2},{4,5},{5,4},{6,7},{7,6},{8,9},{9,8},{10,11... | collective-permute-start | bytes 24584 | tf_op jit(solution)/shard_map/ppermute | solution.py:37
  22.4 1.4 %forward.9 = (bf16[8,2048,256]{2,1,0:T(8,128)(2,1)S(1)}, f32[8,16,256]{2,1,0:T(8,128)S(1)}, f32[8,16,256]{2,1,0:T(8,128)S(1)}) custom-call(bf16[8,272,128]{2,1,0:T(8,128)(2,1)S(1)} %collective-permute-done.4.far_ref.q_ref, bf16[2048,128]{1,0:T(8,128)(2,1)S(1)} %get-tuple-element.68.emb_ref, f32[8,256]{1,0:T(8,128)S(1)} %targets.1.rest_3_.rest_0_), custom_call_target="tpu_custom_call" | custom-call | flops 67108864 | bytes 524288 | tf_op jit(solution)/shard_map/forward/pallas_call | solution.py:163
  23.8 1.4 %forward.8 = (bf16[6,2048,256]{2,1,0:T(8,128)(2,1)S(1)}, f32[6,16,256]{2,1,0:T(8,128)S(1)}, f32[6,16,256]{2,1,0:T(8,128)S(1)}) custom-call(bf16[8,272,128]{2,1,0:T(8,128)(2,1)S(1)} %constant_dynamic-update-slice_fusion.q_ref.near_ref, bf16[2048,128]{1,0:T(8,128)(2,1)S(1)} %get-tuple-element.68.emb_ref, ...), custom_call_target="tpu_custom_call", output_to_operand_aliasing={{0}: (2, {}), {1}: (3, {}), {2}: (4, {})} | custom-call | flops 67108864 | bytes 524288 | tf_op jit(solution)/shard_map/forward/pallas_call | solution.py:163
  25.3 2.0 %collective-permute-start.6 = (f32[2,8,256]{2,1,0:T(8,128)S(1)}, f32[2,8,256]{2,1,0:T(8,128)S(1)}, u32[]{:S(2)}, u32[]{:S(2)}) collective-permute-start(f32[2,8,256]{2,1,0:T(8,128)S(1)} %pad_maximum_fusion.3), channel_id=1, source_target_pairs={{0,2},{1,3},{2,4},{3,5},{4,6},{5,7},{6,8},{7,9},{8,10},{9,11},{10,... | collective-permute-start | bytes 49160 | tf_op jit(solution)/shard_map/ppermute | solution.py:50
  27.2 4.0 %collective-permute-start.7 = (f32[2,8,256]{2,1,0:T(8,128)S(1)}, f32[2,8,256]{2,1,0:T(8,128)S(1)}, u32[]{:S(2)}, u32[]{:S(2)}) collective-permute-start(f32[2,8,256]{2,1,0:T(8,128)S(1)} %pad_maximum_fusion.3), channel_id=1, source_target_pairs={{0,14},{1,15},{2,0},{3,1},{4,2},{5,3},{6,4},{7,5},{8,6},{9,7},{10,... | collective-permute-start | bytes 49160 | tf_op jit(solution)/shard_map/ppermute | solution.py:50
  31.3 1.4 %forward.10 = (bf16[8,2048,256]{2,1,0:T(8,128)(2,1)S(1)}, f32[8,16,256]{2,1,0:T(8,128)S(1)}, f32[8,16,256]{2,1,0:T(8,128)S(1)}) custom-call(bf16[8,272,128]{2,1,0:T(8,128)(2,1)S(1)} %collective-permute-done.4.far_ref.q_ref, bf16[2048,128]{1,0:T(8,128)(2,1)S(1)} %get-tuple-element.68.emb_ref, ...), custom_call_target="tpu_custom_call", output_to_operand_aliasing={{0}: (2, {}), {1}: (3, {}), {2}: (4, {})} | custom-call | flops 67108864 | bytes 524288 | tf_op jit(solution)/shard_map/forward/pallas_call | solution.py:163
  32.7 0.2 collective-permute-done.6
  32.9 5.1 %collective-permute-start.8 = (f32[6,8,256]{2,1,0:T(8,128)S(1)}, f32[6,8,256]{2,1,0:T(8,128)S(1)}, u32[]{:S(2)}, u32[]{:S(2)}) collective-permute-start(f32[6,8,256]{2,1,0:T(8,128)S(1)} %pad_maximum_fusion.2.rest_0_), channel_id=1, source_target_pairs={{0,6},{1,7},{2,8},{3,9},{4,10},{5,11},{6,12},{7,13},{8,14},{9,15},... | collective-permute-start | bytes 147464 | tf_op jit(solution)/shard_map/ppermute | solution.py:50
  38.0 2.8 %forward.11 = (bf16[8,2048,256]{2,1,0:T(8,128)(2,1)S(1)}, f32[8,16,256]{2,1,0:T(8,128)S(1)}, f32[8,16,256]{2,1,0:T(8,128)S(1)}) custom-call(bf16[8,272,128]{2,1,0:T(8,128)(2,1)S(1)} %collective-permute-done.4.far_ref.q_ref, bf16[2048,128]{1,0:T(8,128)(2,1)S(1)} %get-tuple-element.68.emb_ref, ...), custom_call_target="tpu_custom_call", output_to_operand_aliasing={{0}: (2, {}), {1}: (3, {}), {2}: (4, {})} | custom-call | flops 134217728 | bytes 1048576 | tf_op jit(solution)/shard_map/forward/pallas_call | solution.py:163
  40.9 4.2 %collective-permute-done.9.rest_2_ = f32[6,8,256]{2,1,0:T(8,128)S(1)} collective-permute-done((f32[6,8,256]{2,1,0:T(8,128)S(1)}, f32[6,8,256]{2,1,0:T(8,128)S(1)}, u32[]{:S(2)}, u32[]{:S(2)}) %collective-permute-start.9) | collective-permute-done | bytes 49184 | tf_op jit(solution)/shard_map/ppermute | solution.py:50
  45.1 4.9 %backward.3 = (bf16[8,256,128]{2,1,0:T(8,128)(2,1)S(1)}, f32[2048,128]{1,0:T(8,128)S(1)}) custom-call(bf16[8,272,128]{2,1,0:T(8,128)(2,1)S(1)} %collective-permute-done.4.far_ref.q_ref, bf16[8,2048,256]{2,1,0:T(8,128)(2,1)S(1)} %get-tuple-element.114.p_ref, f32[8,16,256]{2,1,0:T(8,128)S(1)} %get-tuple-element.115.lse_ref, ...), custom_call_target="tpu_custom_call" | custom-call | flops 2147483648 | bytes 8388608 | tf_op jit(solution)/shard_map/backward/pallas_call | solution.py:256
  50.1 3.8 %backward.4 = (bf16[6,256,128]{2,1,0:T(8,128)(2,1)S(1)}, f32[2048,128]{1,0:T(8,128)S(1)}) custom-call(bf16[8,272,128]{2,1,0:T(8,128)(2,1)S(1)} %constant_dynamic-update-slice_fusion.q_ref.near_ref, bf16[6,2048,256]{2,1,0:T(8,128)(2,1)S(1)} %get-tuple-element.111.p_ref, f32[6,16,256]{2,1,0:T(8,128)S(1)} %get-tuple-element.112.lse_ref, ...), custom_call_target="tpu_custom_call" | custom-call | flops 1610612736 | bytes 6291456 | tf_op jit(solution)/shard_map/backward/pallas_call | solution.py:256
  53.9 0.1 add_convert_fusion
  54.0 1.5 %collective-permute-start.11 = (bf16[2,256,128]{2,1,0:T(8,128)(2,1)S(1)}, bf16[2,256,128]{2,1,0:T(8,128)(2,1)S(1)}, u32[]{:S(2)}, u32[]{:S(2)}) collective-permute-start(bf16[2,256,128]{2,1,0:T(8,128)(2,1)S(1)} %get-tuple-element.132), channel_id=1, source_target_pairs={{0,192},{16,208},{32,224},{48,240},{64,0},{80,16},{96,32},{112,48}... | collective-permute-start | bytes 393224 | tf_op jit(solution)/shard_map/ppermute | solution.py:41
  55.5 0.6 collective-permute-start.12
  56.1 3.1 %collective-permute-start.13 = (bf16[2,256,128]{2,1,0:T(8,128)(2,1)S(1)}, bf16[2,256,128]{2,1,0:T(8,128)(2,1)S(1)}, u32[]{:S(2)}, u32[]{:S(2)}) collective-permute-start(bf16[2,256,128]{2,1,0:T(8,128)(2,1)S(1)} %get-tuple-element.130), channel_id=1, source_target_pairs={{0,128},{16,144},{32,160},{48,176},{64,192},{80,208},{96,224},{112... | collective-permute-start | bytes 393224 | tf_op jit(solution)/shard_map/ppermute | solution.py:41
  59.2 1.4 %backward.5 = (bf16[2,256,128]{2,1,0:T(8,128)(2,1)S(1)}, f32[2048,128]{1,0:T(8,128)S(1)}) custom-call(bf16[2,272,128]{2,1,0:T(8,128)(2,1)S(1)} %pad_maximum_fusion.q_ref, bf16[2,2048,256]{2,1,0:T(8,128)(2,1)S(1)} %get-tuple-element.72.p_ref, f32[2,16,256]{2,1,0:T(8,128)S(1)} %get-tuple-element.73.lse_ref, f32[2,16,256]{2,1,0:T(8,128)S(1)} %get-tuple-element.74.total_ref, ...), custom_call_target="tpu_custom_call" | custom-call | flops 536870912 | bytes 2097152 | tf_op jit(solution)/shard_map/backward/pallas_call | solution.py:256
  60.6 3.6 %hidden_gradient.1 = bf16[2048,1024]{1,0:T(8,128)(2,1)} custom-call(f32[2048,128]{1,0:T(8,128)S(1)} %get-tuple-element.122.eg_ref, f32[2048,128]{1,0:T(8,128)S(1)} %get-tuple-element.123.proj_ref, bf16[1024,128]{1,0:T(8,128)(2,1)S(1)} %copy-done), custom_call_target="tpu_custom_call" | custom-call | flops 536870912 | bytes 6291456 | tf_op jit(solution)/shard_map/hidden_gradient/pallas_call | solution.py:294
  64.2 0.1 add_convert_fusion.1
  64.3 0.1 convolution_convert_fusion.1
  64.5 1.1 %collective-permute-start.15 = (bf16[8,16,128]{2,1,0:T(8,128)(2,1)S(1)}, bf16[8,16,128]{2,1,0:T(8,128)(2,1)S(1)}, u32[]{:S(2)}, u32[]{:S(2)}) collective-permute-start(bf16[8,16,128]{2,1,0:T(8,128)(2,1)S(1)} %copy.21), channel_id=1, source_target_pairs={{0,1},{1,0},{2,3},{3,2},{4,5},{5,4},{6,7},{7,6},{8,9},{9,8},{10,11... | collective-permute-start | bytes 98312 | tf_op jit(solution)/shard_map/ppermute | solution.py:61
  65.6 0.1 convolution_convert_fusion
  65.8 2.4 %collective-permute-start.14 = (bf16[8,16,128]{2,1,0:T(8,128)(2,1)S(1)}, bf16[8,16,128]{2,1,0:T(8,128)(2,1)S(1)}, u32[]{:S(2)}, u32[]{:S(2)}) collective-permute-start(bf16[8,16,128]{2,1,0:T(8,128)(2,1)S(1)} %copy.19), channel_id=1, source_target_pairs={{0,33},{1,32},{2,35},{3,34},{4,37},{5,36},{6,39},{7,38},{8,41},{9,... | collective-permute-start | bytes 98312 | tf_op jit(solution)/shard_map/ppermute | solution.py:61
  68.2 0.1 collective-permute-start.16
  68.4 1.6 %collective-permute-done.15 = bf16[8,16,128]{2,1,0:T(8,128)(2,1)S(1)} collective-permute-done((bf16[8,16,128]{2,1,0:T(8,128)(2,1)S(1)}, bf16[8,16,128]{2,1,0:T(8,128)(2,1)S(1)}, u32[]{:S(2)}, u32[]{:S(2)}) %collective-permute-start.15) | collective-permute-done | bytes 32800 | tf_op jit(solution)/shard_map/ppermute | solution.py:61
  70.0 1.0 %collective-permute-done.14 = bf16[8,16,128]{2,1,0:T(8,128)(2,1)S(1)} collective-permute-done((bf16[8,16,128]{2,1,0:T(8,128)(2,1)S(1)}, bf16[8,16,128]{2,1,0:T(8,128)(2,1)S(1)}, u32[]{:S(2)}, u32[]{:S(2)}) %collective-permute-start.14) | collective-permute-done | bytes 32800 | tf_op jit(solution)/shard_map/ppermute | solution.py:61
  71.0 1.1 %collective-permute-done.16 = bf16[8,16,128]{2,1,0:T(8,128)(2,1)S(1)} collective-permute-done((bf16[8,16,128]{2,1,0:T(8,128)(2,1)S(1)}, bf16[8,16,128]{2,1,0:T(8,128)(2,1)S(1)}, u32[]{:S(2)}, u32[]{:S(2)}) %collective-permute-start.16) | collective-permute-done | bytes 32800 | tf_op jit(solution)/shard_map/ppermute | solution.py:61
  72.2 1.6 %collective-permute-start.17 = (bf16[3,16,128]{2,1,0:T(8,128)(2,1)S(1)}, bf16[3,16,128]{2,1,0:T(8,128)(2,1)S(1)}, u32[]{:S(2)}, u32[]{:S(2)}) collective-permute-start(bf16[3,16,128]{2,1,0:T(8,128)(2,1)S(1)} %slice.95), channel_id=1, source_target_pairs={{0,6},{1,7},{2,8},{3,9},{4,10},{5,11},{6,12},{7,13},{8,14},{9,15},... | collective-permute-start | bytes 36872 | tf_op jit(solution)/shard_map/ppermute | solution.py:50
  73.8 3.5 %collective-permute-start.18 = (bf16[2,16,128]{2,1,0:T(8,128)(2,1)S(1)}, bf16[2,16,128]{2,1,0:T(8,128)(2,1)S(1)}, u32[]{:S(2)}, u32[]{:S(2)}) collective-permute-start(bf16[2,16,128]{2,1,0:T(8,128)(2,1)S(1)} %slice.97), channel_id=1, source_target_pairs={{0,10},{1,11},{2,12},{3,13},{4,14},{5,15},{6,0},{7,1},{8,2},{9,3},... | collective-permute-start | bytes 24584 | tf_op jit(solution)/shard_map/ppermute | solution.py:50
  77.3 2.0 %collective-permute-done.18 = bf16[2,16,128]{2,1,0:T(8,128)(2,1)S(1)} collective-permute-done((bf16[2,16,128]{2,1,0:T(8,128)(2,1)S(1)}, bf16[2,16,128]{2,1,0:T(8,128)(2,1)S(1)}, u32[]{:S(2)}, u32[]{:S(2)}) %collective-permute-start.18) | collective-permute-done | bytes 8224 | tf_op jit(solution)/shard_map/ppermute | solution.py:50
  79.3 1.7 %collective-permute-start.19 = (bf16[16,128]{1,0:T(8,128)(2,1)S(1)}, bf16[16,128]{1,0:T(8,128)(2,1)S(1)}, u32[]{:S(2)}, u32[]{:S(2)}) collective-permute-start(bf16[16,128]{1,0:T(8,128)(2,1)S(1)} %get-tuple-element.135), channel_id=1, source_target_pairs={{0,2},{1,3},{2,4},{3,5},{4,6},{5,7},{6,8},{7,9},{8,10},{9,11},{10,... | collective-permute-start | bytes 12296 | tf_op jit(solution)/shard_map/ppermute | solution.py:50
  81.0 2.1 %collective-permute-start.20 = (bf16[16,128]{1,0:T(8,128)(2,1)S(1)}, bf16[16,128]{1,0:T(8,128)(2,1)S(1)}, u32[]{:S(2)}, u32[]{:S(2)}) collective-permute-start(bf16[16,128]{1,0:T(8,128)(2,1)S(1)} %get-tuple-element.136), channel_id=1, source_target_pairs={{0,14},{1,15},{2,0},{3,1},{4,2},{5,3},{6,4},{7,5},{8,6},{9,7},{10,... | collective-permute-start | bytes 12296 | tf_op jit(solution)/shard_map/ppermute | solution.py:50
  83.2 1.5 %collective-permute-done.19 = bf16[16,128]{1,0:T(8,128)(2,1)S(1)} collective-permute-done((bf16[16,128]{1,0:T(8,128)(2,1)S(1)}, bf16[16,128]{1,0:T(8,128)(2,1)S(1)}, u32[]{:S(2)}, u32[]{:S(2)}) %collective-permute-start.19) | collective-permute-done | bytes 4128 | tf_op jit(solution)/shard_map/ppermute | solution.py:50
  84.7 0.6 fusion.7
  (42 shorter events, 0.6 us)
Async XLA Ops:
  2.2 4.4 %collective-permute-start = (bf16[272,128]{1,0:T(8,128)(2,1)S(1)}, bf16[272,128]{1,0:T(8,128)(2,1)S(1)}, u32[]{:S(2)}, u32[]{:S(2)}) collective-permute-start(bf16[272,128]{1,0:T(8,128)(2,1)S(1)} %get-tuple-element.138), channel_id=1, source_target_pairs={{0,32},{16,48},{32,0},{48,16},{64,96},{80,112},{96,64},{112,80},{1... | collective-permute-start | bytes 208904 | tf_op jit(solution)/shard_map/ppermute | solution.py:37
  6.6 9.4 %collective-permute-start.1 = (bf16[2,272,128]{2,1,0:T(8,128)(2,1)S(1)}, bf16[2,272,128]{2,1,0:T(8,128)(2,1)S(1)}, u32[]{:S(2)}, u32[]{:S(2)}) collective-permute-start(bf16[2,272,128]{2,1,0:T(8,128)(2,1)S(1)} %pad_maximum_fusion.q_ref), channel_id=1, source_target_pairs={{0,64},{16,80},{32,96},{48,112},{64,128},{80,144},{96,160},{112,17... | collective-permute-start | bytes 417800 | tf_op jit(solution)/shard_map/ppermute | solution.py:41
  8.2 7.8 %collective-permute-start.2 = (bf16[2,272,128]{2,1,0:T(8,128)(2,1)S(1)}, bf16[2,272,128]{2,1,0:T(8,128)(2,1)S(1)}, u32[]{:S(2)}, u32[]{:S(2)}) collective-permute-start(bf16[2,272,128]{2,1,0:T(8,128)(2,1)S(1)} %pad_maximum_fusion.q_ref), channel_id=1, source_target_pairs={{0,192},{16,208},{32,224},{48,240},{64,0},{80,16},{96,32},{112,48}... | collective-permute-start | bytes 417800 | tf_op jit(solution)/shard_map/ppermute | solution.py:41
  9.1 7.0 %collective-permute-start.3 = (bf16[2,272,128]{2,1,0:T(8,128)(2,1)S(1)}, bf16[2,272,128]{2,1,0:T(8,128)(2,1)S(1)}, u32[]{:S(2)}, u32[]{:S(2)}) collective-permute-start(bf16[2,272,128]{2,1,0:T(8,128)(2,1)S(1)} %pad_maximum_fusion.q_ref), channel_id=1, source_target_pairs={{0,128},{16,144},{32,160},{48,176},{64,192},{80,208},{96,224},{112... | collective-permute-start | bytes 417800 | tf_op jit(solution)/shard_map/ppermute | solution.py:41
  16.1 3.0 %collective-permute-start.4 = (bf16[8,272,128]{2,1,0:T(8,128)(2,1)S(1)}, bf16[8,272,128]{2,1,0:T(8,128)(2,1)S(1)}, u32[]{:S(2)}, u32[]{:S(2)}) collective-permute-start(bf16[8,272,128]{2,1,0:T(8,128)(2,1)S(1)} %constant_dynamic-update-slice_fusion.q_ref.near_ref), channel_id=1, source_target_pairs={{0,16},{16,0},{32,48},{48,32},{64,80},{80,64},{96,112},{112,96},{1... | collective-permute-start | bytes 1671176 | tf_op jit(solution)/shard_map/ppermute | solution.py:37
  19.3 5.9 %collective-permute-start.5 = (f32[8,256]{1,0:T(8,128)S(1)}, f32[8,256]{1,0:T(8,128)S(1)}, u32[]{:S(2)}, u32[]{:S(2)}) collective-permute-start(f32[8,256]{1,0:T(8,128)S(1)} %targets.1.rest_3_.rest_0_), channel_id=1, source_target_pairs={{0,1},{1,0},{2,3},{3,2},{4,5},{5,4},{6,7},{7,6},{8,9},{9,8},{10,11... | collective-permute-start | bytes 24584 | tf_op jit(solution)/shard_map/ppermute | solution.py:37
  25.3 7.6 %collective-permute-start.6 = (f32[2,8,256]{2,1,0:T(8,128)S(1)}, f32[2,8,256]{2,1,0:T(8,128)S(1)}, u32[]{:S(2)}, u32[]{:S(2)}) collective-permute-start(f32[2,8,256]{2,1,0:T(8,128)S(1)} %pad_maximum_fusion.3), channel_id=1, source_target_pairs={{0,2},{1,3},{2,4},{3,5},{4,6},{5,7},{6,8},{7,9},{8,10},{9,11},{10,... | collective-permute-start | bytes 49160 | tf_op jit(solution)/shard_map/ppermute | solution.py:50
  27.2 5.7 %collective-permute-start.7 = (f32[2,8,256]{2,1,0:T(8,128)S(1)}, f32[2,8,256]{2,1,0:T(8,128)S(1)}, u32[]{:S(2)}, u32[]{:S(2)}) collective-permute-start(f32[2,8,256]{2,1,0:T(8,128)S(1)} %pad_maximum_fusion.3), channel_id=1, source_target_pairs={{0,14},{1,15},{2,0},{3,1},{4,2},{5,3},{6,4},{7,5},{8,6},{9,7},{10,... | collective-permute-start | bytes 49160 | tf_op jit(solution)/shard_map/ppermute | solution.py:50
  32.9 8.0 %collective-permute-start.8 = (f32[6,8,256]{2,1,0:T(8,128)S(1)}, f32[6,8,256]{2,1,0:T(8,128)S(1)}, u32[]{:S(2)}, u32[]{:S(2)}) collective-permute-start(f32[6,8,256]{2,1,0:T(8,128)S(1)} %pad_maximum_fusion.2.rest_0_), channel_id=1, source_target_pairs={{0,6},{1,7},{2,8},{3,9},{4,10},{5,11},{6,12},{7,13},{8,14},{9,15},... | collective-permute-start | bytes 147464 | tf_op jit(solution)/shard_map/ppermute | solution.py:50
  38.0 7.0 %collective-permute-start.9 = (f32[6,8,256]{2,1,0:T(8,128)S(1)}, f32[6,8,256]{2,1,0:T(8,128)S(1)}, u32[]{:S(2)}, u32[]{:S(2)}) collective-permute-start(f32[6,8,256]{2,1,0:T(8,128)S(1)} %pad_maximum_fusion.2.rest_0_), channel_id=1, source_target_pairs={{0,10},{1,11},{2,12},{3,13},{4,14},{5,15},{6,0},{7,1},{8,2},{9,3},... | collective-permute-start | bytes 147464 | tf_op jit(solution)/shard_map/ppermute | solution.py:50
  50.0 3.9 %collective-permute-start.10 = (bf16[8,256,128]{2,1,0:T(8,128)(2,1)S(1)}, bf16[8,256,128]{2,1,0:T(8,128)(2,1)S(1)}, u32[]{:S(2)}, u32[]{:S(2)}) collective-permute-start(bf16[8,256,128]{2,1,0:T(8,128)(2,1)S(1)} %get-tuple-element.120), channel_id=1, source_target_pairs={{0,16},{16,0},{32,48},{48,32},{64,80},{80,64},{96,112},{112,96},{1... | collective-permute-start | bytes 1572872 | tf_op jit(solution)/shard_map/ppermute | solution.py:37
  50.1 10.5 %copy-start = (bf16[1024,128]{1,0:T(8,128)(2,1)S(1)}, bf16[1024,128]{1,0:T(8,128)(2,1)}, u32[]{:S(2)}) copy-start(bf16[1024,128]{1,0:T(8,128)(2,1)} %w_ref.2) | copy-start | bytes 786436
  54.0 10.1 %collective-permute-start.11 = (bf16[2,256,128]{2,1,0:T(8,128)(2,1)S(1)}, bf16[2,256,128]{2,1,0:T(8,128)(2,1)S(1)}, u32[]{:S(2)}, u32[]{:S(2)}) collective-permute-start(bf16[2,256,128]{2,1,0:T(8,128)(2,1)S(1)} %get-tuple-element.132), channel_id=1, source_target_pairs={{0,192},{16,208},{32,224},{48,240},{64,0},{80,16},{96,32},{112,48}... | collective-permute-start | bytes 393224 | tf_op jit(solution)/shard_map/ppermute | solution.py:41
  55.5 8.7 %collective-permute-start.12 = (bf16[2,256,128]{2,1,0:T(8,128)(2,1)S(1)}, bf16[2,256,128]{2,1,0:T(8,128)(2,1)S(1)}, u32[]{:S(2)}, u32[]{:S(2)}) collective-permute-start(bf16[2,256,128]{2,1,0:T(8,128)(2,1)S(1)} %get-tuple-element.131), channel_id=1, source_target_pairs={{0,64},{16,80},{32,96},{48,112},{64,128},{80,144},{96,160},{112,17... | collective-permute-start | bytes 393224 | tf_op jit(solution)/shard_map/ppermute | solution.py:41
  56.1 8.0 %collective-permute-start.13 = (bf16[2,256,128]{2,1,0:T(8,128)(2,1)S(1)}, bf16[2,256,128]{2,1,0:T(8,128)(2,1)S(1)}, u32[]{:S(2)}, u32[]{:S(2)}) collective-permute-start(bf16[2,256,128]{2,1,0:T(8,128)(2,1)S(1)} %get-tuple-element.130), channel_id=1, source_target_pairs={{0,128},{16,144},{32,160},{48,176},{64,192},{80,208},{96,224},{112... | collective-permute-start | bytes 393224 | tf_op jit(solution)/shard_map/ppermute | solution.py:41
  64.5 5.5 %collective-permute-start.15 = (bf16[8,16,128]{2,1,0:T(8,128)(2,1)S(1)}, bf16[8,16,128]{2,1,0:T(8,128)(2,1)S(1)}, u32[]{:S(2)}, u32[]{:S(2)}) collective-permute-start(bf16[8,16,128]{2,1,0:T(8,128)(2,1)S(1)} %copy.21), channel_id=1, source_target_pairs={{0,1},{1,0},{2,3},{3,2},{4,5},{5,4},{6,7},{7,6},{8,9},{9,8},{10,11... | collective-permute-start | bytes 98312 | tf_op jit(solution)/shard_map/ppermute | solution.py:61
  65.8 5.2 %collective-permute-start.14 = (bf16[8,16,128]{2,1,0:T(8,128)(2,1)S(1)}, bf16[8,16,128]{2,1,0:T(8,128)(2,1)S(1)}, u32[]{:S(2)}, u32[]{:S(2)}) collective-permute-start(bf16[8,16,128]{2,1,0:T(8,128)(2,1)S(1)} %copy.19), channel_id=1, source_target_pairs={{0,33},{1,32},{2,35},{3,34},{4,37},{5,36},{6,39},{7,38},{8,41},{9,... | collective-permute-start | bytes 98312 | tf_op jit(solution)/shard_map/ppermute | solution.py:61
  68.2 3.9 %collective-permute-start.16 = (bf16[8,16,128]{2,1,0:T(8,128)(2,1)S(1)}, bf16[8,16,128]{2,1,0:T(8,128)(2,1)S(1)}, u32[]{:S(2)}, u32[]{:S(2)}) collective-permute-start(bf16[8,16,128]{2,1,0:T(8,128)(2,1)S(1)} %copy.22), channel_id=1, source_target_pairs={{0,32},{1,33},{2,34},{3,35},{4,36},{5,37},{6,38},{7,39},{8,40},{9,... | collective-permute-start | bytes 98312 | tf_op jit(solution)/shard_map/ppermute | solution.py:61
  72.2 7.1 %collective-permute-start.17 = (bf16[3,16,128]{2,1,0:T(8,128)(2,1)S(1)}, bf16[3,16,128]{2,1,0:T(8,128)(2,1)S(1)}, u32[]{:S(2)}, u32[]{:S(2)}) collective-permute-start(bf16[3,16,128]{2,1,0:T(8,128)(2,1)S(1)} %slice.95), channel_id=1, source_target_pairs={{0,6},{1,7},{2,8},{3,9},{4,10},{5,11},{6,12},{7,13},{8,14},{9,15},... | collective-permute-start | bytes 36872 | tf_op jit(solution)/shard_map/ppermute | solution.py:50
  73.8 5.5 %collective-permute-start.18 = (bf16[2,16,128]{2,1,0:T(8,128)(2,1)S(1)}, bf16[2,16,128]{2,1,0:T(8,128)(2,1)S(1)}, u32[]{:S(2)}, u32[]{:S(2)}) collective-permute-start(bf16[2,16,128]{2,1,0:T(8,128)(2,1)S(1)} %slice.97), channel_id=1, source_target_pairs={{0,10},{1,11},{2,12},{3,13},{4,14},{5,15},{6,0},{7,1},{8,2},{9,3},... | collective-permute-start | bytes 24584 | tf_op jit(solution)/shard_map/ppermute | solution.py:50
  79.3 5.4 %collective-permute-start.19 = (bf16[16,128]{1,0:T(8,128)(2,1)S(1)}, bf16[16,128]{1,0:T(8,128)(2,1)S(1)}, u32[]{:S(2)}, u32[]{:S(2)}) collective-permute-start(bf16[16,128]{1,0:T(8,128)(2,1)S(1)} %get-tuple-element.135), channel_id=1, source_target_pairs={{0,2},{1,3},{2,4},{3,5},{4,6},{5,7},{6,8},{7,9},{8,10},{9,11},{10,... | collective-permute-start | bytes 12296 | tf_op jit(solution)/shard_map/ppermute | solution.py:50
  81.0 3.6 %collective-permute-start.20 = (bf16[16,128]{1,0:T(8,128)(2,1)S(1)}, bf16[16,128]{1,0:T(8,128)(2,1)S(1)}, u32[]{:S(2)}, u32[]{:S(2)}) collective-permute-start(bf16[16,128]{1,0:T(8,128)(2,1)S(1)} %get-tuple-element.136), channel_id=1, source_target_pairs={{0,14},{1,15},{2,0},{3,1},{4,2},{5,3},{6,4},{7,5},{8,6},{9,7},{10,... | collective-permute-start | bytes 12296 | tf_op jit(solution)/shard_map/ppermute | solution.py:50

commit v5 on v4

--- a/solution.py
+++ b/solution.py
@@ -89,6 +89,26 @@
     near_down = (blocks[2] + up[2]).astype(bf16)
     up_one, down_one = shift_z(near_up, 1), shift_z(near_down, -1)
     return blocks[0] + up[0] + down[0] + up_one.astype(f32) + down_one.astype(f32)
+
+
+def join_kernel(query_ref, first_ref, second_ref, out_ref):
+    out_ref[:GR, :] = query_ref[...]
+    ranks = jnp.concatenate([first_ref[...], second_ref[...]])
+    out_ref[GR:, :] = ranks.astype(f32).astype(bf16)
+
+
+def join(queries, bm25_rank, dense_rank):
+    return pl.pallas_call(
+        join_kernel,
+        out_shape=jax.ShapeDtypeStruct((GR + 2 * GQ, DIM), bf16),
+        compiler_params=pltpu.CompilerParams(vmem_limit_bytes=2 * 2**20),
+        name="join",
+    )(
+        *(
+            pltpu.with_memory_space_constraint(x, pltpu.HBM)
+            for x in (queries, bm25_rank, dense_rank)
+        )
+    )
 
 
 def project_kernel(hid_ref, w_ref, proj_ref, emb_ref, emb_t_ref):
@@ -350,8 +370,7 @@
     place = jnp.where(slot_ids >= 0, place, -1)
     rows = jnp.arange(18 * PD, dtype=jnp.int32).reshape(3, 1, 6 * PD)
     pick = (place[None, :, None] == rows).astype(f32)
-    ranks = jnp.concatenate([bm25_rank[:, 0, :], dense_rank[:, 0, :]]).astype(bf16)
-    mine = jnp.concatenate([queries, ranks])
+    mine = join(queries, bm25_rank[:, 0, :], dense_rank[:, 0, :])
     other = swap(mine, "pb", 2)
     first_row, order = (me_pb * PD).reshape(1), order_of(me_pa)
     other, late_weight, pick, order, first_row = lax.optimization_barrier(

time: 86.4 us -> 85.6 us (level)
  other arithmetic: 4.11 us -> 1.71 us
  Pallas kernels: 28.7 us -> 29.6 us
    pallas_call x0 -> x1, Pallas kernels: none -> 0.87 us  [join(): pl.pallas_call(join_kernel, out_shape=jax.ShapeDtypeStruct((GR + 2 * GQ,...]
  transfers between devices with their start and end apart: 21 -> 21, of which waited for: 8 -> 8; matrix products, arithmetic and copies ran while one was open for 2% -> 1% of each run, Pallas kernels for 28% -> 28%
where the time goes in v5:
time: 85.6 us; the launch traced here: 84.5 us
  starting transfers between devices  38.2 us (45%)
  Pallas kernels  29.6 us (35%)
  waiting for transfers between devices  13.5 us (16%)
  other arithmetic  1.71 us (2%)
  between operations  0.95 us (1%)
    ppermute x8, starting transfers between devices, shift_z(): lax.ppermute(value, 'pa', [(i, ((i >> 1) + by) % 8 << 1 | i & 1) for i in...  20.1 us
    pallas_call x6, Pallas kernels, forward(): pl.pallas_call(forward_kernel, grid=(count,), in_specs=[pl.BlockSpec((1,...  11.4 us
    pallas_call x3, Pallas kernels, backward(): pl.pallas_call(functools.partial(backward_kernel, first, half, start), gr...  10.1 us
    ppermute x6, starting transfers between devices, shift_x(): lax.ppermute(value, 'pb', [(i, ((i >> 2) + by) % 4 << 2 | i & 3) for i in...  9.61 us
    ppermute x8, waiting for transfers between devices, shift_z(): lax.ppermute(value, 'pa', [(i, ((i >> 1) + by) % 8 << 1 | i & 1) for i in...  7.83 us
    ppermute x4, starting transfers between devices, swap(): return lax.ppermute(value, axis, [(i, i ^ mask) for i in range(16)])  4.79 us
    ppermute x3, waiting for transfers between devices, swap_y(): return lax.ppermute(value, ('pb', 'pa'), pairs)  3.77 us
    ppermute x3, starting transfers between devices, swap_y(): return lax.ppermute(value, ('pb', 'pa'), pairs)  3.66 us
  transfers between devices with their start and end apart: 21, of which 8 were waited for; matrix products, arithmetic and copies ran while one was open for 1% of the time, Pallas kernels for 28%

profile of v5, /device:TPU:2, one launch (start us, length us, event | category | flops | bytes accessed | tf_op | source)
XLA Modules:
  0.0 84.5 jit_solution(3834747361585526214)
XLA Ops:
  0.6 0.9 %join.1 = bf16[272,128]{1,0:T(8,128)(2,1)S(1)} custom-call(bf16[256,128]{1,0:T(8,128)(2,1)} %query_ref.1, s32[8,128]{1,0:T(8,128)} %bitcast.48, s32[8,128]{1,0:T(8,128)} %bitcast.49), custom_call_target="tpu_custom_call" | custom-call | tf_op jit(solution)/shard_map/join/pallas_call | solution.py:101
  1.5 1.6 %collective-permute-start = (bf16[272,128]{1,0:T(8,128)(2,1)S(1)}, bf16[272,128]{1,0:T(8,128)(2,1)S(1)}, u32[]{:S(2)}, u32[]{:S(2)}) collective-permute-start(bf16[272,128]{1,0:T(8,128)(2,1)S(1)} %join.1), channel_id=1, source_target_pairs={{0,32},{16,48},{32,0},{48,16},{64,96},{80,112},{96,64},{112,80},{1... | collective-permute-start | bytes 208904 | tf_op jit(solution)/shard_map/ppermute | solution.py:37
  3.1 0.7 bitcast_select_fusion
  3.8 0.1 compare_convert_fusion.pick_ref
  3.9 1.9 %collective-permute-done = bf16[272,128]{1,0:T(8,128)(2,1)S(1)} collective-permute-done((bf16[272,128]{1,0:T(8,128)(2,1)S(1)}, bf16[272,128]{1,0:T(8,128)(2,1)S(1)}, u32[]{:S(2)}, u32[]{:S(2)}) %collective-permute-start) | collective-permute-done | bytes 69664 | tf_op jit(solution)/shard_map/ppermute | solution.py:37
  5.8 1.6 %collective-permute-start.1 = (bf16[2,272,128]{2,1,0:T(8,128)(2,1)S(1)}, bf16[2,272,128]{2,1,0:T(8,128)(2,1)S(1)}, u32[]{:S(2)}, u32[]{:S(2)}) collective-permute-start(bf16[2,272,128]{2,1,0:T(8,128)(2,1)S(1)} %pad_maximum_fusion.q_ref), channel_id=1, source_target_pairs={{0,64},{16,80},{32,96},{48,112},{64,128},{80,144},{96,160},{112,17... | collective-permute-start | bytes 417800 | tf_op jit(solution)/shard_map/ppermute | solution.py:41
  7.4 0.9 %collective-permute-start.2 = (bf16[2,272,128]{2,1,0:T(8,128)(2,1)S(1)}, bf16[2,272,128]{2,1,0:T(8,128)(2,1)S(1)}, u32[]{:S(2)}, u32[]{:S(2)}) collective-permute-start(bf16[2,272,128]{2,1,0:T(8,128)(2,1)S(1)} %pad_maximum_fusion.q_ref), channel_id=1, source_target_pairs={{0,192},{16,208},{32,224},{48,240},{64,0},{80,16},{96,32},{112,48}... | collective-permute-start | bytes 417800 | tf_op jit(solution)/shard_map/ppermute | solution.py:41
  8.3 2.0 %collective-permute-start.3 = (bf16[2,272,128]{2,1,0:T(8,128)(2,1)S(1)}, bf16[2,272,128]{2,1,0:T(8,128)(2,1)S(1)}, u32[]{:S(2)}, u32[]{:S(2)}) collective-permute-start(bf16[2,272,128]{2,1,0:T(8,128)(2,1)S(1)} %pad_maximum_fusion.q_ref), channel_id=1, source_target_pairs={{0,128},{16,144},{32,160},{48,176},{64,192},{80,208},{96,224},{112... | collective-permute-start | bytes 417800 | tf_op jit(solution)/shard_map/ppermute | solution.py:41
  10.2 3.5 %project.1 = (f32[2048,128]{1,0:T(8,128)S(1)}, bf16[2048,128]{1,0:T(8,128)(2,1)S(1)}, bf16[128,2048]{1,0:T(8,128)(2,1)S(1)}) custom-call(bf16[2048,1024]{1,0:T(8,128)(2,1)} %bitcast.43, bf16[1024,128]{1,0:T(8,128)(2,1)} %w_ref.2), custom_call_target="tpu_custom_call" | custom-call | flops 536870912 | bytes 6291456 | tf_op jit(solution)/shard_map/project/pallas_call | solution.py:125
  13.8 1.4 %forward.6 = (bf16[2,2048,256]{2,1,0:T(8,128)(2,1)S(1)}, f32[2,16,256]{2,1,0:T(8,128)S(1)}, f32[2,16,256]{2,1,0:T(8,128)S(1)}) custom-call(bf16[2,272,128]{2,1,0:T(8,128)(2,1)S(1)} %pad_maximum_fusion.q_ref, bf16[2048,128]{1,0:T(8,128)(2,1)S(1)} %get-tuple-element.68.emb_ref), custom_call_target="tpu_custom_call" | custom-call | flops 67108864 | bytes 524288 | tf_op jit(solution)/shard_map/forward/pallas_call | solution.py:183
  15.3 0.1 collective-permute-start.4
  15.4 2.9 %forward.7 = (bf16[6,2048,256]{2,1,0:T(8,128)(2,1)S(1)}, f32[6,16,256]{2,1,0:T(8,128)S(1)}, f32[6,16,256]{2,1,0:T(8,128)S(1)}) custom-call(bf16[8,272,128]{2,1,0:T(8,128)(2,1)S(1)} %constant_dynamic-update-slice_fusion.q_ref.near_ref, bf16[2048,128]{1,0:T(8,128)(2,1)S(1)} %get-tuple-element.68.emb_ref), custom_call_target="tpu_custom_call" | custom-call | flops 134217728 | bytes 1048576 | tf_op jit(solution)/shard_map/forward/pallas_call | solution.py:183
  18.3 0.2 targets.1.rest_3_.rest_0_
  18.5 3.0 %collective-permute-start.5 = (f32[8,256]{1,0:T(8,128)S(1)}, f32[8,256]{1,0:T(8,128)S(1)}, u32[]{:S(2)}, u32[]{:S(2)}) collective-permute-start(f32[8,256]{1,0:T(8,128)S(1)} %targets.1.rest_3_.rest_0_), channel_id=1, source_target_pairs={{0,1},{1,0},{2,3},{3,2},{4,5},{5,4},{6,7},{7,6},{8,9},{9,8},{10,11... | collective-permute-start | bytes 24584 | tf_op jit(solution)/shard_map/ppermute | solution.py:37
  21.6 1.4 %forward.9 = (bf16[8,2048,256]{2,1,0:T(8,128)(2,1)S(1)}, f32[8,16,256]{2,1,0:T(8,128)S(1)}, f32[8,16,256]{2,1,0:T(8,128)S(1)}) custom-call(bf16[8,272,128]{2,1,0:T(8,128)(2,1)S(1)} %collective-permute-done.4.far_ref.q_ref, bf16[2048,128]{1,0:T(8,128)(2,1)S(1)} %get-tuple-element.68.emb_ref, f32[8,256]{1,0:T(8,128)S(1)} %targets.1.rest_3_.rest_0_), custom_call_target="tpu_custom_call" | custom-call | flops 67108864 | bytes 524288 | tf_op jit(solution)/shard_map/forward/pallas_call | solution.py:183
  23.0 1.4 %forward.8 = (bf16[6,2048,256]{2,1,0:T(8,128)(2,1)S(1)}, f32[6,16,256]{2,1,0:T(8,128)S(1)}, f32[6,16,256]{2,1,0:T(8,128)S(1)}) custom-call(bf16[8,272,128]{2,1,0:T(8,128)(2,1)S(1)} %constant_dynamic-update-slice_fusion.q_ref.near_ref, bf16[2048,128]{1,0:T(8,128)(2,1)S(1)} %get-tuple-element.68.emb_ref, ...), custom_call_target="tpu_custom_call", output_to_operand_aliasing={{0}: (2, {}), {1}: (3, {}), {2}: (4, {})} | custom-call | flops 67108864 | bytes 524288 | tf_op jit(solution)/shard_map/forward/pallas_call | solution.py:183
  24.5 2.0 %collective-permute-start.6 = (f32[2,8,256]{2,1,0:T(8,128)S(1)}, f32[2,8,256]{2,1,0:T(8,128)S(1)}, u32[]{:S(2)}, u32[]{:S(2)}) collective-permute-start(f32[2,8,256]{2,1,0:T(8,128)S(1)} %pad_maximum_fusion.2), channel_id=1, source_target_pairs={{0,2},{1,3},{2,4},{3,5},{4,6},{5,7},{6,8},{7,9},{8,10},{9,11},{10,... | collective-permute-start | bytes 49160 | tf_op jit(solution)/shard_map/ppermute | solution.py:50
  26.4 4.0 %collective-permute-start.7 = (f32[2,8,256]{2,1,0:T(8,128)S(1)}, f32[2,8,256]{2,1,0:T(8,128)S(1)}, u32[]{:S(2)}, u32[]{:S(2)}) collective-permute-start(f32[2,8,256]{2,1,0:T(8,128)S(1)} %pad_maximum_fusion.2), channel_id=1, source_target_pairs={{0,14},{1,15},{2,0},{3,1},{4,2},{5,3},{6,4},{7,5},{8,6},{9,7},{10,... | collective-permute-start | bytes 49160 | tf_op jit(solution)/shard_map/ppermute | solution.py:50
  30.5 1.4 %forward.10 = (bf16[8,2048,256]{2,1,0:T(8,128)(2,1)S(1)}, f32[8,16,256]{2,1,0:T(8,128)S(1)}, f32[8,16,256]{2,1,0:T(8,128)S(1)}) custom-call(bf16[8,272,128]{2,1,0:T(8,128)(2,1)S(1)} %collective-permute-done.4.far_ref.q_ref, bf16[2048,128]{1,0:T(8,128)(2,1)S(1)} %get-tuple-element.68.emb_ref, ...), custom_call_target="tpu_custom_call", output_to_operand_aliasing={{0}: (2, {}), {1}: (3, {}), {2}: (4, {})} | custom-call | flops 67108864 | bytes 524288 | tf_op jit(solution)/shard_map/forward/pallas_call | solution.py:183
  31.9 0.2 collective-permute-done.6
  32.1 5.1 %collective-permute-start.8 = (f32[6,8,256]{2,1,0:T(8,128)S(1)}, f32[6,8,256]{2,1,0:T(8,128)S(1)}, u32[]{:S(2)}, u32[]{:S(2)}) collective-permute-start(f32[6,8,256]{2,1,0:T(8,128)S(1)} %pad_maximum_fusion.1.rest_0_), channel_id=1, source_target_pairs={{0,6},{1,7},{2,8},{3,9},{4,10},{5,11},{6,12},{7,13},{8,14},{9,15},... | collective-permute-start | bytes 147464 | tf_op jit(solution)/shard_map/ppermute | solution.py:50
  37.2 2.8 %forward.11 = (bf16[8,2048,256]{2,1,0:T(8,128)(2,1)S(1)}, f32[8,16,256]{2,1,0:T(8,128)S(1)}, f32[8,16,256]{2,1,0:T(8,128)S(1)}) custom-call(bf16[8,272,128]{2,1,0:T(8,128)(2,1)S(1)} %collective-permute-done.4.far_ref.q_ref, bf16[2048,128]{1,0:T(8,128)(2,1)S(1)} %get-tuple-element.68.emb_ref, ...), custom_call_target="tpu_custom_call", output_to_operand_aliasing={{0}: (2, {}), {1}: (3, {}), {2}: (4, {})} | custom-call | flops 134217728 | bytes 1048576 | tf_op jit(solution)/shard_map/forward/pallas_call | solution.py:183
  40.1 4.2 %collective-permute-done.9.rest_2_ = f32[6,8,256]{2,1,0:T(8,128)S(1)} collective-permute-done((f32[6,8,256]{2,1,0:T(8,128)S(1)}, f32[6,8,256]{2,1,0:T(8,128)S(1)}, u32[]{:S(2)}, u32[]{:S(2)}) %collective-permute-start.9) | collective-permute-done | bytes 49184 | tf_op jit(solution)/shard_map/ppermute | solution.py:50
  44.3 4.9 %backward.3 = (bf16[8,256,128]{2,1,0:T(8,128)(2,1)S(1)}, f32[2048,128]{1,0:T(8,128)S(1)}) custom-call(bf16[8,272,128]{2,1,0:T(8,128)(2,1)S(1)} %collective-permute-done.4.far_ref.q_ref, bf16[8,2048,256]{2,1,0:T(8,128)(2,1)S(1)} %get-tuple-element.114.p_ref, f32[8,16,256]{2,1,0:T(8,128)S(1)} %get-tuple-element.115.lse_ref, ...), custom_call_target="tpu_custom_call" | custom-call | flops 2147483648 | bytes 8388608 | tf_op jit(solution)/shard_map/backward/pallas_call | solution.py:276
  49.2 0.1 collective-permute-start.10
  49.3 3.8 %backward.4 = (bf16[6,256,128]{2,1,0:T(8,128)(2,1)S(1)}, f32[2048,128]{1,0:T(8,128)S(1)}) custom-call(bf16[8,272,128]{2,1,0:T(8,128)(2,1)S(1)} %constant_dynamic-update-slice_fusion.q_ref.near_ref, bf16[6,2048,256]{2,1,0:T(8,128)(2,1)S(1)} %get-tuple-element.111.p_ref, f32[6,16,256]{2,1,0:T(8,128)S(1)} %get-tuple-element.112.lse_ref, ...), custom_call_target="tpu_custom_call" | custom-call | flops 1610612736 | bytes 6291456 | tf_op jit(solution)/shard_map/backward/pallas_call | solution.py:276
  53.1 0.1 add_convert_fusion
  53.2 1.5 %collective-permute-start.11 = (bf16[2,256,128]{2,1,0:T(8,128)(2,1)S(1)}, bf16[2,256,128]{2,1,0:T(8,128)(2,1)S(1)}, u32[]{:S(2)}, u32[]{:S(2)}) collective-permute-start(bf16[2,256,128]{2,1,0:T(8,128)(2,1)S(1)} %get-tuple-element.132), channel_id=1, source_target_pairs={{0,192},{16,208},{32,224},{48,240},{64,0},{80,16},{96,32},{112,48}... | collective-permute-start | bytes 393224 | tf_op jit(solution)/shard_map/ppermute | solution.py:41
  54.8 0.6 collective-permute-start.12
  55.3 3.1 %collective-permute-start.13 = (bf16[2,256,128]{2,1,0:T(8,128)(2,1)S(1)}, bf16[2,256,128]{2,1,0:T(8,128)(2,1)S(1)}, u32[]{:S(2)}, u32[]{:S(2)}) collective-permute-start(bf16[2,256,128]{2,1,0:T(8,128)(2,1)S(1)} %get-tuple-element.130), channel_id=1, source_target_pairs={{0,128},{16,144},{32,160},{48,176},{64,192},{80,208},{96,224},{112... | collective-permute-start | bytes 393224 | tf_op jit(solution)/shard_map/ppermute | solution.py:41
  58.4 1.4 %backward.5 = (bf16[2,256,128]{2,1,0:T(8,128)(2,1)S(1)}, f32[2048,128]{1,0:T(8,128)S(1)}) custom-call(bf16[2,272,128]{2,1,0:T(8,128)(2,1)S(1)} %pad_maximum_fusion.q_ref, bf16[2,2048,256]{2,1,0:T(8,128)(2,1)S(1)} %get-tuple-element.72.p_ref, f32[2,16,256]{2,1,0:T(8,128)S(1)} %get-tuple-element.73.lse_ref, f32[2,16,256]{2,1,0:T(8,128)S(1)} %get-tuple-element.74.total_ref, ...), custom_call_target="tpu_custom_call" | custom-call | flops 536870912 | bytes 2097152 | tf_op jit(solution)/shard_map/backward/pallas_call | solution.py:276
  59.8 3.6 %hidden_gradient.1 = bf16[2048,1024]{1,0:T(8,128)(2,1)} custom-call(f32[2048,128]{1,0:T(8,128)S(1)} %get-tuple-element.122.eg_ref, f32[2048,128]{1,0:T(8,128)S(1)} %get-tuple-element.123.proj_ref, bf16[1024,128]{1,0:T(8,128)(2,1)S(1)} %copy-done), custom_call_target="tpu_custom_call" | custom-call | flops 536870912 | bytes 6291456 | tf_op jit(solution)/shard_map/hidden_gradient/pallas_call | solution.py:314
  63.4 0.1 add_convert_fusion.1
  63.6 0.1 convolution_convert_fusion.1
  63.7 1.1 %collective-permute-start.15 = (bf16[8,16,128]{2,1,0:T(8,128)(2,1)S(1)}, bf16[8,16,128]{2,1,0:T(8,128)(2,1)S(1)}, u32[]{:S(2)}, u32[]{:S(2)}) collective-permute-start(bf16[8,16,128]{2,1,0:T(8,128)(2,1)S(1)} %copy.19), channel_id=1, source_target_pairs={{0,1},{1,0},{2,3},{3,2},{4,5},{5,4},{6,7},{7,6},{8,9},{9,8},{10,11... | collective-permute-start | bytes 98312 | tf_op jit(solution)/shard_map/ppermute | solution.py:61
  64.9 0.1 convolution_convert_fusion
  65.0 2.4 %collective-permute-start.14 = (bf16[8,16,128]{2,1,0:T(8,128)(2,1)S(1)}, bf16[8,16,128]{2,1,0:T(8,128)(2,1)S(1)}, u32[]{:S(2)}, u32[]{:S(2)}) collective-permute-start(bf16[8,16,128]{2,1,0:T(8,128)(2,1)S(1)} %copy.17), channel_id=1, source_target_pairs={{0,33},{1,32},{2,35},{3,34},{4,37},{5,36},{6,39},{7,38},{8,41},{9,... | collective-permute-start | bytes 98312 | tf_op jit(solution)/shard_map/ppermute | solution.py:61
  67.5 0.1 collective-permute-start.16
  67.6 1.6 %collective-permute-done.15 = bf16[8,16,128]{2,1,0:T(8,128)(2,1)S(1)} collective-permute-done((bf16[8,16,128]{2,1,0:T(8,128)(2,1)S(1)}, bf16[8,16,128]{2,1,0:T(8,128)(2,1)S(1)}, u32[]{:S(2)}, u32[]{:S(2)}) %collective-permute-start.15) | collective-permute-done | bytes 32800 | tf_op jit(solution)/shard_map/ppermute | solution.py:61
  69.2 1.0 %collective-permute-done.14 = bf16[8,16,128]{2,1,0:T(8,128)(2,1)S(1)} collective-permute-done((bf16[8,16,128]{2,1,0:T(8,128)(2,1)S(1)}, bf16[8,16,128]{2,1,0:T(8,128)(2,1)S(1)}, u32[]{:S(2)}, u32[]{:S(2)}) %collective-permute-start.14) | collective-permute-done | bytes 32800 | tf_op jit(solution)/shard_map/ppermute | solution.py:61
  70.2 1.1 %collective-permute-done.16 = bf16[8,16,128]{2,1,0:T(8,128)(2,1)S(1)} collective-permute-done((bf16[8,16,128]{2,1,0:T(8,128)(2,1)S(1)}, bf16[8,16,128]{2,1,0:T(8,128)(2,1)S(1)}, u32[]{:S(2)}, u32[]{:S(2)}) %collective-permute-start.16) | collective-permute-done | bytes 32800 | tf_op jit(solution)/shard_map/ppermute | solution.py:61
  71.4 1.6 %collective-permute-start.17 = (bf16[3,16,128]{2,1,0:T(8,128)(2,1)S(1)}, bf16[3,16,128]{2,1,0:T(8,128)(2,1)S(1)}, u32[]{:S(2)}, u32[]{:S(2)}) collective-permute-start(bf16[3,16,128]{2,1,0:T(8,128)(2,1)S(1)} %slice.95), channel_id=1, source_target_pairs={{0,6},{1,7},{2,8},{3,9},{4,10},{5,11},{6,12},{7,13},{8,14},{9,15},... | collective-permute-start | bytes 36872 | tf_op jit(solution)/shard_map/ppermute | solution.py:50
  73.0 3.5 %collective-permute-start.18 = (bf16[2,16,128]{2,1,0:T(8,128)(2,1)S(1)}, bf16[2,16,128]{2,1,0:T(8,128)(2,1)S(1)}, u32[]{:S(2)}, u32[]{:S(2)}) collective-permute-start(bf16[2,16,128]{2,1,0:T(8,128)(2,1)S(1)} %slice.97), channel_id=1, source_target_pairs={{0,10},{1,11},{2,12},{3,13},{4,14},{5,15},{6,0},{7,1},{8,2},{9,3},... | collective-permute-start | bytes 24584 | tf_op jit(solution)/shard_map/ppermute | solution.py:50
  76.5 1.9 %collective-permute-done.18 = bf16[2,16,128]{2,1,0:T(8,128)(2,1)S(1)} collective-permute-done((bf16[2,16,128]{2,1,0:T(8,128)(2,1)S(1)}, bf16[2,16,128]{2,1,0:T(8,128)(2,1)S(1)}, u32[]{:S(2)}, u32[]{:S(2)}) %collective-permute-start.18) | collective-permute-done | bytes 8224 | tf_op jit(solution)/shard_map/ppermute | solution.py:50
  78.5 1.7 %collective-permute-start.19 = (bf16[16,128]{1,0:T(8,128)(2,1)S(1)}, bf16[16,128]{1,0:T(8,128)(2,1)S(1)}, u32[]{:S(2)}, u32[]{:S(2)}) collective-permute-start(bf16[16,128]{1,0:T(8,128)(2,1)S(1)} %get-tuple-element.135), channel_id=1, source_target_pairs={{0,2},{1,3},{2,4},{3,5},{4,6},{5,7},{6,8},{7,9},{8,10},{9,11},{10,... | collective-permute-start | bytes 12296 | tf_op jit(solution)/shard_map/ppermute | solution.py:50
  80.2 2.2 %collective-permute-start.20 = (bf16[16,128]{1,0:T(8,128)(2,1)S(1)}, bf16[16,128]{1,0:T(8,128)(2,1)S(1)}, u32[]{:S(2)}, u32[]{:S(2)}) collective-permute-start(bf16[16,128]{1,0:T(8,128)(2,1)S(1)} %get-tuple-element.136), channel_id=1, source_target_pairs={{0,14},{1,15},{2,0},{3,1},{4,2},{5,3},{6,4},{7,5},{8,6},{9,7},{10,... | collective-permute-start | bytes 12296 | tf_op jit(solution)/shard_map/ppermute | solution.py:50
  82.4 1.5 %collective-permute-done.19 = bf16[16,128]{1,0:T(8,128)(2,1)S(1)} collective-permute-done((bf16[16,128]{1,0:T(8,128)(2,1)S(1)}, bf16[16,128]{1,0:T(8,128)(2,1)S(1)}, u32[]{:S(2)}, u32[]{:S(2)}) %collective-permute-start.19) | collective-permute-done | bytes 4128 | tf_op jit(solution)/shard_map/ppermute | solution.py:50
  83.9 0.6 fusion.7
  (41 shorter events, 0.4 us)
Async XLA Ops:
  1.5 4.3 %collective-permute-start = (bf16[272,128]{1,0:T(8,128)(2,1)S(1)}, bf16[272,128]{1,0:T(8,128)(2,1)S(1)}, u32[]{:S(2)}, u32[]{:S(2)}) collective-permute-start(bf16[272,128]{1,0:T(8,128)(2,1)S(1)} %join.1), channel_id=1, source_target_pairs={{0,32},{16,48},{32,0},{48,16},{64,96},{80,112},{96,64},{112,80},{1... | collective-permute-start | bytes 208904 | tf_op jit(solution)/shard_map/ppermute | solution.py:37
  5.8 9.4 %collective-permute-start.1 = (bf16[2,272,128]{2,1,0:T(8,128)(2,1)S(1)}, bf16[2,272,128]{2,1,0:T(8,128)(2,1)S(1)}, u32[]{:S(2)}, u32[]{:S(2)}) collective-permute-start(bf16[2,272,128]{2,1,0:T(8,128)(2,1)S(1)} %pad_maximum_fusion.q_ref), channel_id=1, source_target_pairs={{0,64},{16,80},{32,96},{48,112},{64,128},{80,144},{96,160},{112,17... | collective-permute-start | bytes 417800 | tf_op jit(solution)/shard_map/ppermute | solution.py:41
  7.4 7.8 %collective-permute-start.2 = (bf16[2,272,128]{2,1,0:T(8,128)(2,1)S(1)}, bf16[2,272,128]{2,1,0:T(8,128)(2,1)S(1)}, u32[]{:S(2)}, u32[]{:S(2)}) collective-permute-start(bf16[2,272,128]{2,1,0:T(8,128)(2,1)S(1)} %pad_maximum_fusion.q_ref), channel_id=1, source_target_pairs={{0,192},{16,208},{32,224},{48,240},{64,0},{80,16},{96,32},{112,48}... | collective-permute-start | bytes 417800 | tf_op jit(solution)/shard_map/ppermute | solution.py:41
  8.3 7.0 %collective-permute-start.3 = (bf16[2,272,128]{2,1,0:T(8,128)(2,1)S(1)}, bf16[2,272,128]{2,1,0:T(8,128)(2,1)S(1)}, u32[]{:S(2)}, u32[]{:S(2)}) collective-permute-start(bf16[2,272,128]{2,1,0:T(8,128)(2,1)S(1)} %pad_maximum_fusion.q_ref), channel_id=1, source_target_pairs={{0,128},{16,144},{32,160},{48,176},{64,192},{80,208},{96,224},{112... | collective-permute-start | bytes 417800 | tf_op jit(solution)/shard_map/ppermute | solution.py:41
  15.3 3.0 %collective-permute-start.4 = (bf16[8,272,128]{2,1,0:T(8,128)(2,1)S(1)}, bf16[8,272,128]{2,1,0:T(8,128)(2,1)S(1)}, u32[]{:S(2)}, u32[]{:S(2)}) collective-permute-start(bf16[8,272,128]{2,1,0:T(8,128)(2,1)S(1)} %constant_dynamic-update-slice_fusion.q_ref.near_ref), channel_id=1, source_target_pairs={{0,16},{16,0},{32,48},{48,32},{64,80},{80,64},{96,112},{112,96},{1... | collective-permute-start | bytes 1671176 | tf_op jit(solution)/shard_map/ppermute | solution.py:37
  18.5 5.9 %collective-permute-start.5 = (f32[8,256]{1,0:T(8,128)S(1)}, f32[8,256]{1,0:T(8,128)S(1)}, u32[]{:S(2)}, u32[]{:S(2)}) collective-permute-start(f32[8,256]{1,0:T(8,128)S(1)} %targets.1.rest_3_.rest_0_), channel_id=1, source_target_pairs={{0,1},{1,0},{2,3},{3,2},{4,5},{5,4},{6,7},{7,6},{8,9},{9,8},{10,11... | collective-permute-start | bytes 24584 | tf_op jit(solution)/shard_map/ppermute | solution.py:37
  24.5 7.6 %collective-permute-start.6 = (f32[2,8,256]{2,1,0:T(8,128)S(1)}, f32[2,8,256]{2,1,0:T(8,128)S(1)}, u32[]{:S(2)}, u32[]{:S(2)}) collective-permute-start(f32[2,8,256]{2,1,0:T(8,128)S(1)} %pad_maximum_fusion.2), channel_id=1, source_target_pairs={{0,2},{1,3},{2,4},{3,5},{4,6},{5,7},{6,8},{7,9},{8,10},{9,11},{10,... | collective-permute-start | bytes 49160 | tf_op jit(solution)/shard_map/ppermute | solution.py:50
  26.4 5.7 %collective-permute-start.7 = (f32[2,8,256]{2,1,0:T(8,128)S(1)}, f32[2,8,256]{2,1,0:T(8,128)S(1)}, u32[]{:S(2)}, u32[]{:S(2)}) collective-permute-start(f32[2,8,256]{2,1,0:T(8,128)S(1)} %pad_maximum_fusion.2), channel_id=1, source_target_pairs={{0,14},{1,15},{2,0},{3,1},{4,2},{5,3},{6,4},{7,5},{8,6},{9,7},{10,... | collective-permute-start | bytes 49160 | tf_op jit(solution)/shard_map/ppermute | solution.py:50
  32.1 8.0 %collective-permute-start.8 = (f32[6,8,256]{2,1,0:T(8,128)S(1)}, f32[6,8,256]{2,1,0:T(8,128)S(1)}, u32[]{:S(2)}, u32[]{:S(2)}) collective-permute-start(f32[6,8,256]{2,1,0:T(8,128)S(1)} %pad_maximum_fusion.1.rest_0_), channel_id=1, source_target_pairs={{0,6},{1,7},{2,8},{3,9},{4,10},{5,11},{6,12},{7,13},{8,14},{9,15},... | collective-permute-start | bytes 147464 | tf_op jit(solution)/shard_map/ppermute | solution.py:50
  37.2 7.1 %collective-permute-start.9 = (f32[6,8,256]{2,1,0:T(8,128)S(1)}, f32[6,8,256]{2,1,0:T(8,128)S(1)}, u32[]{:S(2)}, u32[]{:S(2)}) collective-permute-start(f32[6,8,256]{2,1,0:T(8,128)S(1)} %pad_maximum_fusion.1.rest_0_), channel_id=1, source_target_pairs={{0,10},{1,11},{2,12},{3,13},{4,14},{5,15},{6,0},{7,1},{8,2},{9,3},... | collective-permute-start | bytes 147464 | tf_op jit(solution)/shard_map/ppermute | solution.py:50
  49.2 3.9 %collective-permute-start.10 = (bf16[8,256,128]{2,1,0:T(8,128)(2,1)S(1)}, bf16[8,256,128]{2,1,0:T(8,128)(2,1)S(1)}, u32[]{:S(2)}, u32[]{:S(2)}) collective-permute-start(bf16[8,256,128]{2,1,0:T(8,128)(2,1)S(1)} %get-tuple-element.120), channel_id=1, source_target_pairs={{0,16},{16,0},{32,48},{48,32},{64,80},{80,64},{96,112},{112,96},{1... | collective-permute-start | bytes 1572872 | tf_op jit(solution)/shard_map/ppermute | solution.py:37
  49.3 10.5 %copy-start = (bf16[1024,128]{1,0:T(8,128)(2,1)S(1)}, bf16[1024,128]{1,0:T(8,128)(2,1)}, u32[]{:S(2)}) copy-start(bf16[1024,128]{1,0:T(8,128)(2,1)} %w_ref.2) | copy-start | bytes 786436
  53.2 10.2 %collective-permute-start.11 = (bf16[2,256,128]{2,1,0:T(8,128)(2,1)S(1)}, bf16[2,256,128]{2,1,0:T(8,128)(2,1)S(1)}, u32[]{:S(2)}, u32[]{:S(2)}) collective-permute-start(bf16[2,256,128]{2,1,0:T(8,128)(2,1)S(1)} %get-tuple-element.132), channel_id=1, source_target_pairs={{0,192},{16,208},{32,224},{48,240},{64,0},{80,16},{96,32},{112,48}... | collective-permute-start | bytes 393224 | tf_op jit(solution)/shard_map/ppermute | solution.py:41
  54.8 8.6 %collective-permute-start.12 = (bf16[2,256,128]{2,1,0:T(8,128)(2,1)S(1)}, bf16[2,256,128]{2,1,0:T(8,128)(2,1)S(1)}, u32[]{:S(2)}, u32[]{:S(2)}) collective-permute-start(bf16[2,256,128]{2,1,0:T(8,128)(2,1)S(1)} %get-tuple-element.131), channel_id=1, source_target_pairs={{0,64},{16,80},{32,96},{48,112},{64,128},{80,144},{96,160},{112,17... | collective-permute-start | bytes 393224 | tf_op jit(solution)/shard_map/ppermute | solution.py:41
  55.3 8.1 %collective-permute-start.13 = (bf16[2,256,128]{2,1,0:T(8,128)(2,1)S(1)}, bf16[2,256,128]{2,1,0:T(8,128)(2,1)S(1)}, u32[]{:S(2)}, u32[]{:S(2)}) collective-permute-start(bf16[2,256,128]{2,1,0:T(8,128)(2,1)S(1)} %get-tuple-element.130), channel_id=1, source_target_pairs={{0,128},{16,144},{32,160},{48,176},{64,192},{80,208},{96,224},{112... | collective-permute-start | bytes 393224 | tf_op jit(solution)/shard_map/ppermute | solution.py:41
  63.7 5.5 %collective-permute-start.15 = (bf16[8,16,128]{2,1,0:T(8,128)(2,1)S(1)}, bf16[8,16,128]{2,1,0:T(8,128)(2,1)S(1)}, u32[]{:S(2)}, u32[]{:S(2)}) collective-permute-start(bf16[8,16,128]{2,1,0:T(8,128)(2,1)S(1)} %copy.19), channel_id=1, source_target_pairs={{0,1},{1,0},{2,3},{3,2},{4,5},{5,4},{6,7},{7,6},{8,9},{9,8},{10,11... | collective-permute-start | bytes 98312 | tf_op jit(solution)/shard_map/ppermute | solution.py:61
  65.0 5.2 %collective-permute-start.14 = (bf16[8,16,128]{2,1,0:T(8,128)(2,1)S(1)}, bf16[8,16,128]{2,1,0:T(8,128)(2,1)S(1)}, u32[]{:S(2)}, u32[]{:S(2)}) collective-permute-start(bf16[8,16,128]{2,1,0:T(8,128)(2,1)S(1)} %copy.17), channel_id=1, source_target_pairs={{0,33},{1,32},{2,35},{3,34},{4,37},{5,36},{6,39},{7,38},{8,41},{9,... | collective-permute-start | bytes 98312 | tf_op jit(solution)/shard_map/ppermute | solution.py:61
  67.5 3.9 %collective-permute-start.16 = (bf16[8,16,128]{2,1,0:T(8,128)(2,1)S(1)}, bf16[8,16,128]{2,1,0:T(8,128)(2,1)S(1)}, u32[]{:S(2)}, u32[]{:S(2)}) collective-permute-start(bf16[8,16,128]{2,1,0:T(8,128)(2,1)S(1)} %copy.20), channel_id=1, source_target_pairs={{0,32},{1,33},{2,34},{3,35},{4,36},{5,37},{6,38},{7,39},{8,40},{9,... | collective-permute-start | bytes 98312 | tf_op jit(solution)/shard_map/ppermute | solution.py:61
  71.4 7.1 %collective-permute-start.17 = (bf16[3,16,128]{2,1,0:T(8,128)(2,1)S(1)}, bf16[3,16,128]{2,1,0:T(8,128)(2,1)S(1)}, u32[]{:S(2)}, u32[]{:S(2)}) collective-permute-start(bf16[3,16,128]{2,1,0:T(8,128)(2,1)S(1)} %slice.95), channel_id=1, source_target_pairs={{0,6},{1,7},{2,8},{3,9},{4,10},{5,11},{6,12},{7,13},{8,14},{9,15},... | collective-permute-start | bytes 36872 | tf_op jit(solution)/shard_map/ppermute | solution.py:50
  73.0 5.5 %collective-permute-start.18 = (bf16[2,16,128]{2,1,0:T(8,128)(2,1)S(1)}, bf16[2,16,128]{2,1,0:T(8,128)(2,1)S(1)}, u32[]{:S(2)}, u32[]{:S(2)}) collective-permute-start(bf16[2,16,128]{2,1,0:T(8,128)(2,1)S(1)} %slice.97), channel_id=1, source_target_pairs={{0,10},{1,11},{2,12},{3,13},{4,14},{5,15},{6,0},{7,1},{8,2},{9,3},... | collective-permute-start | bytes 24584 | tf_op jit(solution)/shard_map/ppermute | solution.py:50
  78.5 5.4 %collective-permute-start.19 = (bf16[16,128]{1,0:T(8,128)(2,1)S(1)}, bf16[16,128]{1,0:T(8,128)(2,1)S(1)}, u32[]{:S(2)}, u32[]{:S(2)}) collective-permute-start(bf16[16,128]{1,0:T(8,128)(2,1)S(1)} %get-tuple-element.135), channel_id=1, source_target_pairs={{0,2},{1,3},{2,4},{3,5},{4,6},{5,7},{6,8},{7,9},{8,10},{9,11},{10,... | collective-permute-start | bytes 12296 | tf_op jit(solution)/shard_map/ppermute | solution.py:50
  80.2 3.7 %collective-permute-start.20 = (bf16[16,128]{1,0:T(8,128)(2,1)S(1)}, bf16[16,128]{1,0:T(8,128)(2,1)S(1)}, u32[]{:S(2)}, u32[]{:S(2)}) collective-permute-start(bf16[16,128]{1,0:T(8,128)(2,1)S(1)} %get-tuple-element.136), channel_id=1, source_target_pairs={{0,14},{1,15},{2,0},{3,1},{4,2},{5,3},{6,4},{7,5},{8,6},{9,7},{10,... | collective-permute-start | bytes 12296 | tf_op jit(solution)/shard_map/ppermute | solution.py:50

commit v6 on v5

--- a/solution.py
+++ b/solution.py
@@ -111,7 +111,8 @@
     )
 
 
-def project_kernel(hid_ref, w_ref, proj_ref, emb_ref, emb_t_ref):
+def project_kernel(hid_ref, w_ref, *rest):
+    proj_ref, emb_ref, emb_t_ref = rest[-3:]
     proj = lax.dot_general(hid_ref[...], w_ref[...], NN, preferred_element_type=f32)
     scaling = lax.rsqrt(jnp.sum(proj * proj, axis=-1, keepdims=True) + norm_eps)
     unit = proj * scaling
@@ -120,31 +121,33 @@
     emb_t_ref[...] = unit.T.astype(bf16)
 
 
-def project(hid, weight):
-    step = 1024
+def project(hid, weight, half, made=(), after=()):
+    step = ROWS // 2
     return pl.pallas_call(
         project_kernel,
-        grid=(ROWS // step,),
+        grid=(1,),
         in_specs=[
-            pl.BlockSpec((step, H), lambda i: (i, 0)),
+            pl.BlockSpec((step, H), lambda i: (half, 0)),
             pl.BlockSpec((H, DIM), lambda i: (0, 0)),
-        ],
+        ]
+        + [pl.BlockSpec(memory_space=pl.ANY)] * (len(made) + len(after)),
         out_specs=[
-            pl.BlockSpec((step, DIM), lambda i: (i, 0)),
-            pl.BlockSpec((step, DIM), lambda i: (i, 0)),
-            pl.BlockSpec((DIM, step), lambda i: (0, i)),
+            pl.BlockSpec((step, DIM), lambda i: (half, 0)),
+            pl.BlockSpec((step, DIM), lambda i: (half, 0)),
+            pl.BlockSpec((DIM, step), lambda i: (0, half)),
         ],
         out_shape=[
             jax.ShapeDtypeStruct((ROWS, DIM), f32),
             jax.ShapeDtypeStruct((ROWS, DIM), bf16),
             jax.ShapeDtypeStruct((DIM, ROWS), bf16),
         ],
+        input_output_aliases={2 + i: i for i in range(len(made))},
         compiler_params=pltpu.CompilerParams(vmem_limit_bytes=12 * 2**20),
         cost_estimate=pl.CostEstimate(
-            flops=2 * ROWS * H * DIM, bytes_accessed=ROWS * (2 * H + 8 * DIM), transcendentals=0
+            flops=ROWS * H * DIM // 4, bytes_accessed=ROWS * H // 4, transcendentals=0
         ),
         name="project",
-    )(*(pltpu.with_memory_space_constraint(x, pltpu.HBM) for x in (hid, weight)))
+    )(*(pltpu.with_memory_space_constraint(x, pltpu.HBM) for x in (hid, weight)), *made, *after)
 
 
 def token_sums(value):
@@ -373,11 +376,11 @@
     mine = join(queries, bm25_rank[:, 0, :], dense_rank[:, 0, :])
     other = swap(mine, "pb", 2)
     first_row, order = (me_pb * PD).reshape(1), order_of(me_pa)
-    other, late_weight, pick, order, first_row = lax.optimization_barrier(
-        (other, proj_weight, pick, order, first_row)
-    )
-    proj, emb, emb_t = project(encoder_outputs.reshape(ROWS, H), late_weight)
+    hid = encoder_outputs.reshape(ROWS, H)
+    made = project(hid, proj_weight, 0, after=[mine])
+    other, pick, order, first_row = lax.optimization_barrier((other, pick, order, first_row))
     pair = jnp.stack([mine, other])
+    proj, emb, emb_t = project(hid, proj_weight, 1, made, [pair])
     got = [shift_x(pair, by) for by in SHIFTS[1:]]
     kept_d = forward(pair, 0, 2, emb, 0, 2)
     got, kept_d = lax.optimization_barrier((got, kept_d))

time: 85.6 us -> 86.8 us (1.014)
  Pallas kernels: 29.6 us -> 31.3 us
    ppermute x4, waiting for transfers between devices: 1.9 us -> 0.01 us  [swap(): return lax.ppermute(value, axis, [(i, i ^ mask) for i in range(16)])]
    ppermute x6, waiting for transfers between devices: 0.02 us -> 1.8 us  [shift_x(): lax.ppermute(value, 'pb', [(i, ((i >> 2) + by) % 4 << 2 | i & 3) for i in...]
    pallas_call x1 -> x2, Pallas kernels: 3.5 us -> 5.03 us  [project(): pl.pallas_call(project_kernel, grid=(1,), in_specs=[pl.BlockSpec((step, H...]
  transfers between devices with their start and end apart: 21 -> 21, of which waited for: 8 -> 9; matrix products, arithmetic and copies ran while one was open for 1% -> 1% of each run, Pallas kernels for 28% -> 30%
where the time goes in v6:
time: 86.8 us; the launch traced here: 85.6 us
  starting transfers between devices  37.7 us (43%)
  Pallas kernels  31.3 us (36%)
  waiting for transfers between devices  13.5 us (16%)
  other arithmetic  1.71 us (2%)
  between operations  0.95 us (1%)
    ppermute x8, starting transfers between devices, shift_z(): lax.ppermute(value, 'pa', [(i, ((i >> 1) + by) % 8 << 1 | i & 1) for i in...  19.9 us
    pallas_call x6, Pallas kernels, forward(): pl.pallas_call(forward_kernel, grid=(count,), in_specs=[pl.BlockSpec((1,...  11.5 us
    pallas_call x3, Pallas kernels, backward(): pl.pallas_call(functools.partial(backward_kernel, first, half, start), gr...  10.1 us
    ppermute x6, starting transfers between devices, shift_x(): lax.ppermute(value, 'pb', [(i, ((i >> 2) + by) % 4 << 2 | i & 3) for i in...  9.4 us
    ppermute x8, waiting for transfers between devices, shift_z(): lax.ppermute(value, 'pa', [(i, ((i >> 1) + by) % 8 << 1 | i & 1) for i in...  8.4 us
    pallas_call x2, Pallas kernels, project(): pl.pallas_call(project_kernel, grid=(1,), in_specs=[pl.BlockSpec((step, H...  5.03 us
    ppermute x4, starting transfers between devices, swap(): return lax.ppermute(value, axis, [(i, i ^ mask) for i in range(16)])  4.69 us
    ppermute x3, starting transfers between devices, swap_y(): return lax.ppermute(value, ('pb', 'pa'), pairs)  3.66 us
  transfers between devices with their start and end apart: 21, of which 9 were waited for; matrix products, arithmetic and copies ran while one was open for 1% of the time, Pallas kernels for 30%

profile of v6, /device:TPU:2, one launch (start us, length us, event | category | flops | bytes accessed | tf_op | source)
XLA Modules:
  0.0 85.6 jit_solution(680344493709271280)
XLA Ops:
  0.6 0.9 %join.1.rest_0_ = bf16[272,128]{1,0:T(8,128)(2,1)S(1)} custom-call(bf16[256,128]{1,0:T(8,128)(2,1)} %query_ref.1, s32[8,128]{1,0:T(8,128)} %bitcast.49, s32[8,128]{1,0:T(8,128)} %bitcast.50), custom_call_target="tpu_custom_call" | custom-call | tf_op jit(solution)/shard_map/join/pallas_call | solution.py:101
  1.5 1.6 %collective-permute-start = (bf16[272,128]{1,0:T(8,128)(2,1)S(1)}, bf16[272,128]{1,0:T(8,128)(2,1)S(1)}, u32[]{:S(2)}, u32[]{:S(2)}) collective-permute-start(bf16[272,128]{1,0:T(8,128)(2,1)S(1)} %join.1.rest_0_), channel_id=1, source_target_pairs={{0,32},{16,48},{32,0},{48,16},{64,96},{80,112},{96,64},{112,80},{1... | collective-permute-start | bytes 208904 | tf_op jit(solution)/shard_map/ppermute | solution.py:37
  3.1 0.7 bitcast_select_fusion
  3.9 2.5 %project.2 = (f32[2048,128]{1,0:T(8,128)S(1)}, bf16[2048,128]{1,0:T(8,128)(2,1)S(1)}, bf16[128,2048]{1,0:T(8,128)(2,1)S(1)}) custom-call(bf16[2048,1024]{1,0:T(8,128)(2,1)} %bitcast.43, bf16[1024,128]{1,0:T(8,128)(2,1)} %w_ref.5, bf16[272,128]{1,0:T(8,128)(2,1)S(1)} %join.1.rest_0_), custom_call_target="tpu_custom_call" | custom-call | flops 67108864 | bytes 524288 | tf_op jit(solution)/shard_map/project/pallas_call | solution.py:126
  6.5 1.6 %collective-permute-start.1 = (bf16[2,272,128]{2,1,0:T(8,128)(2,1)S(1)}, bf16[2,272,128]{2,1,0:T(8,128)(2,1)S(1)}, u32[]{:S(2)}, u32[]{:S(2)}) collective-permute-start(bf16[2,272,128]{2,1,0:T(8,128)(2,1)S(1)} %pad_maximum_fusion.rest_3_.q_ref), channel_id=1, source_target_pairs={{0,64},{16,80},{32,96},{48,112},{64,128},{80,144},{96,160},{112,17... | collective-permute-start | bytes 417800 | tf_op jit(solution)/shard_map/ppermute | solution.py:41
  8.0 0.5 collective-permute-start.2
  8.6 2.1 %collective-permute-start.3 = (bf16[2,272,128]{2,1,0:T(8,128)(2,1)S(1)}, bf16[2,272,128]{2,1,0:T(8,128)(2,1)S(1)}, u32[]{:S(2)}, u32[]{:S(2)}) collective-permute-start(bf16[2,272,128]{2,1,0:T(8,128)(2,1)S(1)} %pad_maximum_fusion.rest_3_.q_ref), channel_id=1, source_target_pairs={{0,128},{16,144},{32,160},{48,176},{64,192},{80,208},{96,224},{112... | collective-permute-start | bytes 417800 | tf_op jit(solution)/shard_map/ppermute | solution.py:41
  10.7 2.5 %project.3 = (f32[2048,128]{1,0:T(8,128)S(1)}, bf16[2048,128]{1,0:T(8,128)(2,1)S(1)}, bf16[128,2048]{1,0:T(8,128)(2,1)S(1)}) custom-call(bf16[2048,1024]{1,0:T(8,128)(2,1)} %bitcast.44, bf16[1024,128]{1,0:T(8,128)(2,1)} %w_ref.5, f32[2048,128]{1,0:T(8,128)S(1)} %get-tuple-element.69.rest_0_, ...), custom_call_target="tpu_custom_call", output_to_operand_aliasing={{0}: (2, {}), {1}: (3, {}), {2}: (4, {})} | custom-call | flops 67108864 | bytes 524288 | tf_op jit(solution)/shard_map/project/pallas_call | solution.py:126
  13.2 1.4 %forward.6 = (bf16[2,2048,256]{2,1,0:T(8,128)(2,1)S(1)}, f32[2,16,256]{2,1,0:T(8,128)S(1)}, f32[2,16,256]{2,1,0:T(8,128)S(1)}) custom-call(bf16[2,272,128]{2,1,0:T(8,128)(2,1)S(1)} %pad_maximum_fusion.rest_3_.q_ref, bf16[2048,128]{1,0:T(8,128)(2,1)S(1)} %get-tuple-element.72.emb_ref), custom_call_target="tpu_custom_call" | custom-call | flops 67108864 | bytes 524288 | tf_op jit(solution)/shard_map/forward/pallas_call | solution.py:186
  14.7 1.8 %collective-permute-done.3 = bf16[2,272,128]{2,1,0:T(8,128)(2,1)S(1)} collective-permute-done((bf16[2,272,128]{2,1,0:T(8,128)(2,1)S(1)}, bf16[2,272,128]{2,1,0:T(8,128)(2,1)S(1)}, u32[]{:S(2)}, u32[]{:S(2)}) %collective-permute-start.3) | collective-permute-done | bytes 139296 | tf_op jit(solution)/shard_map/ppermute | solution.py:41
  16.6 0.1 collective-permute-start.4
  16.7 2.9 %forward.7 = (bf16[6,2048,256]{2,1,0:T(8,128)(2,1)S(1)}, f32[6,16,256]{2,1,0:T(8,128)S(1)}, f32[6,16,256]{2,1,0:T(8,128)S(1)}) custom-call(bf16[8,272,128]{2,1,0:T(8,128)(2,1)S(1)} %constant_dynamic-update-slice_fusion.q_ref.near_ref, bf16[2048,128]{1,0:T(8,128)(2,1)S(1)} %get-tuple-element.72.emb_ref), custom_call_target="tpu_custom_call" | custom-call | flops 134217728 | bytes 1048576 | tf_op jit(solution)/shard_map/forward/pallas_call | solution.py:186
  19.6 0.2 targets.1.rest_3_.rest_0_
  19.8 2.9 %collective-permute-start.5 = (f32[8,256]{1,0:T(8,128)S(1)}, f32[8,256]{1,0:T(8,128)S(1)}, u32[]{:S(2)}, u32[]{:S(2)}) collective-permute-start(f32[8,256]{1,0:T(8,128)S(1)} %targets.1.rest_3_.rest_0_), channel_id=1, source_target_pairs={{0,1},{1,0},{2,3},{3,2},{4,5},{5,4},{6,7},{7,6},{8,9},{9,8},{10,11... | collective-permute-start | bytes 24584 | tf_op jit(solution)/shard_map/ppermute | solution.py:37
  22.7 1.4 %forward.9 = (bf16[8,2048,256]{2,1,0:T(8,128)(2,1)S(1)}, f32[8,16,256]{2,1,0:T(8,128)S(1)}, f32[8,16,256]{2,1,0:T(8,128)S(1)}) custom-call(bf16[8,272,128]{2,1,0:T(8,128)(2,1)S(1)} %collective-permute-done.4.far_ref.q_ref, bf16[2048,128]{1,0:T(8,128)(2,1)S(1)} %get-tuple-element.72.emb_ref, f32[8,256]{1,0:T(8,128)S(1)} %targets.1.rest_3_.rest_0_), custom_call_target="tpu_custom_call" | custom-call | flops 67108864 | bytes 524288 | tf_op jit(solution)/shard_map/forward/pallas_call | solution.py:186
  24.2 1.5 %forward.8 = (bf16[6,2048,256]{2,1,0:T(8,128)(2,1)S(1)}, f32[6,16,256]{2,1,0:T(8,128)S(1)}, f32[6,16,256]{2,1,0:T(8,128)S(1)}) custom-call(bf16[8,272,128]{2,1,0:T(8,128)(2,1)S(1)} %constant_dynamic-update-slice_fusion.q_ref.near_ref, bf16[2048,128]{1,0:T(8,128)(2,1)S(1)} %get-tuple-element.72.emb_ref, ...), custom_call_target="tpu_custom_call", output_to_operand_aliasing={{0}: (2, {}), {1}: (3, {}), {2}: (4, {})} | custom-call | flops 67108864 | bytes 524288 | tf_op jit(solution)/shard_map/forward/pallas_call | solution.py:186
  25.6 2.0 %collective-permute-start.6 = (f32[2,8,256]{2,1,0:T(8,128)S(1)}, f32[2,8,256]{2,1,0:T(8,128)S(1)}, u32[]{:S(2)}, u32[]{:S(2)}) collective-permute-start(f32[2,8,256]{2,1,0:T(8,128)S(1)} %pad_maximum_fusion.2), channel_id=1, source_target_pairs={{0,2},{1,3},{2,4},{3,5},{4,6},{5,7},{6,8},{7,9},{8,10},{9,11},{10,... | collective-permute-start | bytes 49160 | tf_op jit(solution)/shard_map/ppermute | solution.py:50
  27.6 4.0 %collective-permute-start.7 = (f32[2,8,256]{2,1,0:T(8,128)S(1)}, f32[2,8,256]{2,1,0:T(8,128)S(1)}, u32[]{:S(2)}, u32[]{:S(2)}) collective-permute-start(f32[2,8,256]{2,1,0:T(8,128)S(1)} %pad_maximum_fusion.2), channel_id=1, source_target_pairs={{0,14},{1,15},{2,0},{3,1},{4,2},{5,3},{6,4},{7,5},{8,6},{9,7},{10,... | collective-permute-start | bytes 49160 | tf_op jit(solution)/shard_map/ppermute | solution.py:50
  31.7 1.4 %forward.10 = (bf16[8,2048,256]{2,1,0:T(8,128)(2,1)S(1)}, f32[8,16,256]{2,1,0:T(8,128)S(1)}, f32[8,16,256]{2,1,0:T(8,128)S(1)}) custom-call(bf16[8,272,128]{2,1,0:T(8,128)(2,1)S(1)} %collective-permute-done.4.far_ref.q_ref, bf16[2048,128]{1,0:T(8,128)(2,1)S(1)} %get-tuple-element.72.emb_ref, ...), custom_call_target="tpu_custom_call", output_to_operand_aliasing={{0}: (2, {}), {1}: (3, {}), {2}: (4, {})} | custom-call | flops 67108864 | bytes 524288 | tf_op jit(solution)/shard_map/forward/pallas_call | solution.py:186
  33.1 0.2 collective-permute-done.6
  33.3 5.1 %collective-permute-start.8 = (f32[6,8,256]{2,1,0:T(8,128)S(1)}, f32[6,8,256]{2,1,0:T(8,128)S(1)}, u32[]{:S(2)}, u32[]{:S(2)}) collective-permute-start(f32[6,8,256]{2,1,0:T(8,128)S(1)} %pad_maximum_fusion.1.rest_0_), channel_id=1, source_target_pairs={{0,6},{1,7},{2,8},{3,9},{4,10},{5,11},{6,12},{7,13},{8,14},{9,15},... | collective-permute-start | bytes 147464 | tf_op jit(solution)/shard_map/ppermute | solution.py:50
  38.4 2.9 %forward.11 = (bf16[8,2048,256]{2,1,0:T(8,128)(2,1)S(1)}, f32[8,16,256]{2,1,0:T(8,128)S(1)}, f32[8,16,256]{2,1,0:T(8,128)S(1)}) custom-call(bf16[8,272,128]{2,1,0:T(8,128)(2,1)S(1)} %collective-permute-done.4.far_ref.q_ref, bf16[2048,128]{1,0:T(8,128)(2,1)S(1)} %get-tuple-element.72.emb_ref, ...), custom_call_target="tpu_custom_call", output_to_operand_aliasing={{0}: (2, {}), {1}: (3, {}), {2}: (4, {})} | custom-call | flops 134217728 | bytes 1048576 | tf_op jit(solution)/shard_map/forward/pallas_call | solution.py:186
  41.3 4.2 %collective-permute-done.9.rest_2_ = f32[6,8,256]{2,1,0:T(8,128)S(1)} collective-permute-done((f32[6,8,256]{2,1,0:T(8,128)S(1)}, f32[6,8,256]{2,1,0:T(8,128)S(1)}, u32[]{:S(2)}, u32[]{:S(2)}) %collective-permute-start.9) | collective-permute-done | bytes 49184 | tf_op jit(solution)/shard_map/ppermute | solution.py:50
  45.5 4.9 %backward.3 = (bf16[8,256,128]{2,1,0:T(8,128)(2,1)S(1)}, f32[2048,128]{1,0:T(8,128)S(1)}) custom-call(bf16[8,272,128]{2,1,0:T(8,128)(2,1)S(1)} %collective-permute-done.4.far_ref.q_ref, bf16[8,2048,256]{2,1,0:T(8,128)(2,1)S(1)} %get-tuple-element.118.p_ref, f32[8,16,256]{2,1,0:T(8,128)S(1)} %get-tuple-element.119.lse_ref, ...), custom_call_target="tpu_custom_call" | custom-call | flops 2147483648 | bytes 8388608 | tf_op jit(solution)/shard_map/backward/pallas_call | solution.py:279
  50.5 3.8 %backward.4 = (bf16[6,256,128]{2,1,0:T(8,128)(2,1)S(1)}, f32[2048,128]{1,0:T(8,128)S(1)}) custom-call(bf16[8,272,128]{2,1,0:T(8,128)(2,1)S(1)} %constant_dynamic-update-slice_fusion.q_ref.near_ref, bf16[6,2048,256]{2,1,0:T(8,128)(2,1)S(1)} %get-tuple-element.115.p_ref, f32[6,16,256]{2,1,0:T(8,128)S(1)} %get-tuple-element.116.lse_ref, ...), custom_call_target="tpu_custom_call" | custom-call | flops 1610612736 | bytes 6291456 | tf_op jit(solution)/shard_map/backward/pallas_call | solution.py:279
  54.3 0.1 add_convert_fusion
  54.5 0.9 %collective-permute-start.11 = (bf16[2,256,128]{2,1,0:T(8,128)(2,1)S(1)}, bf16[2,256,128]{2,1,0:T(8,128)(2,1)S(1)}, u32[]{:S(2)}, u32[]{:S(2)}) collective-permute-start(bf16[2,256,128]{2,1,0:T(8,128)(2,1)S(1)} %get-tuple-element.136), channel_id=1, source_target_pairs={{0,192},{16,208},{32,224},{48,240},{64,0},{80,16},{96,32},{112,48}... | collective-permute-start | bytes 393224 | tf_op jit(solution)/shard_map/ppermute | solution.py:41
  55.4 1.2 %collective-permute-start.12 = (bf16[2,256,128]{2,1,0:T(8,128)(2,1)S(1)}, bf16[2,256,128]{2,1,0:T(8,128)(2,1)S(1)}, u32[]{:S(2)}, u32[]{:S(2)}) collective-permute-start(bf16[2,256,128]{2,1,0:T(8,128)(2,1)S(1)} %get-tuple-element.135), channel_id=1, source_target_pairs={{0,64},{16,80},{32,96},{48,112},{64,128},{80,144},{96,160},{112,17... | collective-permute-start | bytes 393224 | tf_op jit(solution)/shard_map/ppermute | solution.py:41
  56.6 3.1 %collective-permute-start.13 = (bf16[2,256,128]{2,1,0:T(8,128)(2,1)S(1)}, bf16[2,256,128]{2,1,0:T(8,128)(2,1)S(1)}, u32[]{:S(2)}, u32[]{:S(2)}) collective-permute-start(bf16[2,256,128]{2,1,0:T(8,128)(2,1)S(1)} %get-tuple-element.134), channel_id=1, source_target_pairs={{0,128},{16,144},{32,160},{48,176},{64,192},{80,208},{96,224},{112... | collective-permute-start | bytes 393224 | tf_op jit(solution)/shard_map/ppermute | solution.py:41
  59.6 1.4 %backward.5 = (bf16[2,256,128]{2,1,0:T(8,128)(2,1)S(1)}, f32[2048,128]{1,0:T(8,128)S(1)}) custom-call(bf16[2,272,128]{2,1,0:T(8,128)(2,1)S(1)} %pad_maximum_fusion.rest_3_.q_ref, bf16[2,2048,256]{2,1,0:T(8,128)(2,1)S(1)} %get-tuple-element.76.p_ref, f32[2,16,256]{2,1,0:T(8,128)S(1)} %get-tuple-element.77.lse_ref, ...), custom_call_target="tpu_custom_call" | custom-call | flops 536870912 | bytes 2097152 | tf_op jit(solution)/shard_map/backward/pallas_call | solution.py:279
  61.0 3.6 %hidden_gradient.1 = bf16[2048,1024]{1,0:T(8,128)(2,1)} custom-call(f32[2048,128]{1,0:T(8,128)S(1)} %get-tuple-element.126.eg_ref, f32[2048,128]{1,0:T(8,128)S(1)} %get-tuple-element.127.proj_ref, bf16[1024,128]{1,0:T(8,128)(2,1)S(1)} %copy-done), custom_call_target="tpu_custom_call" | custom-call | flops 536870912 | bytes 6291456 | tf_op jit(solution)/shard_map/hidden_gradient/pallas_call | solution.py:317
  64.6 0.1 add_convert_fusion.1
  64.8 0.1 convolution_convert_fusion.1
  65.0 1.1 %collective-permute-start.15 = (bf16[8,16,128]{2,1,0:T(8,128)(2,1)S(1)}, bf16[8,16,128]{2,1,0:T(8,128)(2,1)S(1)}, u32[]{:S(2)}, u32[]{:S(2)}) collective-permute-start(bf16[8,16,128]{2,1,0:T(8,128)(2,1)S(1)} %copy.22), channel_id=1, source_target_pairs={{0,1},{1,0},{2,3},{3,2},{4,5},{5,4},{6,7},{7,6},{8,9},{9,8},{10,11... | collective-permute-start | bytes 98312 | tf_op jit(solution)/shard_map/ppermute | solution.py:61
  66.0 0.1 convolution_convert_fusion
  66.2 2.0 %collective-permute-start.14 = (bf16[8,16,128]{2,1,0:T(8,128)(2,1)S(1)}, bf16[8,16,128]{2,1,0:T(8,128)(2,1)S(1)}, u32[]{:S(2)}, u32[]{:S(2)}) collective-permute-start(bf16[8,16,128]{2,1,0:T(8,128)(2,1)S(1)} %copy.20), channel_id=1, source_target_pairs={{0,33},{1,32},{2,35},{3,34},{4,37},{5,36},{6,39},{7,38},{8,41},{9,... | collective-permute-start | bytes 98312 | tf_op jit(solution)/shard_map/ppermute | solution.py:61
  68.2 0.6 collective-permute-start.16
  68.8 1.6 %collective-permute-done.15 = bf16[8,16,128]{2,1,0:T(8,128)(2,1)S(1)} collective-permute-done((bf16[8,16,128]{2,1,0:T(8,128)(2,1)S(1)}, bf16[8,16,128]{2,1,0:T(8,128)(2,1)S(1)}, u32[]{:S(2)}, u32[]{:S(2)}) %collective-permute-start.15) | collective-permute-done | bytes 32800 | tf_op jit(solution)/shard_map/ppermute | solution.py:61
  70.5 1.0 %collective-permute-done.14 = bf16[8,16,128]{2,1,0:T(8,128)(2,1)S(1)} collective-permute-done((bf16[8,16,128]{2,1,0:T(8,128)(2,1)S(1)}, bf16[8,16,128]{2,1,0:T(8,128)(2,1)S(1)}, u32[]{:S(2)}, u32[]{:S(2)}) %collective-permute-start.14) | collective-permute-done | bytes 32800 | tf_op jit(solution)/shard_map/ppermute | solution.py:61
  71.4 0.7 collective-permute-done.16
  72.2 2.0 %collective-permute-start.17 = (bf16[3,16,128]{2,1,0:T(8,128)(2,1)S(1)}, bf16[3,16,128]{2,1,0:T(8,128)(2,1)S(1)}, u32[]{:S(2)}, u32[]{:S(2)}) collective-permute-start(bf16[3,16,128]{2,1,0:T(8,128)(2,1)S(1)} %slice.95), channel_id=1, source_target_pairs={{0,6},{1,7},{2,8},{3,9},{4,10},{5,11},{6,12},{7,13},{8,14},{9,15},... | collective-permute-start | bytes 36872 | tf_op jit(solution)/shard_map/ppermute | solution.py:50
  74.2 3.1 %collective-permute-start.18 = (bf16[2,16,128]{2,1,0:T(8,128)(2,1)S(1)}, bf16[2,16,128]{2,1,0:T(8,128)(2,1)S(1)}, u32[]{:S(2)}, u32[]{:S(2)}) collective-permute-start(bf16[2,16,128]{2,1,0:T(8,128)(2,1)S(1)} %slice.97), channel_id=1, source_target_pairs={{0,10},{1,11},{2,12},{3,13},{4,14},{5,15},{6,0},{7,1},{8,2},{9,3},... | collective-permute-start | bytes 24584 | tf_op jit(solution)/shard_map/ppermute | solution.py:50
  77.3 2.3 %collective-permute-done.18 = bf16[2,16,128]{2,1,0:T(8,128)(2,1)S(1)} collective-permute-done((bf16[2,16,128]{2,1,0:T(8,128)(2,1)S(1)}, bf16[2,16,128]{2,1,0:T(8,128)(2,1)S(1)}, u32[]{:S(2)}, u32[]{:S(2)}) %collective-permute-start.18) | collective-permute-done | bytes 8224 | tf_op jit(solution)/shard_map/ppermute | solution.py:50
  79.7 1.7 %collective-permute-start.19 = (bf16[16,128]{1,0:T(8,128)(2,1)S(1)}, bf16[16,128]{1,0:T(8,128)(2,1)S(1)}, u32[]{:S(2)}, u32[]{:S(2)}) collective-permute-start(bf16[16,128]{1,0:T(8,128)(2,1)S(1)} %get-tuple-element.139), channel_id=1, source_target_pairs={{0,2},{1,3},{2,4},{3,5},{4,6},{5,7},{6,8},{7,9},{8,10},{9,11},{10,... | collective-permute-start | bytes 12296 | tf_op jit(solution)/shard_map/ppermute | solution.py:50
  81.4 1.9 %collective-permute-start.20 = (bf16[16,128]{1,0:T(8,128)(2,1)S(1)}, bf16[16,128]{1,0:T(8,128)(2,1)S(1)}, u32[]{:S(2)}, u32[]{:S(2)}) collective-permute-start(bf16[16,128]{1,0:T(8,128)(2,1)S(1)} %get-tuple-element.140), channel_id=1, source_target_pairs={{0,14},{1,15},{2,0},{3,1},{4,2},{5,3},{6,4},{7,5},{8,6},{9,7},{10,... | collective-permute-start | bytes 12296 | tf_op jit(solution)/shard_map/ppermute | solution.py:50
  83.3 1.5 %collective-permute-done.19 = bf16[16,128]{1,0:T(8,128)(2,1)S(1)} collective-permute-done((bf16[16,128]{1,0:T(8,128)(2,1)S(1)}, bf16[16,128]{1,0:T(8,128)(2,1)S(1)}, u32[]{:S(2)}, u32[]{:S(2)}) %collective-permute-start.19) | collective-permute-done | bytes 4128 | tf_op jit(solution)/shard_map/ppermute | solution.py:50
  84.8 0.2 collective-permute-done.20
  85.0 0.6 fusion.7
  (42 shorter events, 0.6 us)
Async XLA Ops:
  1.5 4.9 %collective-permute-start = (bf16[272,128]{1,0:T(8,128)(2,1)S(1)}, bf16[272,128]{1,0:T(8,128)(2,1)S(1)}, u32[]{:S(2)}, u32[]{:S(2)}) collective-permute-start(bf16[272,128]{1,0:T(8,128)(2,1)S(1)} %join.1.rest_0_), channel_id=1, source_target_pairs={{0,32},{16,48},{32,0},{48,16},{64,96},{80,112},{96,64},{112,80},{1... | collective-permute-start | bytes 208904 | tf_op jit(solution)/shard_map/ppermute | solution.py:37
  6.5 8.2 %collective-permute-start.1 = (bf16[2,272,128]{2,1,0:T(8,128)(2,1)S(1)}, bf16[2,272,128]{2,1,0:T(8,128)(2,1)S(1)}, u32[]{:S(2)}, u32[]{:S(2)}) collective-permute-start(bf16[2,272,128]{2,1,0:T(8,128)(2,1)S(1)} %pad_maximum_fusion.rest_3_.q_ref), channel_id=1, source_target_pairs={{0,64},{16,80},{32,96},{48,112},{64,128},{80,144},{96,160},{112,17... | collective-permute-start | bytes 417800 | tf_op jit(solution)/shard_map/ppermute | solution.py:41
  8.0 6.7 %collective-permute-start.2 = (bf16[2,272,128]{2,1,0:T(8,128)(2,1)S(1)}, bf16[2,272,128]{2,1,0:T(8,128)(2,1)S(1)}, u32[]{:S(2)}, u32[]{:S(2)}) collective-permute-start(bf16[2,272,128]{2,1,0:T(8,128)(2,1)S(1)} %pad_maximum_fusion.rest_3_.q_ref), channel_id=1, source_target_pairs={{0,192},{16,208},{32,224},{48,240},{64,0},{80,16},{96,32},{112,48}... | collective-permute-start | bytes 417800 | tf_op jit(solution)/shard_map/ppermute | solution.py:41
  8.6 7.9 %collective-permute-start.3 = (bf16[2,272,128]{2,1,0:T(8,128)(2,1)S(1)}, bf16[2,272,128]{2,1,0:T(8,128)(2,1)S(1)}, u32[]{:S(2)}, u32[]{:S(2)}) collective-permute-start(bf16[2,272,128]{2,1,0:T(8,128)(2,1)S(1)} %pad_maximum_fusion.rest_3_.q_ref), channel_id=1, source_target_pairs={{0,128},{16,144},{32,160},{48,176},{64,192},{80,208},{96,224},{112... | collective-permute-start | bytes 417800 | tf_op jit(solution)/shard_map/ppermute | solution.py:41
  16.6 3.0 %collective-permute-start.4 = (bf16[8,272,128]{2,1,0:T(8,128)(2,1)S(1)}, bf16[8,272,128]{2,1,0:T(8,128)(2,1)S(1)}, u32[]{:S(2)}, u32[]{:S(2)}) collective-permute-start(bf16[8,272,128]{2,1,0:T(8,128)(2,1)S(1)} %constant_dynamic-update-slice_fusion.q_ref.near_ref), channel_id=1, source_target_pairs={{0,16},{16,0},{32,48},{48,32},{64,80},{80,64},{96,112},{112,96},{1... | collective-permute-start | bytes 1671176 | tf_op jit(solution)/shard_map/ppermute | solution.py:37
  19.8 5.8 %collective-permute-start.5 = (f32[8,256]{1,0:T(8,128)S(1)}, f32[8,256]{1,0:T(8,128)S(1)}, u32[]{:S(2)}, u32[]{:S(2)}) collective-permute-start(f32[8,256]{1,0:T(8,128)S(1)} %targets.1.rest_3_.rest_0_), channel_id=1, source_target_pairs={{0,1},{1,0},{2,3},{3,2},{4,5},{5,4},{6,7},{7,6},{8,9},{9,8},{10,11... | collective-permute-start | bytes 24584 | tf_op jit(solution)/shard_map/ppermute | solution.py:37
  25.6 7.7 %collective-permute-start.6 = (f32[2,8,256]{2,1,0:T(8,128)S(1)}, f32[2,8,256]{2,1,0:T(8,128)S(1)}, u32[]{:S(2)}, u32[]{:S(2)}) collective-permute-start(f32[2,8,256]{2,1,0:T(8,128)S(1)} %pad_maximum_fusion.2), channel_id=1, source_target_pairs={{0,2},{1,3},{2,4},{3,5},{4,6},{5,7},{6,8},{7,9},{8,10},{9,11},{10,... | collective-permute-start | bytes 49160 | tf_op jit(solution)/shard_map/ppermute | solution.py:50
  27.6 5.7 %collective-permute-start.7 = (f32[2,8,256]{2,1,0:T(8,128)S(1)}, f32[2,8,256]{2,1,0:T(8,128)S(1)}, u32[]{:S(2)}, u32[]{:S(2)}) collective-permute-start(f32[2,8,256]{2,1,0:T(8,128)S(1)} %pad_maximum_fusion.2), channel_id=1, source_target_pairs={{0,14},{1,15},{2,0},{3,1},{4,2},{5,3},{6,4},{7,5},{8,6},{9,7},{10,... | collective-permute-start | bytes 49160 | tf_op jit(solution)/shard_map/ppermute | solution.py:50
  33.3 8.0 %collective-permute-start.8 = (f32[6,8,256]{2,1,0:T(8,128)S(1)}, f32[6,8,256]{2,1,0:T(8,128)S(1)}, u32[]{:S(2)}, u32[]{:S(2)}) collective-permute-start(f32[6,8,256]{2,1,0:T(8,128)S(1)} %pad_maximum_fusion.1.rest_0_), channel_id=1, source_target_pairs={{0,6},{1,7},{2,8},{3,9},{4,10},{5,11},{6,12},{7,13},{8,14},{9,15},... | collective-permute-start | bytes 147464 | tf_op jit(solution)/shard_map/ppermute | solution.py:50
  38.4 7.0 %collective-permute-start.9 = (f32[6,8,256]{2,1,0:T(8,128)S(1)}, f32[6,8,256]{2,1,0:T(8,128)S(1)}, u32[]{:S(2)}, u32[]{:S(2)}) collective-permute-start(f32[6,8,256]{2,1,0:T(8,128)S(1)} %pad_maximum_fusion.1.rest_0_), channel_id=1, source_target_pairs={{0,10},{1,11},{2,12},{3,13},{4,14},{5,15},{6,0},{7,1},{8,2},{9,3},... | collective-permute-start | bytes 147464 | tf_op jit(solution)/shard_map/ppermute | solution.py:50
  50.4 3.9 %collective-permute-start.10 = (bf16[8,256,128]{2,1,0:T(8,128)(2,1)S(1)}, bf16[8,256,128]{2,1,0:T(8,128)(2,1)S(1)}, u32[]{:S(2)}, u32[]{:S(2)}) collective-permute-start(bf16[8,256,128]{2,1,0:T(8,128)(2,1)S(1)} %get-tuple-element.124), channel_id=1, source_target_pairs={{0,16},{16,0},{32,48},{48,32},{64,80},{80,64},{96,112},{112,96},{1... | collective-permute-start | bytes 1572872 | tf_op jit(solution)/shard_map/ppermute | solution.py:37
  50.5 10.5 %copy-start = (bf16[1024,128]{1,0:T(8,128)(2,1)S(1)}, bf16[1024,128]{1,0:T(8,128)(2,1)}, u32[]{:S(2)}) copy-start(bf16[1024,128]{1,0:T(8,128)(2,1)} %w_ref.5) | copy-start | bytes 786436
  54.5 10.1 %collective-permute-start.11 = (bf16[2,256,128]{2,1,0:T(8,128)(2,1)S(1)}, bf16[2,256,128]{2,1,0:T(8,128)(2,1)S(1)}, u32[]{:S(2)}, u32[]{:S(2)}) collective-permute-start(bf16[2,256,128]{2,1,0:T(8,128)(2,1)S(1)} %get-tuple-element.136), channel_id=1, source_target_pairs={{0,192},{16,208},{32,224},{48,240},{64,0},{80,16},{96,32},{112,48}... | collective-permute-start | bytes 393224 | tf_op jit(solution)/shard_map/ppermute | solution.py:41
  55.4 9.2 %collective-permute-start.12 = (bf16[2,256,128]{2,1,0:T(8,128)(2,1)S(1)}, bf16[2,256,128]{2,1,0:T(8,128)(2,1)S(1)}, u32[]{:S(2)}, u32[]{:S(2)}) collective-permute-start(bf16[2,256,128]{2,1,0:T(8,128)(2,1)S(1)} %get-tuple-element.135), channel_id=1, source_target_pairs={{0,64},{16,80},{32,96},{48,112},{64,128},{80,144},{96,160},{112,17... | collective-permute-start | bytes 393224 | tf_op jit(solution)/shard_map/ppermute | solution.py:41
  56.6 8.0 %collective-permute-start.13 = (bf16[2,256,128]{2,1,0:T(8,128)(2,1)S(1)}, bf16[2,256,128]{2,1,0:T(8,128)(2,1)S(1)}, u32[]{:S(2)}, u32[]{:S(2)}) collective-permute-start(bf16[2,256,128]{2,1,0:T(8,128)(2,1)S(1)} %get-tuple-element.134), channel_id=1, source_target_pairs={{0,128},{16,144},{32,160},{48,176},{64,192},{80,208},{96,224},{112... | collective-permute-start | bytes 393224 | tf_op jit(solution)/shard_map/ppermute | solution.py:41
  65.0 5.5 %collective-permute-start.15 = (bf16[8,16,128]{2,1,0:T(8,128)(2,1)S(1)}, bf16[8,16,128]{2,1,0:T(8,128)(2,1)S(1)}, u32[]{:S(2)}, u32[]{:S(2)}) collective-permute-start(bf16[8,16,128]{2,1,0:T(8,128)(2,1)S(1)} %copy.22), channel_id=1, source_target_pairs={{0,1},{1,0},{2,3},{3,2},{4,5},{5,4},{6,7},{7,6},{8,9},{9,8},{10,11... | collective-permute-start | bytes 98312 | tf_op jit(solution)/shard_map/ppermute | solution.py:61
  66.2 5.2 %collective-permute-start.14 = (bf16[8,16,128]{2,1,0:T(8,128)(2,1)S(1)}, bf16[8,16,128]{2,1,0:T(8,128)(2,1)S(1)}, u32[]{:S(2)}, u32[]{:S(2)}) collective-permute-start(bf16[8,16,128]{2,1,0:T(8,128)(2,1)S(1)} %copy.20), channel_id=1, source_target_pairs={{0,33},{1,32},{2,35},{3,34},{4,37},{5,36},{6,39},{7,38},{8,41},{9,... | collective-permute-start | bytes 98312 | tf_op jit(solution)/shard_map/ppermute | solution.py:61
  68.2 3.9 %collective-permute-start.16 = (bf16[8,16,128]{2,1,0:T(8,128)(2,1)S(1)}, bf16[8,16,128]{2,1,0:T(8,128)(2,1)S(1)}, u32[]{:S(2)}, u32[]{:S(2)}) collective-permute-start(bf16[8,16,128]{2,1,0:T(8,128)(2,1)S(1)} %copy.23), channel_id=1, source_target_pairs={{0,32},{1,33},{2,34},{3,35},{4,36},{5,37},{6,38},{7,39},{8,40},{9,... | collective-permute-start | bytes 98312 | tf_op jit(solution)/shard_map/ppermute | solution.py:61
  72.2 7.5 %collective-permute-start.17 = (bf16[3,16,128]{2,1,0:T(8,128)(2,1)S(1)}, bf16[3,16,128]{2,1,0:T(8,128)(2,1)S(1)}, u32[]{:S(2)}, u32[]{:S(2)}) collective-permute-start(bf16[3,16,128]{2,1,0:T(8,128)(2,1)S(1)} %slice.95), channel_id=1, source_target_pairs={{0,6},{1,7},{2,8},{3,9},{4,10},{5,11},{6,12},{7,13},{8,14},{9,15},... | collective-permute-start | bytes 36872 | tf_op jit(solution)/shard_map/ppermute | solution.py:50
  74.2 5.4 %collective-permute-start.18 = (bf16[2,16,128]{2,1,0:T(8,128)(2,1)S(1)}, bf16[2,16,128]{2,1,0:T(8,128)(2,1)S(1)}, u32[]{:S(2)}, u32[]{:S(2)}) collective-permute-start(bf16[2,16,128]{2,1,0:T(8,128)(2,1)S(1)} %slice.97), channel_id=1, source_target_pairs={{0,10},{1,11},{2,12},{3,13},{4,14},{5,15},{6,0},{7,1},{8,2},{9,3},... | collective-permute-start | bytes 24584 | tf_op jit(solution)/shard_map/ppermute | solution.py:50
  79.7 5.1 %collective-permute-start.19 = (bf16[16,128]{1,0:T(8,128)(2,1)S(1)}, bf16[16,128]{1,0:T(8,128)(2,1)S(1)}, u32[]{:S(2)}, u32[]{:S(2)}) collective-permute-start(bf16[16,128]{1,0:T(8,128)(2,1)S(1)} %get-tuple-element.139), channel_id=1, source_target_pairs={{0,2},{1,3},{2,4},{3,5},{4,6},{5,7},{6,8},{7,9},{8,10},{9,11},{10,... | collective-permute-start | bytes 12296 | tf_op jit(solution)/shard_map/ppermute | solution.py:50
  81.4 3.6 %collective-permute-start.20 = (bf16[16,128]{1,0:T(8,128)(2,1)S(1)}, bf16[16,128]{1,0:T(8,128)(2,1)S(1)}, u32[]{:S(2)}, u32[]{:S(2)}) collective-permute-start(bf16[16,128]{1,0:T(8,128)(2,1)S(1)} %get-tuple-element.140), channel_id=1, source_target_pairs={{0,14},{1,15},{2,0},{3,1},{4,2},{5,3},{6,4},{7,5},{8,6},{9,7},{10,... | collective-permute-start | bytes 12296 | tf_op jit(solution)/shard_map/ppermute | solution.py:50
